TPU v7x, 32 devices: a whole 2x2x4 slice. The times are simulated.
32 devices in a mesh: seq: 8 (over y, x, core), ch: 4 (over z).
Axes of the slice: x: 2, y: 2, z: 4, core: 2. Of those that a mesh axis runs over, the one named last changes fastest.
Arguments:
- tokens: bfloat16 [3072, 8192], P('seq', 'ch'), may hold values from -6 to 6
- in_weight: bfloat16 [3, 8192, 1024], P(None, 'seq', 'ch'), may hold values from -0.0625 to 0.0625
- short_filter: float32 [7, 3, 1024], P(None, None, 'ch'), may hold values from -2.4 to 2.4
- long_taps: float32 [128, 1024], P(None, 'ch'), may hold values from -0.5 to 0.5
- decay_rate: float32 [16, 1024], P(None, 'ch'), may hold values from 6.510417e-06 to 0.033333335
- residue: float32 [16, 1024], P(None, 'ch'), may hold values from -1.5 to 1.5
Outputs:
- gated: bfloat16 [3072, 1024], P('seq', 'ch')
All inputs are finite; a program needn't handle non-finite values.
Results may differ from a plain program's by a relative error of at most 0.017.
Values may be sent and summed in bfloat16 or wider, within the bound.
A program may use at most 64 MiB of HBM per device.

v0:
```python
import math

import jax
import jax.numpy as jnp
from jax import lax
from jax.sharding import PartitionSpec as P

TAPS = 128
SHORT = 7


def from_behind(value, axis, steps):
    count = lax.axis_size(axis)
    initial, last = (max(0, -steps), min(count, count - steps))
    return lax.ppermute(value, axis, [(source, source + steps) for source in range(initial, last)])


def prefix_2(array, axis, join, neutral):
    place = lax.axis_index(axis)
    gathered = jax.tree.map(
        lambda a, kind: lax.all_gather(a.astype(kind), axis),
        array,
        jax.tree.map(lambda a: jnp.bfloat16 if a.dtype == jnp.float32 else a.dtype, array),
    )
    state = jax.tree.map(lambda a, e: jnp.zeros_like(a) + jnp.asarray(e, a.dtype), array, neutral)

    def one(lap, state):
        return join(
            state,
            jax.tree.map(
                lambda a, own: lax.dynamic_index_in_dim(a, lap, 0, False).astype(own.dtype),
                gathered,
                array,
            ),
        )

    return lax.fori_loop(0, place, one, state)


def depthwise(signal, kernel):
    flipped = kernel[::-1][:, None, :]
    result = lax.conv_general_dilated(
        signal[None],
        flipped,
        (1,),
        "VALID",
        dimension_numbers=("NWC", "WIO", "NWC"),
        feature_group_count=kernel.shape[1],
        precision=lax.Precision.HIGHEST,
    )
    return result[0]


def phase_angle(steps, mode_count):
    period = 4 * mode_count
    odd_numbers = 2 * jnp.arange(mode_count) + 1
    turns = steps[:, None] % period * odd_numbers[None, :] % period
    return turns.astype(jnp.float32) * (math.pi / (2 * mode_count))


def damped(decay_rate, steps):
    angle = phase_angle(steps, decay_rate.shape[0])
    magnitude = jnp.exp(-decay_rate[None] * steps.astype(jnp.float32)[:, None, None])
    return (magnitude * jnp.cos(angle)[:, :, None], magnitude * jnp.sin(angle)[:, :, None])


def on_device(tokens, in_weight, short_filter, long_taps, decay_rate, residue):
    gathered = lax.all_gather(tokens, "ch", axis=1, tiled=True)
    tok_rows = gathered.shape[0]
    chan_width = in_weight.shape[2]

    def add_rows(portion):
        return jnp.dot(gathered, portion, preferred_element_type=jnp.float32)

    portion = lax.all_gather(in_weight, "seq", axis=1, tiled=True)
    blocks = tuple((add_rows(portion[which]) for which in range(3)))
    features = jnp.concatenate(list(blocks), axis=1).astype(jnp.bfloat16)
    short_taps = short_filter.reshape(SHORT, 3 * chan_width)
    head_rows = from_behind(features[tok_rows - (SHORT - 1) :], "seq", 1)
    filtered = depthwise(
        jnp.concatenate([head_rows, features], axis=0).astype(jnp.float32), short_taps
    )
    product = (filtered[:, chan_width : 2 * chan_width] * filtered[:, 2 * chan_width :]).astype(
        jnp.bfloat16
    )
    product_tail = from_behind(product[tok_rows - (TAPS - 1) :], "seq", 1)
    product_f = product.astype(jnp.float32)
    explicit = depthwise(
        jnp.concatenate([product_tail.astype(jnp.float32), product_f], axis=0), long_taps
    )
    coef = residue * jnp.sqrt(-jnp.expm1(-2.0 * decay_rate))
    offsets = jnp.arange(tok_rows)
    kernel_cos, kernel_sin = damped(decay_rate, offsets)
    modal_kernel = jnp.einsum("dnc,nc->dc", kernel_cos, coef, precision=lax.Precision.HIGHEST)
    local = depthwise(
        jnp.concatenate([jnp.zeros((tok_rows - 1, chan_width), jnp.float32), product_f], axis=0),
        modal_kernel,
    )
    back_cos, back_sin = damped(decay_rate, tok_rows - 1 - offsets)
    own_real = jnp.einsum("snc,sc->nc", back_cos, product_f, precision=lax.Precision.HIGHEST)
    own_imag = jnp.einsum("snc,sc->nc", back_sin, product_f, precision=lax.Precision.HIGHEST)
    span_cos, span_sin = damped(decay_rate, jnp.full((1,), tok_rows, jnp.int32))
    span_real = span_cos[0]
    span_imag = span_sin[0]

    def combine(earlier_set, later_set):
        early_ar, early_ai, early_br, early_bi = earlier_set
        later_ar, later_ai, later_br, later_bi = later_set
        joint_ar = later_ar * early_ar - later_ai * early_ai
        joint_ai = later_ar * early_ai + later_ai * early_ar
        joint_br = later_ar * early_br - later_ai * early_bi + later_br
        joint_bi = later_ar * early_bi + later_ai * early_br + later_bi
        return (joint_ar, joint_ai, joint_br, joint_bi)

    identity = (
        jnp.ones_like(span_real),
        jnp.zeros_like(span_imag),
        jnp.zeros_like(own_real),
        jnp.zeros_like(own_imag),
    )
    prefix = prefix_2((span_real, span_imag, own_real, own_imag), "seq", combine, identity)
    inflow_real = prefix[2]
    inflow_imag = prefix[3]
    ahead_cos, ahead_sin = damped(decay_rate, offsets + 1)
    inflow = jnp.einsum(
        "tnc,nc->tc", ahead_cos, coef * inflow_real, precision=lax.Precision.HIGHEST
    ) - jnp.einsum("tnc,nc->tc", ahead_sin, coef * inflow_imag, precision=lax.Precision.HIGHEST)
    return (filtered[:, :chan_width] * (explicit + (local + inflow))).astype(jnp.bfloat16)


def solution(mesh):
    placed = (
        P("seq", "ch"),
        P(None, "seq", "ch"),
        P(None, None, "ch"),
        P(None, "ch"),
        P(None, "ch"),
        P(None, "ch"),
    )
    return jax.shard_map(
        on_device, mesh=mesh, in_specs=placed, out_specs=P("seq", "ch"), check_vma=False
    )
```

profile of v0, /device:TPU:0, one launch (start us, length us, event | category | flops | bytes accessed | tf_op | source)
XLA Modules:
  0.0 286.9 jit_solution(49117539384713898)
XLA Ops:
  6.5 0.0 all-gather.7.cloned.1.call-start
  6.5 0.7 all-gather.7.cloned.1.call-update
  7.3 0.0 all-gather.9.cloned.1.call-start
  7.3 0.7 all-gather.9.cloned.1.call-update
  8.0 2.1 rev.9
  10.1 1.5 rev.10
  11.7 0.4 fusion.37
  12.0 0.1 copy.24
  12.2 0.8 copy.25
  13.0 0.1 copy.22
  13.1 0.1 copy.26
  13.3 0.1 copy.27
  13.4 0.7 fusion.53
  14.1 10.7 %all-gather = bf16[128,256]{1,0:T(8,128)(2,1)S(1)} all-gather(bf16[16,256]{1,0:T(8,128)(2,1)S(1)} %get-tuple-element.106), channel_id=2, replica_groups=mesh['seq'=8,'ch'=4] {'seq'}, dimensions={0}, use_global_device_ids=true | all-gather | bytes 73728 | tf_op jit(solution)/shard_map/all_gather | solution.py:21
  24.8 0.6 fusion.43
  25.4 0.6 fusion.42
  26.0 101.0 %all-gather.7.cloned.1.call-done = bf16[384,8192]{1,0:T(8,128)(2,1)} async-done(((bf16[384,2048]{1,0:T(8,128)(2,1)}), bf16[384,8192]{1,0:T(8,128)(2,1)}) %all-gather.7.cloned.1.call-update) | async-done | bytes 6291472 | tf_op jit(solution)/shard_map/all_gather | solution.py:68
  127.0 72.2 %all-gather.9.cloned.1.call-done = bf16[3,8192,256]{2,1,0:T(8,128)(2,1)} async-done(((bf16[3,1024,256]{2,1,0:T(8,128)(2,1)}), bf16[3,8192,256]{2,1,0:T(8,128)(2,1)}) %all-gather.9.cloned.1.call-update) | async-done | bytes 12582928 | tf_op jit(solution)/shard_map/all_gather | solution.py:75
  199.3 0.0 copy-start.3
  199.3 0.0 slice-start
  199.3 6.5 %fusion.10 = bf16[384,256]{0,1:T(8,128)(2,1)S(1)} fusion(bf16[384,8192]{1,0:T(8,128)(2,1)} %all-gather.7.cloned.1.call-done, bf16[3,8192,256]{2,1,0:T(8,128)(2,1)} %all-gather.9.cloned.1.call-done), kind=kOutput, calls=%fused_computation.27 | convolution fusion | flops 1610711040 | bytes 10682368 | tf_op jit(solution)/shard_map/dot_general | solution.py:73
  205.8 1.0 copy-done.3
  206.8 0.0 slice-start.1
  206.8 5.4 %fusion.8 = bf16[384,256]{0,1:T(8,128)(2,1)S(1)} fusion(bf16[384,8192]{1,0:T(8,128)(2,1)} %all-gather.7.cloned.1.call-done, bf16[3,8192,256]{2,1,0:T(8,128)(2,1)S(1)} %copy-done.3), kind=kOutput, calls=%fused_computation.25 | convolution fusion | flops 1610711040 | bytes 10682368 | tf_op jit(solution)/shard_map/dot_general | solution.py:73
  212.3 0.0 slice-done
  212.3 0.0 slice-done.1
  212.3 2.4 fusion.9
  214.7 0.0 copy-start.4
  214.7 0.1 pad_maximum_fusion.1
  214.8 2.2 collective-permute-start
  217.0 9.5 %all-gather.1 = bf16[128,256]{1,0:T(8,128)(2,1)S(1)} all-gather(bf16[16,256]{1,0:T(8,128)(2,1)S(1)} %get-tuple-element.107), channel_id=3, replica_groups=mesh['seq'=8,'ch'=4] {'seq'}, dimensions={0}, use_global_device_ids=true | all-gather | bytes 73728 | tf_op jit(solution)/shard_map/all_gather | solution.py:21
  226.5 0.0 collective-permute-done
  226.5 0.4 maximum_bitcast_fusion
  226.9 0.2 copy.64
  227.2 0.2 reshape.302
  227.4 0.1 copy.19
  227.5 0.0 copy-done.4
  227.5 0.6 convolution_select_fusion
  228.2 0.0 copy-start.1
  228.2 0.0 copy-start.2
  228.2 0.4 copy.20
  228.6 0.2 reshape.306
  228.8 0.1 slice_bitcast_fusion.6
  228.9 0.1 fusion.51
  228.9 0.6 slice.42
  229.6 2.9 collective-permute-start.1
  232.5 5.5 %multiply_reduce_fusion.2 = (bf16[256,16]{0,1:T(8,128)(2,1)S(1)}, bf16[256,16]{0,1:T(8,128)(2,1)S(1)}) fusion(f32[256,384]{0,1:T(8,128)S(1)} %bitcast_convert_fusion, f32[384,16]{1,0:T(8,128)} %copy.25, f32[384]{0:T(512)} %fusion.43, f32[16,256]{1,0:T(8,128)S(1)} %get-tuple-element.105, f32[384,16]{1,0:T(8,128)S(1)} %copy.24), kind=kLoop, calls=%fused_computation.10 | loop fusion | flops 11001856 | bytes 476672 | tf_op jit(solution)/shard_map/snc,sc->nc/dot_general | solution.py:101
  237.9 7.8 %all-gather.2 = bf16[128,256]{1,0:T(8,128)(2,1)S(1)} all-gather(bf16[16,256]{1,0:T(8,128)(2,1)S(1)} %bitcast.100), channel_id=4, replica_groups=mesh['seq'=8,'ch'=4] {'seq'}, dimensions={0}, use_global_device_ids=true | all-gather | bytes 73728 | tf_op jit(solution)/shard_map/all_gather | solution.py:21
  245.7 9.7 %all-gather.3 = bf16[128,256]{1,0:T(8,128)(2,1)S(1)} all-gather(bf16[16,256]{1,0:T(8,128)(2,1)S(1)} %bitcast.99), channel_id=5, replica_groups=mesh['seq'=8,'ch'=4] {'seq'}, dimensions={0}, use_global_device_ids=true | all-gather | bytes 73728 | tf_op jit(solution)/shard_map/all_gather | solution.py:21
  255.4 0.0 copy-done.1
  255.4 0.0 copy-done.2
  255.5 7.2 %multiply_reduce_fusion = (f32[256,384]{0,1:T(8,128)S(1)}, f32[256,384]{0,1:T(8,128)S(1)}, f32[256,384]{0,1:T(8,128)S(1)}) fusion(f32[256,16]{0,1:T(8,128)S(1)} %get-tuple-element.104, f32[384,16]{1,0:T(8,128)S(1)} %copy.27, f32[384]{0:T(512)} %get-tuple-element.118, f32[16,256]{1,0:T(8,128)S(1)} %get-tuple-element.105, f32[384,16]{1,0:T(8,128)S(1)} %copy.26, ...), kind=kLoop, calls=%fused_computation.8 | loop fusion | flops 17006592 | bytes 1321984 | tf_op jit(solution)/shard_map/tnc,nc->tc/dot_general | solution.py:127
  262.6 0.2 rev.11
  262.8 0.3 broadcast_in_dim.17
  263.1 0.1 pad_bitcast_fusion
  263.2 0.0 copy-start
  263.2 10.7 %fusion.11 = f32[1,384,256]{2,0,1:T(1,128)S(1)} fusion(f32[384,1,256]{2,1,0:T(1,128)S(1)} %broadcast_in_dim.17, f32[1,767,256]{2,1,0:T(8,128)S(1)} %pad_bitcast_fusion), kind=kOutput, calls=%fused_computation.30 | convolution fusion | flops 452984832 | bytes 1571840 | tf_op jit(solution)/shard_map/conv_general_dilated | solution.py:42
  273.9 0.0 collective-permute-done.1
  273.9 0.9 convert_element_type.134
  274.8 0.4 broadcast_in_dim.14
  275.1 0.0 copy-done
  275.2 4.1 %fusion.23 = f32[1,384,256]{2,0,1:T(1,128)S(1)} fusion(f32[1,511,256]{2,0,1:T(1,128)S(1)} %broadcast_in_dim.14, f32[128,1,256]{2,0,1:T(8,128)S(1)} %bitcast.97), kind=kOutput, calls=%fused_computation.48 | convolution fusion | flops 150994944 | bytes 1047552 | tf_op jit(solution)/shard_map/conv_general_dilated | solution.py:42
  279.2 0.8 fusion.20
  (13 shorter events, 0.2 us)
Async XLA Ops:
  6.5 120.5 %all-gather.7.cloned.1.call-start = ((), (), s32[]{:S(2)}) async-start(), calls=%async_computation | async-start | bytes 7864320 | tf_op jit(solution)/shard_map/all_gather | solution.py:68
  7.3 192.0 %all-gather.9.cloned.1.call-start = ((), (), s32[]{:S(2)}) async-start(), calls=%async_computation.1 | async-start | bytes 14155776 | tf_op jit(solution)/shard_map/all_gather | solution.py:75
  199.3 7.6 %copy-start.3 = (bf16[3,8192,256]{2,1,0:T(8,128)(2,1)S(1)}, bf16[3,8192,256]{2,1,0:T(8,128)(2,1)}, u32[]{:S(2)}) copy-start(bf16[3,8192,256]{2,1,0:T(8,128)(2,1)} %all-gather.9.cloned.1.call-done) | copy-start | bytes 37748740
  199.3 13.0 %slice-start = ((s8[6291456]{0:T(1024)(128)(4,1)}), s8[4194304]{0:T(1024)(128)(4,1)S(1)}, s32[]{:S(2)}) async-start(s8[6291456]{0:T(1024)(128)(4,1)} %bitcast.101), calls=%async_computation.2 | async-start | bytes 8388608
  206.8 5.4 %slice-start.1 = ((s8[6291456]{0:T(1024)(128)(4,1)}), s8[2097152]{0:T(1024)(128)(4,1)S(1)}, s32[]{:S(2)}) async-start(s8[6291456]{0:T(1024)(128)(4,1)} %bitcast.101), calls=%async_computation.3 | async-start | bytes 4194304
  214.7 12.8 %copy-start.4 = (pred[8,49]{0,1:T(8,128)(4,1)S(1)}, pred[8,49]{0,1:T(8,128)(4,1)}, u32[]{:S(2)}) copy-start(pred[8,49]{0,1:T(8,128)(4,1)} %constant.134) | copy-start | bytes 1180
  214.8 11.7 %collective-permute-start = (bf16[6,768]{0,1:T(8,128)(2,1)S(1)}, bf16[6,768]{0,1:T(8,128)(2,1)S(1)}, u32[]{:S(2)}, u32[]{:S(2)}) collective-permute-start(bf16[6,768]{0,1:T(8,128)(2,1)S(1)} %pad_maximum_fusion.1), channel_id=1, source_target_pairs={{0,4},{4,8},{8,12},{12,16},{16,20},{20,24},{24,28},{1,5},{5,9},{9,... | collective-permute-start | bytes 27656 | tf_op jit(solution)/shard_map/ppermute | solution.py:15
  228.2 27.2 %copy-start.1 = (f32[16,256]{1,0:T(8,128)S(1)}, f32[16,256]{1,0:T(8,128)}, u32[]{:S(2)}) copy-start(f32[16,256]{1,0:T(8,128)} %param.12) | copy-start | bytes 49156
  228.2 27.2 %copy-start.2 = (f32[16,256]{1,0:T(8,128)S(1)}, f32[16,256]{1,0:T(8,128)}, u32[]{:S(2)}) copy-start(f32[16,256]{1,0:T(8,128)} %param.13) | copy-start | bytes 49156
  229.6 44.2 %collective-permute-start.1 = (bf16[127,256]{1,0:T(8,128)(2,1)}, bf16[127,256]{1,0:T(8,128)(2,1)}, u32[]{:S(2)}, u32[]{:S(2)}) collective-permute-start(bf16[127,256]{1,0:T(8,128)(2,1)} %slice.42), channel_id=1, source_target_pairs={{0,4},{4,8},{8,12},{12,16},{16,20},{20,24},{24,28},{1,5},{5,9},{9,... | collective-permute-start | bytes 195080 | tf_op jit(solution)/shard_map/ppermute | solution.py:15
  263.2 12.0 %copy-start = (f32[128,256]{1,0:T(8,128)S(1)}, f32[128,256]{1,0:T(8,128)}, u32[]{:S(2)}) copy-start(f32[128,256]{1,0:T(8,128)} %rev.10) | copy-start | bytes 393220
Sparse Core Ops, SparseCore 0:
  8.9 118.0 all-gather.6
  128.9 70.3 all-gather.8
where the time goes:
time: 288 us; the launch traced here: 287 us
  waiting for transfers between devices  175 us (61%)
  blocking collectives  37.6 us (13%)
  matrix products  29.7 us (10%)
  other arithmetic  17.2 us (6%)
  between operations  13.7 us (5%)
  local copies, waits for them, and re-layouts  8.87 us (3%)
  starting transfers between devices  5.07 us (2%)
    all_gather x1, waiting for transfers between devices, on_device(): gathered = lax.all_gather(tokens, 'ch', axis=1, tiled=True)  101 us
    all_gather x1, waiting for transfers between devices, on_device(): portion = lax.all_gather(in_weight, 'seq', axis=1, tiled=True)  72.2 us
    all_gather x4, blocking collectives, prefix_2(): lax.all_gather(a.astype(kind), axis)  37.6 us
    conv_general_dilated x3, matrix products, depthwise(): lax.conv_general_dilated(signal[None], flipped, (1,), 'VALID', dimension_...  15.4 us
    dot_general x3, matrix products, add_rows(): return jnp.dot(gathered, portion, preferred_element_type=jnp.float32)  14.3 us
    dot_general x1, other arithmetic, on_device(): jnp.einsum('tnc,nc->tc', ahead_sin, coef * inflow_imag, precision=lax.Pre...  7.16 us
  transfers between devices with their start and end apart: 4, of which 2 were waited for; matrix products, arithmetic and copies ran while one was open for 11% of the time, Pallas kernels for 0%

commit v1 on v0

v1 whole, which is shorter than its diff:
```python
import math

import jax
import jax.numpy as jnp
import numpy as np
from jax import lax
from jax.sharding import PartitionSpec as P

TAPS = 128
SHORT = 7


def from_behind(value, axis):
    count = lax.axis_size(axis)
    return lax.ppermute(value, axis, [(source, source + 1) for source in range(count - 1)])


def flip(value, mask):
    count = lax.axis_size("seq")
    return lax.ppermute(value, "seq", [(s, s ^ mask) for s in range(count)])


def gather_weights(weight):
    count = lax.axis_size("seq")
    if count != 8:
        return lax.all_gather(weight, "seq", axis=1, tiled=True)
    me = lax.axis_index("seq")
    over_x = flip(weight, 2)
    over_y = flip(weight, 4)
    onward = jnp.where(me % 2 == 0, over_x, over_y)
    diagonal = lax.ppermute(onward, "seq", [(s, s ^ (4 if s % 2 == 0 else 2)) for s in range(8)])
    pieces = [(0, weight), (2, over_x), (4, over_y), (6, diagonal)]
    pieces += [(mask ^ 1, flip(piece, 1)) for mask, piece in pieces]
    depth = weight.shape[1]
    whole = jnp.zeros((3, count * depth, weight.shape[2]), weight.dtype)
    for mask, piece in pieces:
        whole = lax.dynamic_update_slice(whole, piece, (0, (me ^ mask) * depth, 0))
    return whole


def phase_angle(steps, mode_count):
    period = 4 * mode_count
    odd_numbers = 2 * jnp.arange(mode_count) + 1
    turns = steps[:, None] % period * odd_numbers[None, :] % period
    return turns.astype(jnp.float32) * (math.pi / (2 * mode_count))


def damped(decay_rate, steps):
    angle = phase_angle(steps, decay_rate.shape[0])
    magnitude = jnp.exp(-decay_rate[None] * steps.astype(jnp.float32)[:, None, None])
    return (magnitude * jnp.cos(angle)[:, :, None], magnitude * jnp.sin(angle)[:, :, None])


def fourier(rows, initial, count):
    turns = np.outer(2 * np.arange(rows) + 1, np.arange(initial, initial + count)) % (4 * rows)
    angle = turns * (math.pi / (2 * rows))
    return np.cos(angle).astype(np.float32), np.sin(angle).astype(np.float32)


def times(matrix, value):
    return jnp.dot(
        jnp.asarray(matrix), value, precision=lax.Precision.HIGH, preferred_element_type=jnp.float32
    )


def on_device(tokens, in_weight, short_filter, long_taps, decay_rate, residue):
    place = lax.axis_index("seq")
    count = lax.axis_size("seq")
    rows = tokens.shape[0]
    width = in_weight.shape[2]
    modes = decay_rate.shape[0]
    half = 2 * modes
    laps = rows // half

    gathered = lax.all_gather(tokens, "ch", axis=1, tiled=True)
    weights = gather_weights(in_weight)

    coef = residue * jnp.sqrt(-jnp.expm1(-2.0 * decay_rate))
    near_cos, near_sin = damped(decay_rate, jnp.arange(half + 1))
    sign = jnp.where(jnp.arange(laps) % 2 == 0, 1.0, -1.0)[:, None, None]
    far = sign * jnp.exp(
        -decay_rate[None] * (half * jnp.arange(laps)).astype(jnp.float32)[:, None, None]
    )
    near_kernel = jnp.sum(near_cos[:half, None] * far[None] * coef[None, None], axis=2)
    modal_kernel = near_kernel.transpose(1, 0, 2).reshape(rows, width)
    kernel = modal_kernel.at[:TAPS].add(long_taps)
    cos, sin = fourier(rows, 0, rows)
    cos_sin = np.concatenate([cos, -sin], axis=0)
    spectrum = times(cos_sin, kernel) * (1.0 / rows)
    taps_spectrum = times(cos_sin[:, :TAPS], long_taps) * (1.0 / rows)
    kernel_re, kernel_im = spectrum[:rows], spectrum[rows:]
    taps_re, taps_im = taps_spectrum[:rows], taps_spectrum[rows:]
    behind = place - 1 - jnp.arange(count)
    since_re, since_im = damped(decay_rate, jnp.maximum(behind, 0) * rows)
    before = (behind >= 0)[:, None, None]
    since_re = jnp.where(before, since_re, 0.0)
    since_im = jnp.where(before, since_im, 0.0)
    ahead_re = (coef[None] * near_cos[1:]).transpose(1, 0, 2)
    ahead_im = (coef[None] * near_sin[1:]).transpose(1, 0, 2)
    back_re, back_im, back_far = near_cos[:half][::-1], near_sin[:half][::-1], far[::-1]

    blocks = [jnp.dot(gathered, weights[j], preferred_element_type=jnp.float32) for j in range(3)]
    features = jnp.concatenate(blocks, axis=1).astype(jnp.bfloat16)
    head = from_behind(features[rows - (SHORT - 1) :], "seq")
    extended = jnp.concatenate([head, features], axis=0).astype(jnp.float32)
    short_taps = short_filter.reshape(SHORT, 3 * width)
    filtered = sum(
        short_taps[i][None] * extended[SHORT - 1 - i : SHORT - 1 - i + rows] for i in range(SHORT)
    )
    product = (filtered[:, width : 2 * width] * filtered[:, 2 * width :]).astype(jnp.bfloat16)

    tail = from_behind(product[rows - TAPS :], "seq").astype(jnp.float32)
    product_f = product.astype(jnp.float32)
    by_lap = product_f.reshape(laps, half, width)
    folded = jnp.sum(back_far[:, None] * by_lap[:, :, None, :], axis=0)
    own = jnp.concatenate(
        [jnp.sum(back_re * folded, axis=0), jnp.sum(back_im * folded, axis=0)], axis=0
    ).astype(jnp.bfloat16)
    states = lax.all_gather(own, "seq").astype(jnp.float32)

    seen = times(cos_sin, product_f)
    seen_re, seen_im = seen[:rows], seen[rows:]
    tail_cos, tail_sin = fourier(rows, -TAPS, TAPS)
    halo = times(np.concatenate([tail_cos, -tail_sin], axis=0), tail)
    halo_re, halo_im = halo[:rows], halo[rows:]
    out_re = kernel_re * seen_re - kernel_im * seen_im + taps_re * halo_re - taps_im * halo_im
    out_im = kernel_re * seen_im + kernel_im * seen_re + taps_re * halo_im + taps_im * halo_re
    local = times(
        np.concatenate([cos.T, -sin.T], axis=1), jnp.concatenate([out_re, out_im], axis=0)
    )

    state_re, state_im = states[:, :modes], states[:, modes:]
    inflow_re = jnp.sum(since_re * state_re - since_im * state_im, axis=0)
    inflow_im = jnp.sum(since_re * state_im + since_im * state_re, axis=0)
    ahead = ahead_re * inflow_re[:, None] - ahead_im * inflow_im[:, None]
    inflow = jnp.sum(far[:, :, None, :] * ahead[None], axis=1).reshape(rows, width)
    return (filtered[:, :width] * (local + inflow)).astype(jnp.bfloat16)


def solution(mesh):
    placed = (
        P("seq", "ch"),
        P(None, "seq", "ch"),
        P(None, None, "ch"),
        P(None, "ch"),
        P(None, "ch"),
        P(None, "ch"),
    )
    return jax.shard_map(
        on_device, mesh=mesh, in_specs=placed, out_specs=P("seq", "ch"), check_vma=False
    )
```

time: 288 us -> 186 us (0.65)
  waiting for transfers between devices: 175 us -> 74.6 us
  blocking collectives: 37.6 us -> 10.3 us
  local copies, waits for them, and re-layouts: 8.87 us -> 32.9 us
  starting transfers between devices: 5.07 us -> 14.3 us
  matrix products: 29.7 us -> 24.1 us
    all_gather x1 -> x0, waiting for transfers between devices: 72.2 us -> none  [on_device(): portion = lax.all_gather(in_weight, 'seq', axis=1, tiled=True)]
    all_gather x1, waiting for transfers between devices: 101 us -> 40.1 us  [on_device(): gathered = lax.all_gather(tokens, 'ch', axis=1, tiled=True)]
    ppermute x2 -> x9, waiting for transfers between devices: 0.01 us -> 33.8 us  [the longest x6 24.9 us: flip(): return lax.ppermute(value, 'seq', [(s, s ^ mask) for s in range(count)])]
    all_gather x4 -> x1, blocking collectives: 37.6 us -> 10.3 us  [on_device(): states = lax.all_gather(own, 'seq').astype(jnp.float32)]
    conv_general_dilated x3 -> x0, matrix products: 15.4 us -> none  [depthwise(): lax.conv_general_dilated(signal[None], flipped, (1,), 'VALID', dimension_...]
    dynamic_update_slice x0 -> x7, local copies, waits for them, and re-layouts: none -> 14.7 us  [gather_weights(): whole = lax.dynamic_update_slice(whole, piece, (0, (me ^ mask) * depth, 0))]
    dot_general x2 -> x0, other arithmetic: 12.6 us -> none  [the longest x1 7.16 us: on_device(): jnp.einsum('tnc,nc->tc', ahead_sin, coef * inflow_imag, precision=lax.Pre...]
    dot_general x3 -> x9, matrix products: 14.3 us -> 24.1 us  [the longest x3 14.6 us: on_device(): jnp.dot(gathered, weights[j], preferred_element_type=jnp.float32)]
  transfers between devices with their start and end apart: 4 -> 10, of which waited for: 2 -> 5; matrix products, arithmetic and copies ran while one was open for 11% -> 24% of each run, Pallas kernels for 0% -> 0%
where the time goes in v1:
time: 186 us
  waiting for transfers between devices  74.6 us (40%)
  local copies, waits for them, and re-layouts  32.9 us (18%)
  matrix products  24.1 us (13%)
  other arithmetic  15.8 us (8%)
  starting transfers between devices  14.3 us (8%)
  between operations  13.8 us (7%)
  blocking collectives  10.3 us (6%)
    all_gather x1, waiting for transfers between devices, on_device(): gathered = lax.all_gather(tokens, 'ch', axis=1, tiled=True)  40.1 us
    ppermute x6, waiting for transfers between devices, flip(): return lax.ppermute(value, 'seq', [(s, s ^ mask) for s in range(count)])  24.9 us
    dynamic_update_slice x7, local copies, waits for them, and re-layouts, gather_weights(): whole = lax.dynamic_update_slice(whole, piece, (0, (me ^ mask) * depth, 0))  14.7 us
    dot_general x3, matrix products, on_device(): jnp.dot(gathered, weights[j], preferred_element_type=jnp.float32)  14.6 us
    all_gather x1, blocking collectives, on_device(): states = lax.all_gather(own, 'seq').astype(jnp.float32)  10.3 us
    dot_general x6, matrix products, times(): jnp.dot(jnp.asarray(matrix), value, precision=lax.Precision.HIGH, preferr...  9.59 us
    ppermute x1, waiting for transfers between devices, gather_weights(): lax.ppermute(onward, 'seq', [(s, s ^ (4 if s % 2 == 0 else 2)) for s in r...  8.61 us
    ppermute x2, starting transfers between devices, from_behind(): lax.ppermute(value, axis, [(source, source + 1) for source in range(count...  7.66 us
  transfers between devices with their start and end apart: 10, of which 5 were waited for; matrix products, arithmetic and copies ran while one was open for 24% of the time, Pallas kernels for 0%

profile of v1, /device:TPU:0, one launch (start us, length us, event | category | flops | bytes accessed | tf_op | source)
XLA Modules:
  0.0 185.8 jit_solution(2809379831962530014)
XLA Ops:
  6.5 0.7 all-gather.2.cloned.1.call-update
  7.3 3.0 %collective-permute-start = (bf16[3,1024,256]{2,1,0:T(8,128)(2,1)}, bf16[3,1024,256]{2,1,0:T(8,128)(2,1)S(1)}, u32[]{:S(2)}, u32[]{:S(2)}) collective-permute-start(bf16[3,1024,256]{2,1,0:T(8,128)(2,1)} %param.13), channel_id=1, source_target_pairs={{0,8},{4,12},{8,0},{12,4},{16,24},{20,28},{24,16},{28,20},{1,9},{5... | collective-permute-start | bytes 4718600 | tf_op jit(solution)/shard_map/ppermute | solution.py:20
  10.3 1.5 collective-permute-start.1
  11.8 5.4 %broadcast_in_dim.22 = bf16[3,8192,256]{2,1,0:T(8,128)(2,1)} broadcast(bf16[]{:T(256)} %constant.119.clone.1), dimensions={} | broadcast | bytes 12582914 | tf_op jit(solution)/shard_map/broadcast_in_dim | solution.py:35
  17.2 2.9 %constant_dynamic-update-slice_fusion.8 = bf16[3,8192,256]{2,1,0:T(8,128)(2,1)} fusion(bf16[3,8192,256]{2,1,0:T(8,128)(2,1)} %broadcast_in_dim.22, bf16[3,1024,256]{2,1,0:T(8,128)(2,1)} %param.13, s32[]{:T(128)S(6)} %select_n.116), kind=kLoop, calls=%fused_computation.128 | loop fusion | bytes 3145732 | tf_op jit(solution)/shard_map/dynamic_update_slice | solution.py:37
  20.1 0.2 fusion.62
  20.2 24.6 %collective-permute-done = bf16[3,1024,256]{2,1,0:T(8,128)(2,1)S(1)} collective-permute-done((bf16[3,1024,256]{2,1,0:T(8,128)(2,1)}, bf16[3,1024,256]{2,1,0:T(8,128)(2,1)S(1)}, u32[]{:S(2)}, u32[]{:S(2)}) %collective-permute-start) | collective-permute-done | bytes 1572896 | tf_op jit(solution)/shard_map/ppermute | solution.py:20
  44.9 1.2 constant_dynamic-update-slice_fusion.7
  46.1 0.2 collective-permute-done.1
  46.3 2.2 %broadcast_select_fusion = (bf16[3,1024,256]{2,1,0:T(8,128)(2,1)}, bf16[3,8192,256]{2,1,0:T(8,128)(2,1)}) fusion(bf16[3,1024,256]{2,1,0:T(8,128)(2,1)S(1)} %collective-permute-done, bf16[3,1024,256]{2,1,0:T(8,128)(2,1)S(1)} %collective-permute-done.1, pred[]{:T(512)S(6)} %eq.22, bf16[3,8192,256]{2,1,0:T(8,128)(2,1)} %constant_dynamic-update-slice_fusion.7, ...), kind=kLoop, calls=%fused_computation.9 | loop fusion | flops 786432 | bytes 6291461 | tf_op jit(solution)/shard_map/jit(_where)/select_n | solution.py:30
  48.6 1.6 collective-permute-start.2
  50.2 1.0 fusion.21
  51.2 0.8 copy-done.2
  52.1 0.0 copy-start.17
  52.1 0.1 exponential_multiply_fusion
  52.2 2.4 %multiply_reduce_fusion.2 = f32[32,12,256]{2,1,0:T(8,128)} fusion(f32[16,256]{1,0:T(8,128)S(1)} %get-tuple-element.32, f32[12,16,256]{2,1,0:T(8,128)S(1)} %exponential_multiply_fusion, f32[32,16,256]{2,1,0:T(8,128)S(1)} %slice.186), kind=kLoop, calls=%fused_computation.2 | loop fusion | flops 4620288 | bytes 1130496 | tf_op jit(solution)/shard_map/reduce_sum | solution.py:84
  54.6 0.6 and_select_fusion
  55.2 2.1 %copy.46 = f32[12,32,256]{2,1,0:T(8,128)} copy(f32[12,32,256]{2,0,1:T(8,128)} %bitcast.64) | data formatting | bytes 786432 | tf_op jit(solution)/shard_map/transpose | solution.py:85
  57.3 1.0 slice.187
  58.3 0.7 copy.47
  59.0 0.6 fusion.69
  59.6 0.5 collective-permute-start.5
  60.1 0.6 slice_reduce_fusion.6
  60.7 8.6 %collective-permute-done.2 = bf16[3,1024,256]{2,1,0:T(8,128)(2,1)} collective-permute-done((bf16[3,1024,256]{2,1,0:T(8,128)(2,1)}, bf16[3,1024,256]{2,1,0:T(8,128)(2,1)}, u32[]{:S(2)}, u32[]{:S(2)}) %collective-permute-start.2) | collective-permute-done | bytes 1572896 | tf_op jit(solution)/shard_map/ppermute | solution.py:31
  69.3 0.8 fusion.67
  70.1 1.6 constant_dynamic-update-slice_fusion
  71.7 2.5 %convolution_multiply_fusion = f32[768,256]{0,1:T(8,128)} fusion(f32[768,128]{1,0:T(8,128)} %constant.144.clone, f32[128,256]{1,0:T(8,128)} %param.15), kind=kOutput, calls=%fused_computation.10 | convolution fusion | flops 151191552 | bytes 1310720 | tf_op jit(solution)/shard_map/dot_general | solution.py:61
  74.3 2.0 %fusion.3 = f32[768,256]{0,1:T(8,128)} fusion(f32[384,256]{1,0:T(8,128)S(1)} %copy-done.12, f32[768,384]{1,0:T(8,128)S(1)} %copy-done.1), kind=kOutput, calls=%fused_computation.12 | convolution fusion | flops 453181440 | bytes 2359296 | tf_op jit(solution)/shard_map/dot_general | solution.py:61
  76.3 2.6 %constant_dynamic-update-slice_fusion.5 = bf16[3,8192,256]{2,1,0:T(8,128)(2,1)} fusion(bf16[3,8192,256]{2,1,0:T(8,128)(2,1)} %get-tuple-element.29, bf16[3,1024,256]{2,1,0:T(8,128)(2,1)} %collective-permute-done.2, s32[]{:T(128)S(6)} %select_n.122), kind=kLoop, calls=%fused_computation.125 | loop fusion | bytes 3145732 | tf_op jit(solution)/shard_map/dynamic_update_slice | solution.py:37
  79.0 2.7 %constant_dynamic-update-slice_fusion.4 = bf16[3,8192,256]{2,1,0:T(8,128)(2,1)} fusion(bf16[3,8192,256]{2,1,0:T(8,128)(2,1)} %constant_dynamic-update-slice_fusion.5, bf16[3,1024,256]{2,1,0:T(8,128)(2,1)} %collective-permute-done.3, s32[]{:T(128)S(6)} %select_n.123), kind=kLoop, calls=%fused_computation.124 | loop fusion | bytes 3145732 | tf_op jit(solution)/shard_map/dynamic_update_slice | solution.py:37
  81.7 2.7 %constant_dynamic-update-slice_fusion.3 = bf16[3,8192,256]{2,1,0:T(8,128)(2,1)} fusion(bf16[3,8192,256]{2,1,0:T(8,128)(2,1)} %constant_dynamic-update-slice_fusion.4, bf16[3,1024,256]{2,1,0:T(8,128)(2,1)} %collective-permute-done.4, s32[]{:T(128)S(6)} %select_n.124), kind=kLoop, calls=%fused_computation.123 | loop fusion | bytes 3145732 | tf_op jit(solution)/shard_map/dynamic_update_slice | solution.py:37
  84.3 1.3 constant_dynamic-update-slice_fusion.2
  85.6 1.3 constant_dynamic-update-slice_fusion.1
  86.9 40.1 %all-gather.2.cloned.1.call-done = bf16[384,8192]{1,0:T(8,128)(2,1)} async-done(((bf16[384,2048]{1,0:T(8,128)(2,1)}), bf16[384,8192]{1,0:T(8,128)(2,1)}) %all-gather.2.cloned.1.call-update) | async-done | bytes 6291472 | tf_op jit(solution)/shard_map/all_gather | solution.py:75
  127.0 6.6 %fusion.18 = bf16[384,256]{0,1:T(8,128)(2,1)S(1)} fusion(bf16[384,8192]{1,0:T(8,128)(2,1)} %all-gather.2.cloned.1.call-done, bf16[3,8192,256]{2,1,0:T(8,128)(2,1)} %constant_dynamic-update-slice_fusion.1), kind=kOutput, calls=%fused_computation.35 | convolution fusion | flops 1610711040 | bytes 10682368 | tf_op jit(solution)/shard_map/dot_general | solution.py:102
  133.6 1.0 copy-done
  134.6 5.4 %fusion.19 = bf16[384,256]{0,1:T(8,128)(2,1)S(1)} fusion(bf16[384,8192]{1,0:T(8,128)(2,1)} %all-gather.2.cloned.1.call-done, bf16[3,8192,256]{2,1,0:T(8,128)(2,1)S(1)} %copy-done), kind=kOutput, calls=%fused_computation.36 | convolution fusion | flops 1610711040 | bytes 10682368 | tf_op jit(solution)/shard_map/dot_general | solution.py:102
  140.1 2.6 %fusion.17 = bf16[384,256]{0,1:T(8,128)(2,1)S(1)} fusion(bf16[384,8192]{1,0:T(8,128)(2,1)S(1)} %bitcast.72, bf16[3,8192,256]{2,1,0:T(8,128)(2,1)S(1)} %copy-done), kind=kOutput, calls=%fused_computation.34 | convolution fusion | flops 1610711040 | bytes 10682368 | tf_op jit(solution)/shard_map/dot_general | solution.py:102
  142.7 0.8 pad_maximum_fusion
  143.5 2.0 %collective-permute-start.7 = (bf16[6,768]{0,1:T(8,128)(2,1)}, bf16[6,768]{0,1:T(8,128)(2,1)S(1)}, u32[]{:S(2)}, u32[]{:S(2)}) collective-permute-start(bf16[6,768]{0,1:T(8,128)(2,1)} %pad_maximum_fusion), channel_id=1, source_target_pairs={{0,4},{4,8},{8,12},{12,16},{16,20},{20,24},{24,28},{1,5},{5,9},{9,... | collective-permute-start | bytes 27656 | tf_op jit(solution)/shard_map/ppermute | solution.py:15
  145.6 0.8 slice.200
  146.4 0.3 collective-permute-done.7
  146.7 0.3 maximum_convert_fusion
  147.1 2.9 %fusion.7 = f32[384,768]{0,1:T(8,128)S(1)} fusion(f32[390,768]{0,1:T(8,128)S(1)} %maximum_convert_fusion, f32[768]{0:T(1024)S(1)} %mul.469, f32[768]{0:T(1024)S(1)} %mul.466, f32[768]{0:T(1024)S(1)} %mul.463, f32[768]{0:T(1024)S(1)} %mul.460, f32[768]{0:T(1024)S(1)} %mul.457, f32[768]{0:T(1024)S(1)} %mul.454, f32[768]{0:T(1024)S(1)} %mul.443), kind=kLoop, calls=%fused_computation.18 | loop fusion | flops 3833856 | bytes 9458688 | tf_op jit(solution)/shard_map/add | solution.py:107
  150.0 0.6 slice.195
  150.6 1.5 fusion.71
  152.1 0.1 copy.53
  152.3 5.7 %collective-permute-start.8 = (bf16[128,256]{0,1:T(8,128)(2,1)}, bf16[128,256]{0,1:T(8,128)(2,1)}, u32[]{:S(2)}, u32[]{:S(2)}) collective-permute-start(bf16[128,256]{0,1:T(8,128)(2,1)} %slice.195), channel_id=1, source_target_pairs={{0,4},{4,8},{8,12},{12,16},{16,20},{20,24},{24,28},{1,5},{5,9},{9,... | collective-permute-start | bytes 196616 | tf_op jit(solution)/shard_map/ppermute | solution.py:15
  158.0 0.5 multiply_reduce_fusion.1
  158.5 0.2 multiply_reduce_fusion.4
  158.7 10.3 %all_gather.8 = bf16[8,32,256]{2,1,0:T(8,128)(2,1)S(1)} all-gather(bf16[1,32,256]{2,1,0:T(8,128)(2,1)S(1)} %pad_maximum_fusion.2), channel_id=1, replica_groups=mesh['seq'=8,'ch'=4] {'seq'}, dimensions={0}, use_global_device_ids=true | all-gather | bytes 147456 | tf_op jit(solution)/shard_map/all_gather | solution.py:119
  169.0 0.1 subtract_reduce_fusion
  169.2 0.1 fusion.24
  169.3 0.3 copy.54
  169.6 0.3 copy-done.10
  170.0 1.3 multiply_reduce_fusion
  171.2 1.9 %copy.55 = f32[384,256]{0,1:T(8,128)} copy(f32[384,256]{1,0:T(8,128)} %bitcast.68) | data formatting | bytes 786432 | tf_op jit(solution)/shard_map/reshape | solution.py:136
  173.1 1.4 fusion.72
  174.6 0.0 copy-start.15
  174.6 0.7 fusion.34
  175.3 0.3 copy-done.13
  175.6 0.2 copy-done.15
  175.8 1.4 fusion.16
  177.2 1.7 copy.56
  (72 shorter events, 0.3 us)
Async XLA Ops:
  6.5 120.5 %all-gather.2.cloned.1.call-start = ((), (), s32[]{:S(2)}) async-start(), calls=%async_computation | async-start | bytes 7864320 | tf_op jit(solution)/shard_map/all_gather | solution.py:75
  7.3 37.6 %collective-permute-start = (bf16[3,1024,256]{2,1,0:T(8,128)(2,1)}, bf16[3,1024,256]{2,1,0:T(8,128)(2,1)S(1)}, u32[]{:S(2)}, u32[]{:S(2)}) collective-permute-start(bf16[3,1024,256]{2,1,0:T(8,128)(2,1)} %param.13), channel_id=1, source_target_pairs={{0,8},{4,12},{8,0},{12,4},{16,24},{20,28},{24,16},{28,20},{1,9},{5... | collective-permute-start | bytes 4718600 | tf_op jit(solution)/shard_map/ppermute | solution.py:20
  10.3 36.1 %collective-permute-start.1 = (bf16[3,1024,256]{2,1,0:T(8,128)(2,1)}, bf16[3,1024,256]{2,1,0:T(8,128)(2,1)S(1)}, u32[]{:S(2)}, u32[]{:S(2)}) collective-permute-start(bf16[3,1024,256]{2,1,0:T(8,128)(2,1)} %param.13), channel_id=1, source_target_pairs={{0,16},{4,20},{8,24},{12,28},{16,0},{20,4},{24,8},{28,12},{1,17},{... | collective-permute-start | bytes 4718600 | tf_op jit(solution)/shard_map/ppermute | solution.py:20
  11.8 67.2 %collective-permute-start.3 = (bf16[3,1024,256]{2,1,0:T(8,128)(2,1)}, bf16[3,1024,256]{2,1,0:T(8,128)(2,1)}, u32[]{:S(2)}, u32[]{:S(2)}) collective-permute-start(bf16[3,1024,256]{2,1,0:T(8,128)(2,1)} %param.13), channel_id=1, source_target_pairs={{0,4},{4,0},{8,12},{12,8},{16,20},{20,16},{24,28},{28,24},{1,5},{5... | collective-permute-start | bytes 4718600 | tf_op jit(solution)/shard_map/ppermute | solution.py:20
  11.8 8.3 %copy-start.21 = (s32[16]{0:T(128)}, s32[16]{0:T(128)S(1)}, u32[]{:S(2)}) copy-start(s32[16]{0:T(128)S(1)} %multiply_add_fusion) | copy-start | bytes 196
  46.1 4.1 %copy-start.19 = (f32[16,256]{1,0:T(8,128)S(1)}, f32[16,256]{1,0:T(8,128)}, u32[]{:S(2)}) copy-start(f32[16,256]{1,0:T(8,128)} %param.17) | copy-start | bytes 49156
  46.1 4.1 %copy-start.20 = (f32[16,256]{1,0:T(8,128)S(1)}, f32[16,256]{1,0:T(8,128)}, u32[]{:S(2)}) copy-start(f32[16,256]{1,0:T(8,128)} %param.16) | copy-start | bytes 49156
  46.3 2.2 %copy-start.14 = (bf16[3,1024,256]{2,1,0:T(8,128)(2,1)}, bf16[3,1024,256]{2,1,0:T(8,128)(2,1)S(1)}, u32[]{:S(2)}) copy-start(bf16[3,1024,256]{2,1,0:T(8,128)(2,1)S(1)} %collective-permute-done.1) | copy-start | bytes 4718596
  48.6 20.7 %collective-permute-start.2 = (bf16[3,1024,256]{2,1,0:T(8,128)(2,1)}, bf16[3,1024,256]{2,1,0:T(8,128)(2,1)}, u32[]{:S(2)}, u32[]{:S(2)}) collective-permute-start(bf16[3,1024,256]{2,1,0:T(8,128)(2,1)} %get-tuple-element.28), channel_id=1, source_target_pairs={{0,16},{4,12},{8,24},{12,4},{16,0},{20,28},{24,8},{28,20},{1,17},{... | collective-permute-start | bytes 4718600 | tf_op jit(solution)/shard_map/ppermute | solution.py:31
  51.2 0.8 copy-start.2
  52.1 8.0 %copy-start.17 = (f32[7,3,256]{2,0,1:T(8,128)S(1)}, f32[7,3,256]{2,0,1:T(8,128)}, u32[]{:S(2)}) copy-start(f32[7,3,256]{2,0,1:T(8,128)} %param.14) | copy-start | bytes 64516
  52.2 93.2 %copy-start.9 = (f32[12,16,256]{2,1,0:T(8,128)}, f32[12,16,256]{2,1,0:T(8,128)S(1)}, u32[]{:S(2)}) copy-start(f32[12,16,256]{2,1,0:T(8,128)S(1)} %exponential_multiply_fusion) | copy-start | bytes 589828
  54.6 27.1 %collective-permute-start.4 = (bf16[3,1024,256]{2,1,0:T(8,128)(2,1)S(1)}, bf16[3,1024,256]{2,1,0:T(8,128)(2,1)}, u32[]{:S(2)}, u32[]{:S(2)}) collective-permute-start(bf16[3,1024,256]{2,1,0:T(8,128)(2,1)S(1)} %collective-permute-done), channel_id=1, source_target_pairs={{0,4},{4,0},{8,12},{12,8},{16,20},{20,16},{24,28},{28,24},{1,5},{5... | collective-permute-start | bytes 4718600 | tf_op jit(solution)/shard_map/ppermute | solution.py:20
  55.2 19.0 %copy-start.1 = (f32[768,384]{1,0:T(8,128)S(1)}, f32[768,384]{1,0:T(8,128)}, u32[]{:S(2)}) copy-start(f32[768,384]{1,0:T(8,128)} %constant.143.clone) | copy-start | bytes 3538948
  59.6 24.8 %collective-permute-start.5 = (bf16[3,1024,256]{2,1,0:T(8,128)(2,1)}, bf16[3,1024,256]{2,1,0:T(8,128)(2,1)S(1)}, u32[]{:S(2)}, u32[]{:S(2)}) collective-permute-start(bf16[3,1024,256]{2,1,0:T(8,128)(2,1)} %copy-done.14), channel_id=1, source_target_pairs={{0,4},{4,0},{8,12},{12,8},{16,20},{20,16},{24,28},{28,24},{1,5},{5... | collective-permute-start | bytes 4718600 | tf_op jit(solution)/shard_map/ppermute | solution.py:20
  69.3 16.3 %collective-permute-start.6 = (bf16[3,1024,256]{2,1,0:T(8,128)(2,1)}, bf16[3,1024,256]{2,1,0:T(8,128)(2,1)S(1)}, u32[]{:S(2)}, u32[]{:S(2)}) collective-permute-start(bf16[3,1024,256]{2,1,0:T(8,128)(2,1)} %collective-permute-done.2), channel_id=1, source_target_pairs={{0,4},{4,0},{8,12},{12,8},{16,20},{20,16},{24,28},{28,24},{1,5},{5... | collective-permute-start | bytes 4718600 | tf_op jit(solution)/shard_map/ppermute | solution.py:20
  71.7 2.5 %copy-start.12 = (f32[384,256]{1,0:T(8,128)S(1)}, f32[384,256]{1,0:T(8,128)}, u32[]{:S(2)}) copy-start(f32[384,256]{1,0:T(8,128)} %constant_dynamic-update-slice_fusion) | copy-start | bytes 1179652
  127.0 7.6 %copy-start = (bf16[3,8192,256]{2,1,0:T(8,128)(2,1)S(1)}, bf16[3,8192,256]{2,1,0:T(8,128)(2,1)}, u32[]{:S(2)}) copy-start(bf16[3,8192,256]{2,1,0:T(8,128)(2,1)} %constant_dynamic-update-slice_fusion.1) | copy-start | bytes 37748740
  127.0 13.1 %slice-start = ((s8[6291456]{0:T(1024)(128)(4,1)}), s8[4194304]{0:T(1024)(128)(4,1)S(1)}, s32[]{:S(2)}) async-start(s8[6291456]{0:T(1024)(128)(4,1)} %bitcast.71), calls=%async_computation.1 | async-start | bytes 8388608
  134.6 5.4 %slice-start.1 = ((s8[6291456]{0:T(1024)(128)(4,1)}), s8[2097152]{0:T(1024)(128)(4,1)S(1)}, s32[]{:S(2)}) async-start(s8[6291456]{0:T(1024)(128)(4,1)} %bitcast.71), calls=%async_computation.2 | async-start | bytes 4194304
  140.1 5.4 %copy-start.18 = (f32[3,256]{1,0:T(4,128)S(1)}, f32[3,256]{1,0:T(4,128)}, u32[]{:S(2)}) copy-start(f32[3,256]{1,0:T(4,128)} %get-tuple-element.21) | copy-start | bytes 9220
  142.7 2.9 %copy-start.4 = (f32[33,16,256]{2,1,0:T(8,128)S(1)}, f32[33,16,256]{2,1,0:T(8,128)}, u32[]{:S(2)}) copy-start(f32[33,16,256]{2,1,0:T(8,128)} %get-tuple-element.31) | copy-start | bytes 1622020
  143.5 3.2 %collective-permute-start.7 = (bf16[6,768]{0,1:T(8,128)(2,1)}, bf16[6,768]{0,1:T(8,128)(2,1)S(1)}, u32[]{:S(2)}, u32[]{:S(2)}) collective-permute-start(bf16[6,768]{0,1:T(8,128)(2,1)} %pad_maximum_fusion), channel_id=1, source_target_pairs={{0,4},{4,8},{8,12},{12,16},{16,20},{20,24},{24,28},{1,5},{5,9},{9,... | collective-permute-start | bytes 27656 | tf_op jit(solution)/shard_map/ppermute | solution.py:15
  152.1 6.4 %copy-start.11 = (f32[32,16,256]{2,1,0:T(8,128)S(1)}, f32[32,16,256]{2,1,0:T(8,128)}, u32[]{:S(2)}) copy-start(f32[32,16,256]{2,1,0:T(8,128)} %slice.200) | copy-start | bytes 1572868
  152.3 20.9 %collective-permute-start.8 = (bf16[128,256]{0,1:T(8,128)(2,1)}, bf16[128,256]{0,1:T(8,128)(2,1)}, u32[]{:S(2)}, u32[]{:S(2)}) collective-permute-start(bf16[128,256]{0,1:T(8,128)(2,1)} %slice.195), channel_id=1, source_target_pairs={{0,4},{4,8},{8,12},{12,16},{16,20},{20,24},{24,28},{1,5},{5,9},{9,... | collective-permute-start | bytes 196616 | tf_op jit(solution)/shard_map/ppermute | solution.py:15
  158.0 11.1 %copy-start.22 = (pred[8]{0:T(512)(128)(4,1)S(1)}, pred[8]{0:T(512)(128)(4,1)}, u32[]{:S(2)}) copy-start(pred[8]{0:T(512)(128)(4,1)} %fusion.69) | copy-start | bytes 28
  158.0 11.2 %copy-start.3 = (f32[33,16,256]{2,1,0:T(8,128)S(1)}, f32[33,16,256]{2,1,0:T(8,128)}, u32[]{:S(2)}) copy-start(f32[33,16,256]{2,1,0:T(8,128)} %copy-done.2) | copy-start | bytes 1622020
  158.0 11.2 %copy-start.5 = (f32[33,16,256]{2,1,0:T(8,128)S(1)}, f32[33,16,256]{2,1,0:T(8,128)}, u32[]{:S(2)}) copy-start(f32[33,16,256]{2,1,0:T(8,128)} %get-tuple-element.31) | copy-start | bytes 1622020
  169.0 0.9 copy-start.10
  170.0 4.6 %copy-start.6 = (f32[768,256]{0,1:T(8,128)S(1)}, f32[768,256]{0,1:T(8,128)}, u32[]{:S(2)}) copy-start(f32[768,256]{0,1:T(8,128)} %convolution_multiply_fusion) | copy-start | bytes 2359300
  170.0 4.6 %copy-start.7 = (f32[768,256]{0,1:T(8,128)S(1)}, f32[768,256]{0,1:T(8,128)}, u32[]{:S(2)}) copy-start(f32[768,256]{0,1:T(8,128)} %fusion.71) | copy-start | bytes 2359300
  170.0 4.6 %copy-start.8 = (f32[768,256]{0,1:T(8,128)S(1)}, f32[768,256]{0,1:T(8,128)}, u32[]{:S(2)}) copy-start(f32[768,256]{0,1:T(8,128)} %fusion.3) | copy-start | bytes 2359300
  173.1 1.5 copy-start.16
  174.6 1.0 copy-start.13
  174.6 1.2 copy-start.15
Sparse Core Ops, SparseCore 0:
  8.9 118.0 all-gather.1

commit v2 on v1

--- a/solution.py
+++ b/solution.py
@@ -38,6 +38,42 @@
     return whole
 
 
+def project(tokens, in_weight):
+    count = lax.axis_size("ch")
+    if count != 4:
+        gathered = lax.all_gather(tokens, "ch", axis=1, tiled=True)
+        weights = gather_weights(in_weight)
+        blocks = [
+            jnp.dot(gathered, weights[j], preferred_element_type=jnp.float32) for j in range(3)
+        ]
+        return jnp.concatenate(blocks, axis=1)
+    me = lax.axis_index("ch")
+    depth = tokens.shape[1]
+
+    def shift(value, pairs):
+        return lax.ppermute(value, "ch", pairs)
+
+    up_1 = shift(tokens, [(0, 1), (1, 2), (2, 3)])
+    down_1 = shift(tokens, [(1, 0), (2, 1), (3, 2)])
+    up_2 = shift(up_1, [(1, 2), (2, 3)])
+    down_2 = shift(down_1, [(1, 0), (2, 1)])
+    up_3 = shift(up_2, [(2, 3)])
+    down_3 = shift(down_2, [(1, 0)])
+    weights = gather_weights(in_weight)
+
+    def add_rows(value, source):
+        portion = lax.dynamic_slice_in_dim(weights, source * depth, depth, 1)
+        return jnp.concatenate(
+            [jnp.dot(value, portion[j], preferred_element_type=jnp.float32) for j in range(3)],
+            axis=1,
+        )
+
+    total = add_rows(tokens, me)
+    total += add_rows(up_1, (me + 3) % 4) + add_rows(down_1, (me + 1) % 4)
+    total += add_rows(up_2 + down_2, (me + 2) % 4)
+    return total + add_rows(up_3 + down_3, 3 - me)
+
+
 def phase_angle(steps, mode_count):
     period = 4 * mode_count
     odd_numbers = 2 * jnp.arange(mode_count) + 1
@@ -72,8 +108,7 @@
     half = 2 * modes
     laps = rows // half
 
-    gathered = lax.all_gather(tokens, "ch", axis=1, tiled=True)
-    weights = gather_weights(in_weight)
+    features = project(tokens, in_weight).astype(jnp.bfloat16)
 
     coef = residue * jnp.sqrt(-jnp.expm1(-2.0 * decay_rate))
     near_cos, near_sin = damped(decay_rate, jnp.arange(half + 1))
@@ -99,8 +134,6 @@
     ahead_im = (coef[None] * near_sin[1:]).transpose(1, 0, 2)
     back_re, back_im, back_far = near_cos[:half][::-1], near_sin[:half][::-1], far[::-1]
 
-    blocks = [jnp.dot(gathered, weights[j], preferred_element_type=jnp.float32) for j in range(3)]
-    features = jnp.concatenate(blocks, axis=1).astype(jnp.bfloat16)
     head = from_behind(features[rows - (SHORT - 1) :], "seq")
     extended = jnp.concatenate([head, features], axis=0).astype(jnp.float32)
     short_taps = short_filter.reshape(SHORT, 3 * width)

time: 186 us -> 179 us (0.962)
  waiting for transfers between devices: 74.6 us -> 56.8 us
  between operations: 13.8 us -> 0.56 us
  matrix products: 24.1 us -> 34.9 us
  starting transfers between devices: 14.3 us -> 21.8 us
  blocking collectives: 10.3 us -> 13.4 us
  other arithmetic: 15.8 us -> 18.4 us
    all_gather x1 -> x0, waiting for transfers between devices: 40.1 us -> none  [on_device(): gathered = lax.all_gather(tokens, 'ch', axis=1, tiled=True)]
    ppermute x0 -> x6, waiting for transfers between devices: none -> 34.5 us  [shift(): return lax.ppermute(value, 'ch', pairs)]
    dot_general x3 -> x15, matrix products: 14.6 us -> 25.7 us  [add_rows(): jnp.dot(value, portion[j], preferred_element_type=jnp.float32)]
    ppermute x0 -> x6, starting transfers between devices: none -> 10.2 us  [shift(): return lax.ppermute(value, 'ch', pairs)]
    ppermute x1, waiting for transfers between devices: 8.61 us -> 2 us  [gather_weights(): lax.ppermute(onward, 'seq', [(s, s ^ (4 if s % 2 == 0 else 2)) for s in r...]
    ppermute x6, waiting for transfers between devices: 24.9 us -> 20.3 us  [flip(): return lax.ppermute(value, 'seq', [(s, s ^ mask) for s in range(count)])]
    all_gather x1, blocking collectives: 10.3 us -> 13.4 us  [on_device(): states = lax.all_gather(own, 'seq').astype(jnp.float32)]
    ppermute x2, starting transfers between devices: 7.66 us -> 4.84 us  [from_behind(): lax.ppermute(value, axis, [(source, source + 1) for source in range(count...]
  transfers between devices with their start and end apart: 10 -> 15, of which waited for: 5 -> 6; matrix products, arithmetic and copies ran while one was open for 24% -> 30% of each run, Pallas kernels for 0% -> 0%
where the time goes in v2:
time: 179 us
  waiting for transfers between devices  56.8 us (32%)
  matrix products  34.9 us (19%)
  local copies, waits for them, and re-layouts  32.6 us (18%)
  starting transfers between devices  21.8 us (12%)
  other arithmetic  18.4 us (10%)
  blocking collectives  13.4 us (7%)
    ppermute x6, waiting for transfers between devices, shift(): return lax.ppermute(value, 'ch', pairs)  34.5 us
    dot_general x15, matrix products, add_rows(): jnp.dot(value, portion[j], preferred_element_type=jnp.float32)  25.7 us
    ppermute x6, waiting for transfers between devices, flip(): return lax.ppermute(value, 'seq', [(s, s ^ mask) for s in range(count)])  20.3 us
    all_gather x1, blocking collectives, on_device(): states = lax.all_gather(own, 'seq').astype(jnp.float32)  13.4 us
    dynamic_update_slice x7, local copies, waits for them, and re-layouts, gather_weights(): whole = lax.dynamic_update_slice(whole, piece, (0, (me ^ mask) * depth, 0))  13.2 us
    ppermute x6, starting transfers between devices, shift(): return lax.ppermute(value, 'ch', pairs)  10.2 us
    dot_general x6, matrix products, times(): jnp.dot(jnp.asarray(matrix), value, precision=lax.Precision.HIGH, preferr...  9.2 us
    broadcast_in_dim x1, local copies, waits for them, and re-layouts, gather_weights(): whole = jnp.zeros((3, count * depth, weight.shape[2]), weight.dtype)  5.36 us
  transfers between devices with their start and end apart: 15, of which 6 were waited for; matrix products, arithmetic and copies ran while one was open for 30% of the time, Pallas kernels for 0%

profile of v2, /device:TPU:0, one launch (start us, length us, event | category | flops | bytes accessed | tf_op | source)
XLA Modules:
  0.0 178.5 jit_solution(16745189676121361866)
XLA Ops:
  0.0 2.9 %collective-permute-start = (bf16[3,1024,256]{2,1,0:T(8,128)(2,1)}, bf16[3,1024,256]{2,1,0:T(8,128)(2,1)S(1)}, u32[]{:S(2)}, u32[]{:S(2)}) collective-permute-start(bf16[3,1024,256]{2,1,0:T(8,128)(2,1)} %param.13), channel_id=1, source_target_pairs={{0,8},{4,12},{8,0},{12,4},{16,24},{20,28},{24,16},{28,20},{1,9},{5... | collective-permute-start | bytes 4718600 | tf_op jit(solution)/shard_map/ppermute | solution.py:20
  2.9 1.5 collective-permute-start.1
  4.5 4.7 %collective-permute-start.7 = (bf16[384,2048]{1,0:T(8,128)(2,1)}, bf16[384,2048]{1,0:T(8,128)(2,1)}, u32[]{:S(2)}, u32[]{:S(2)}) collective-permute-start(bf16[384,2048]{1,0:T(8,128)(2,1)} %param.12), channel_id=1, source_target_pairs={{0,1},{1,2},{2,3},{4,5},{5,6},{6,7},{8,9},{9,10},{10,11},{12,13},{... | collective-permute-start | bytes 4718600 | tf_op jit(solution)/shard_map/ppermute | solution.py:54
  9.1 1.3 collective-permute-start.8
  10.5 5.4 %broadcast_in_dim.22 = bf16[3,8192,256]{2,1,0:T(8,128)(2,1)} broadcast(bf16[]{:T(256)} %constant.137.clone.1), dimensions={} | broadcast | bytes 12582914 | tf_op jit(solution)/shard_map/broadcast_in_dim | solution.py:35
  15.9 1.3 constant_dynamic-update-slice_fusion.8
  17.3 20.2 %collective-permute-done = bf16[3,1024,256]{2,1,0:T(8,128)(2,1)S(1)} collective-permute-done((bf16[3,1024,256]{2,1,0:T(8,128)(2,1)}, bf16[3,1024,256]{2,1,0:T(8,128)(2,1)S(1)}, u32[]{:S(2)}, u32[]{:S(2)}) %collective-permute-start) | collective-permute-done | bytes 1572896 | tf_op jit(solution)/shard_map/ppermute | solution.py:20
  37.5 1.3 constant_dynamic-update-slice_fusion.7
  39.2 2.1 %broadcast_select_fusion = (bf16[3,1024,256]{2,1,0:T(8,128)(2,1)}, bf16[3,8192,256]{2,1,0:T(8,128)(2,1)}) fusion(bf16[3,1024,256]{2,1,0:T(8,128)(2,1)S(1)} %collective-permute-done, bf16[3,1024,256]{2,1,0:T(8,128)(2,1)S(1)} %collective-permute-done.1, pred[]{:T(512)S(6)} %eq.25, bf16[3,8192,256]{2,1,0:T(8,128)(2,1)} %constant_dynamic-update-slice_fusion.7, ...), kind=kLoop, calls=%fused_computation.3 | loop fusion | flops 786432 | bytes 6291461 | tf_op jit(solution)/shard_map/jit(_where)/select_n | solution.py:30
  41.3 1.8 %collective-permute-start.2 = (bf16[3,1024,256]{2,1,0:T(8,128)(2,1)}, bf16[3,1024,256]{2,1,0:T(8,128)(2,1)}, u32[]{:S(2)}, u32[]{:S(2)}) collective-permute-start(bf16[3,1024,256]{2,1,0:T(8,128)(2,1)} %get-tuple-element.28), channel_id=1, source_target_pairs={{0,16},{4,12},{8,24},{12,4},{16,0},{20,28},{24,8},{28,20},{1,17},{... | collective-permute-start | bytes 4718600 | tf_op jit(solution)/shard_map/ppermute | solution.py:31
  43.2 1.1 fusion.21
  44.2 0.9 copy-done.6
  45.1 0.8 slice.232
  46.1 0.8 collective-permute-start.9
  46.8 1.0 collective-permute-done.8
  47.9 1.3 collective-permute-start.10
  49.2 3.4 %multiply_reduce_fusion.2 = f32[32,12,256]{2,1,0:T(8,128)} fusion(f32[16,256]{1,0:T(8,128)S(1)} %get-tuple-element.32, f32[12,16,256]{2,1,0:T(8,128)S(1)} %exponential_multiply_fusion, f32[32,16,256]{2,1,0:T(8,128)} %slice.232), kind=kLoop, calls=%fused_computation.2 | loop fusion | flops 4620288 | bytes 1130496 | tf_op jit(solution)/shard_map/reduce_sum | solution.py:119
  53.1 2.0 %copy.46 = f32[12,32,256]{2,1,0:T(8,128)} copy(f32[12,32,256]{2,0,1:T(8,128)} %bitcast.106) | data formatting | bytes 786432 | tf_op jit(solution)/shard_map/transpose | solution.py:120
  55.2 1.6 slice.233
  56.8 1.6 copy.47
  60.0 2.0 %collective-permute-done.2 = bf16[3,1024,256]{2,1,0:T(8,128)(2,1)} collective-permute-done((bf16[3,1024,256]{2,1,0:T(8,128)(2,1)}, bf16[3,1024,256]{2,1,0:T(8,128)(2,1)}, u32[]{:S(2)}, u32[]{:S(2)}) %collective-permute-start.2) | collective-permute-done | bytes 1572896 | tf_op jit(solution)/shard_map/ppermute | solution.py:31
  62.1 0.7 fusion.82
  62.8 1.6 constant_dynamic-update-slice_fusion
  64.4 2.4 %convolution_multiply_fusion = f32[768,256]{0,1:T(8,128)} fusion(f32[768,128]{1,0:T(8,128)} %constant.164.clone, f32[128,256]{1,0:T(8,128)S(1)} %copy-done.16), kind=kOutput, calls=%fused_computation.4 | convolution fusion | flops 151191552 | bytes 1310720 | tf_op jit(solution)/shard_map/dot_general | solution.py:97
  66.8 2.1 %fusion = f32[768,256]{0,1:T(8,128)} fusion(f32[384,256]{1,0:T(8,128)S(1)} %copy-done.11, f32[768,384]{1,0:T(8,128)S(1)} %copy-done.4), kind=kOutput, calls=%fused_computation.6 | convolution fusion | flops 453181440 | bytes 2359296 | tf_op jit(solution)/shard_map/dot_general | solution.py:97
  68.9 0.8 collective-permute-start.11
  69.7 16.8 %collective-permute-done.10 = bf16[384,2048]{1,0:T(8,128)(2,1)S(1)} collective-permute-done((bf16[384,2048]{1,0:T(8,128)(2,1)}, bf16[384,2048]{1,0:T(8,128)(2,1)S(1)}, u32[]{:S(2)}, u32[]{:S(2)}) %collective-permute-start.10) | collective-permute-done | bytes 1572896 | tf_op jit(solution)/shard_map/ppermute | solution.py:54
  86.5 1.5 collective-permute-start.12
  87.9 2.6 %constant_dynamic-update-slice_fusion.5 = bf16[3,8192,256]{2,1,0:T(8,128)(2,1)} fusion(bf16[3,8192,256]{2,1,0:T(8,128)(2,1)} %get-tuple-element.29, bf16[3,1024,256]{2,1,0:T(8,128)(2,1)} %collective-permute-done.2, s32[]{:T(128)S(6)} %select_n.149), kind=kLoop, calls=%fused_computation.151 | loop fusion | bytes 3145732 | tf_op jit(solution)/shard_map/dynamic_update_slice | solution.py:37
  90.6 2.7 %constant_dynamic-update-slice_fusion.4 = bf16[3,8192,256]{2,1,0:T(8,128)(2,1)} fusion(bf16[3,8192,256]{2,1,0:T(8,128)(2,1)} %constant_dynamic-update-slice_fusion.5, bf16[3,1024,256]{2,1,0:T(8,128)(2,1)} %collective-permute-done.3, s32[]{:T(128)S(6)} %select_n.150), kind=kLoop, calls=%fused_computation.150 | loop fusion | bytes 3145732 | tf_op jit(solution)/shard_map/dynamic_update_slice | solution.py:37
  93.3 2.7 %constant_dynamic-update-slice_fusion.3 = bf16[3,8192,256]{2,1,0:T(8,128)(2,1)} fusion(bf16[3,8192,256]{2,1,0:T(8,128)(2,1)} %constant_dynamic-update-slice_fusion.4, bf16[3,1024,256]{2,1,0:T(8,128)(2,1)} %collective-permute-done.4, s32[]{:T(128)S(6)} %select_n.151), kind=kLoop, calls=%fused_computation.149 | loop fusion | bytes 3145732 | tf_op jit(solution)/shard_map/dynamic_update_slice | solution.py:37
  96.0 1.3 constant_dynamic-update-slice_fusion.2
  97.2 1.3 constant_dynamic-update-slice_fusion.1
  98.5 0.7 copy-done.1
  99.2 2.1 %convolution_bitcast_fusion.8 = f32[384,256]{0,1:T(8,128)S(1)} fusion(bf16[384,2048]{1,0:T(8,128)(2,1)S(1)} %copy-done.1, bf16[3,8192,256]{2,1,0:T(8,128)(2,1)} %constant_dynamic-update-slice_fusion.1, s32[]{:T(128)S(6)} %select_n.154), kind=kOutput, calls=%fused_computation.15 | convolution fusion | flops 402653184 | bytes 3014660 | tf_op jit(solution)/shard_map/dot_general | solution.py:67
  101.4 2.5 %convolution_bitcast_fusion.7 = f32[384,256]{0,1:T(8,128)S(1)} fusion(bf16[384,2048]{1,0:T(8,128)(2,1)S(1)} %copy-done.1, bf16[3,8192,256]{2,1,0:T(8,128)(2,1)} %constant_dynamic-update-slice_fusion.1, s32[]{:T(128)S(6)} %add.250, s32[]{:T(128)S(6)} %select_n.154), kind=kOutput, calls=%fused_computation.14 | convolution fusion | flops 402653184 | bytes 3014664 | tf_op jit(solution)/shard_map/dot_general | solution.py:67
  103.9 2.0 %convolution_bitcast_fusion.6 = f32[384,256]{0,1:T(8,128)S(1)} fusion(bf16[384,2048]{1,0:T(8,128)(2,1)S(1)} %copy-done.1, bf16[3,8192,256]{2,1,0:T(8,128)(2,1)} %constant_dynamic-update-slice_fusion.1, s32[]{:T(128)S(6)} %add.251, s32[]{:T(128)S(6)} %select_n.154), kind=kOutput, calls=%fused_computation.13 | convolution fusion | flops 402653184 | bytes 3014664 | tf_op jit(solution)/shard_map/dot_general | solution.py:67
  105.9 16.7 %collective-permute-done.12 = bf16[384,2048]{1,0:T(8,128)(2,1)S(1)} collective-permute-done((bf16[384,2048]{1,0:T(8,128)(2,1)S(1)}, bf16[384,2048]{1,0:T(8,128)(2,1)S(1)}, u32[]{:S(2)}, u32[]{:S(2)}) %collective-permute-start.12) | collective-permute-done | bytes 1572896 | tf_op jit(solution)/shard_map/ppermute | solution.py:54
  122.6 2.0 %fusion.14 = f32[384,256]{0,1:T(8,128)S(1)} fusion(bf16[3,8192,256]{2,1,0:T(8,128)(2,1)} %constant_dynamic-update-slice_fusion.1, s32[]{:T(128)S(6)} %add.251, s32[]{:T(128)S(6)} %select_n.161, bf16[384,2048]{1,0:T(8,128)(2,1)S(1)} %collective-permute-done.11, bf16[384,2048]{1,0:T(8,128)(2,1)S(1)} %collective-permute-done.12), kind=kOutput, calls=%fused_computation.40 | convolution fusion | flops 403439616 | bytes 4587528 | tf_op jit(solution)/shard_map/dot_general | solution.py:67
  124.6 0.8 fusion.15
  125.4 0.8 fusion.16
  126.1 0.8 fusion.17
  126.9 0.8 fusion.18
  127.8 0.8 fusion.19
  128.6 2.2 %convolution_bitcast_fusion = f32[384,256]{0,1:T(8,128)S(1)} fusion(bf16[384,2048]{1,0:T(8,128)(2,1)} %collective-permute-done.8, bf16[3,8192,256]{2,1,0:T(8,128)(2,1)S(1)} %copy-done, s32[]{:T(128)S(6)} %add.251, s32[]{:T(128)S(6)} %select_n.158), kind=kOutput, calls=%fused_computation.7 | convolution fusion | flops 402653184 | bytes 3014664 | tf_op jit(solution)/shard_map/dot_general | solution.py:67
  130.7 2.2 %convolution_bitcast_fusion.1 = f32[384,256]{0,1:T(8,128)S(1)} fusion(bf16[384,2048]{1,0:T(8,128)(2,1)} %collective-permute-done.8, bf16[3,8192,256]{2,1,0:T(8,128)(2,1)S(1)} %copy-done, s32[]{:T(128)S(6)} %add.250, s32[]{:T(128)S(6)} %select_n.158), kind=kOutput, calls=%fused_computation.8 | convolution fusion | flops 402653184 | bytes 3014664 | tf_op jit(solution)/shard_map/dot_general | solution.py:67
  132.9 2.2 %convolution_bitcast_fusion.3 = f32[384,256]{0,1:T(8,128)S(1)} fusion(bf16[384,2048]{1,0:T(8,128)(2,1)} %collective-permute-done.7, bf16[3,8192,256]{2,1,0:T(8,128)(2,1)S(1)} %copy-done, s32[]{:T(128)S(6)} %add.251, s32[]{:T(128)S(6)} %select_n.156), kind=kOutput, calls=%fused_computation.10 | convolution fusion | flops 402653184 | bytes 3014664 | tf_op jit(solution)/shard_map/dot_general | solution.py:67
  135.1 2.2 %convolution_bitcast_fusion.4 = f32[384,256]{0,1:T(8,128)S(1)} fusion(bf16[384,2048]{1,0:T(8,128)(2,1)} %collective-permute-done.7, bf16[3,8192,256]{2,1,0:T(8,128)(2,1)S(1)} %copy-done, s32[]{:T(128)S(6)} %add.250, s32[]{:T(128)S(6)} %select_n.156), kind=kOutput, calls=%fused_computation.11 | convolution fusion | flops 402653184 | bytes 3014664 | tf_op jit(solution)/shard_map/dot_general | solution.py:67
  137.3 2.2 %convolution_bitcast_fusion.2 = f32[384,256]{0,1:T(8,128)S(1)} fusion(bf16[384,2048]{1,0:T(8,128)(2,1)} %collective-permute-done.8, bf16[3,8192,256]{2,1,0:T(8,128)(2,1)S(1)} %copy-done, s32[]{:T(128)S(6)} %select_n.158), kind=kOutput, calls=%fused_computation.9 | convolution fusion | flops 402653184 | bytes 3014660 | tf_op jit(solution)/shard_map/dot_general | solution.py:67
  139.5 2.2 %convolution_bitcast_fusion.5 = f32[384,256]{0,1:T(8,128)S(1)} fusion(bf16[384,2048]{1,0:T(8,128)(2,1)} %collective-permute-done.7, bf16[3,8192,256]{2,1,0:T(8,128)(2,1)S(1)} %copy-done, s32[]{:T(128)S(6)} %select_n.156), kind=kOutput, calls=%fused_computation.12 | convolution fusion | flops 402653184 | bytes 3014660 | tf_op jit(solution)/shard_map/dot_general | solution.py:67
  142.2 1.5 collective-permute-start.13
  144.5 0.9 slice.246
  145.8 2.9 %fusion.4 = f32[384,768]{0,1:T(8,128)S(1)} fusion(f32[390,768]{0,1:T(8,128)S(1)} %maximum_convert_fusion, f32[768]{0:T(1024)S(1)} %mul.489, f32[768]{0:T(1024)S(1)} %mul.486, f32[768]{0:T(1024)S(1)} %mul.483, f32[768]{0:T(1024)S(1)} %mul.480, f32[768]{0:T(1024)S(1)} %mul.477, f32[768]{0:T(1024)S(1)} %mul.474, f32[768]{0:T(1024)S(1)} %mul.458), kind=kLoop, calls=%fused_computation.21 | loop fusion | flops 3833856 | bytes 9458688 | tf_op jit(solution)/shard_map/add | solution.py:140
  150.0 0.9 copy.53
  150.9 3.3 %collective-permute-start.14 = (bf16[128,256]{0,1:T(8,128)(2,1)}, bf16[128,256]{0,1:T(8,128)(2,1)}, u32[]{:S(2)}, u32[]{:S(2)}) collective-permute-start(bf16[128,256]{0,1:T(8,128)(2,1)} %slice.241), channel_id=1, source_target_pairs={{0,4},{4,8},{8,12},{12,16},{16,20},{20,24},{24,28},{1,5},{5,9},{9,... | collective-permute-start | bytes 196616 | tf_op jit(solution)/shard_map/ppermute | solution.py:15
  154.2 1.7 multiply_reduce_fusion.1
  155.8 1.2 multiply_reduce_fusion.4
  157.1 13.4 %all_gather.4 = bf16[8,32,256]{2,1,0:T(8,128)(2,1)S(1)} all-gather(bf16[1,32,256]{2,1,0:T(8,128)(2,1)S(1)} %pad_maximum_fusion), channel_id=1, replica_groups=mesh['seq'=8,'ch'=4] {'seq'}, dimensions={0}, use_global_device_ids=true | all-gather | bytes 147456 | tf_op jit(solution)/shard_map/all_gather | solution.py:152
  171.1 1.3 multiply_reduce_fusion
  172.4 1.2 copy.55
  173.6 1.4 fusion.93
  175.0 1.9 %fusion.34 = f32[256,384]{1,0:T(8,128)S(1)} fusion(f32[384,384]{1,0:T(8,128)S(1)} %copy-done.15, f32[768,256]{0,1:T(8,128)S(1)} %fusion.93, f32[768,256]{0,1:T(8,128)S(1)} %copy-done.9, f32[768,256]{0,1:T(8,128)S(1)} %fusion.92, f32[768,256]{0,1:T(8,128)} %fusion), kind=kOutput, calls=%fused_computation.81 | convolution fusion | flops 227180544 | bytes 4128768 | tf_op jit(solution)/shard_map/dot_general | solution.py:97
  177.0 0.7 fusion.13
  177.7 0.8 copy.56
  (89 shorter events, 6.5 us)
Async XLA Ops:
  0.0 37.5 %collective-permute-start = (bf16[3,1024,256]{2,1,0:T(8,128)(2,1)}, bf16[3,1024,256]{2,1,0:T(8,128)(2,1)S(1)}, u32[]{:S(2)}, u32[]{:S(2)}) collective-permute-start(bf16[3,1024,256]{2,1,0:T(8,128)(2,1)} %param.13), channel_id=1, source_target_pairs={{0,8},{4,12},{8,0},{12,4},{16,24},{20,28},{24,16},{28,20},{1,9},{5... | collective-permute-start | bytes 4718600 | tf_op jit(solution)/shard_map/ppermute | solution.py:20
  2.9 36.1 %collective-permute-start.1 = (bf16[3,1024,256]{2,1,0:T(8,128)(2,1)}, bf16[3,1024,256]{2,1,0:T(8,128)(2,1)S(1)}, u32[]{:S(2)}, u32[]{:S(2)}) collective-permute-start(bf16[3,1024,256]{2,1,0:T(8,128)(2,1)} %param.13), channel_id=1, source_target_pairs={{0,16},{4,20},{8,24},{12,28},{16,0},{20,4},{24,8},{28,12},{1,17},{... | collective-permute-start | bytes 4718600 | tf_op jit(solution)/shard_map/ppermute | solution.py:20
  4.5 54.5 %collective-permute-start.3 = (bf16[3,1024,256]{2,1,0:T(8,128)(2,1)}, bf16[3,1024,256]{2,1,0:T(8,128)(2,1)}, u32[]{:S(2)}, u32[]{:S(2)}) collective-permute-start(bf16[3,1024,256]{2,1,0:T(8,128)(2,1)} %param.13), channel_id=1, source_target_pairs={{0,4},{4,0},{8,12},{12,8},{16,20},{20,16},{24,28},{28,24},{1,5},{5... | collective-permute-start | bytes 4718600 | tf_op jit(solution)/shard_map/ppermute | solution.py:20
  4.5 41.6 %collective-permute-start.7 = (bf16[384,2048]{1,0:T(8,128)(2,1)}, bf16[384,2048]{1,0:T(8,128)(2,1)}, u32[]{:S(2)}, u32[]{:S(2)}) collective-permute-start(bf16[384,2048]{1,0:T(8,128)(2,1)} %param.12), channel_id=1, source_target_pairs={{0,1},{1,2},{2,3},{4,5},{5,6},{6,7},{8,9},{9,10},{10,11},{12,13},{... | collective-permute-start | bytes 4718600 | tf_op jit(solution)/shard_map/ppermute | solution.py:54
  9.1 38.7 %collective-permute-start.8 = (bf16[384,2048]{1,0:T(8,128)(2,1)}, bf16[384,2048]{1,0:T(8,128)(2,1)}, u32[]{:S(2)}, u32[]{:S(2)}) collective-permute-start(bf16[384,2048]{1,0:T(8,128)(2,1)} %param.12), channel_id=1, source_target_pairs={{1,0},{2,1},{3,2},{5,4},{6,5},{7,6},{9,8},{10,9},{11,10},{13,12},{... | collective-permute-start | bytes 4718600 | tf_op jit(solution)/shard_map/ppermute | solution.py:54
  10.5 6.7 %copy-start.21 = (s32[16]{0:T(128)}, s32[16]{0:T(128)S(1)}, u32[]{:S(2)}) copy-start(s32[16]{0:T(128)S(1)} %multiply_add_fusion) | copy-start | bytes 196
  10.5 5.4 %copy-start.12 = (bf16[3,1024,256]{2,1,0:T(8,128)(2,1)S(1)}, bf16[3,1024,256]{2,1,0:T(8,128)(2,1)}, u32[]{:S(2)}) copy-start(bf16[3,1024,256]{2,1,0:T(8,128)(2,1)} %param.13) | copy-start | bytes 4718596
  37.5 1.7 copy-start.2
  38.9 4.3 %copy-start.19 = (f32[16,256]{1,0:T(8,128)S(1)}, f32[16,256]{1,0:T(8,128)}, u32[]{:S(2)}) copy-start(f32[16,256]{1,0:T(8,128)} %param.17) | copy-start | bytes 49156
  38.9 4.3 %copy-start.20 = (f32[16,256]{1,0:T(8,128)S(1)}, f32[16,256]{1,0:T(8,128)}, u32[]{:S(2)}) copy-start(f32[16,256]{1,0:T(8,128)} %param.16) | copy-start | bytes 49156
  39.2 2.1 %copy-start.13 = (bf16[3,1024,256]{2,1,0:T(8,128)(2,1)}, bf16[3,1024,256]{2,1,0:T(8,128)(2,1)S(1)}, u32[]{:S(2)}) copy-start(bf16[3,1024,256]{2,1,0:T(8,128)(2,1)S(1)} %collective-permute-done.1) | copy-start | bytes 4718596
  41.3 20.7 %collective-permute-start.2 = (bf16[3,1024,256]{2,1,0:T(8,128)(2,1)}, bf16[3,1024,256]{2,1,0:T(8,128)(2,1)}, u32[]{:S(2)}, u32[]{:S(2)}) collective-permute-start(bf16[3,1024,256]{2,1,0:T(8,128)(2,1)} %get-tuple-element.28), channel_id=1, source_target_pairs={{0,16},{4,12},{8,24},{12,4},{16,0},{20,28},{24,8},{28,20},{1,17},{... | collective-permute-start | bytes 4718600 | tf_op jit(solution)/shard_map/ppermute | solution.py:31
  44.2 0.9 copy-start.6
  45.9 13.5 %copy-start.17 = (f32[7,3,256]{2,0,1:T(8,128)S(1)}, f32[7,3,256]{2,0,1:T(8,128)}, u32[]{:S(2)}) copy-start(f32[7,3,256]{2,0,1:T(8,128)} %param.14) | copy-start | bytes 64516
  45.9 16.9 %copy-start.16 = (f32[128,256]{1,0:T(8,128)S(1)}, f32[128,256]{1,0:T(8,128)}, u32[]{:S(2)}) copy-start(f32[128,256]{1,0:T(8,128)} %param.15) | copy-start | bytes 393220
  46.1 22.9 %collective-permute-start.9 = (bf16[384,2048]{1,0:T(8,128)(2,1)}, bf16[384,2048]{1,0:T(8,128)(2,1)S(1)}, u32[]{:S(2)}, u32[]{:S(2)}) collective-permute-start(bf16[384,2048]{1,0:T(8,128)(2,1)} %collective-permute-done.7), channel_id=1, source_target_pairs={{1,2},{2,3},{5,6},{6,7},{9,10},{10,11},{13,14},{14,15},{17,18},{18... | collective-permute-start | bytes 4718600 | tf_op jit(solution)/shard_map/ppermute | solution.py:54
  47.9 38.6 %collective-permute-start.10 = (bf16[384,2048]{1,0:T(8,128)(2,1)}, bf16[384,2048]{1,0:T(8,128)(2,1)S(1)}, u32[]{:S(2)}, u32[]{:S(2)}) collective-permute-start(bf16[384,2048]{1,0:T(8,128)(2,1)} %collective-permute-done.8), channel_id=1, source_target_pairs={{1,0},{2,1},{5,4},{6,5},{9,8},{10,9},{13,12},{14,13},{17,16},{18,1... | collective-permute-start | bytes 4718600 | tf_op jit(solution)/shard_map/ppermute | solution.py:54
  52.6 40.7 %collective-permute-start.4 = (bf16[3,1024,256]{2,1,0:T(8,128)(2,1)}, bf16[3,1024,256]{2,1,0:T(8,128)(2,1)}, u32[]{:S(2)}, u32[]{:S(2)}) collective-permute-start(bf16[3,1024,256]{2,1,0:T(8,128)(2,1)} %copy-done.2), channel_id=1, source_target_pairs={{0,4},{4,0},{8,12},{12,8},{16,20},{20,16},{24,28},{28,24},{1,5},{5... | collective-permute-start | bytes 4718600 | tf_op jit(solution)/shard_map/ppermute | solution.py:20
  58.4 8.5 %copy-start.4 = (f32[768,384]{1,0:T(8,128)S(1)}, f32[768,384]{1,0:T(8,128)}, u32[]{:S(2)}) copy-start(f32[768,384]{1,0:T(8,128)} %constant.163.clone) | copy-start | bytes 3538948
  58.9 37.0 %collective-permute-start.5 = (bf16[3,1024,256]{2,1,0:T(8,128)(2,1)}, bf16[3,1024,256]{2,1,0:T(8,128)(2,1)S(1)}, u32[]{:S(2)}, u32[]{:S(2)}) collective-permute-start(bf16[3,1024,256]{2,1,0:T(8,128)(2,1)} %copy-done.13), channel_id=1, source_target_pairs={{0,4},{4,0},{8,12},{12,8},{16,20},{20,16},{24,28},{28,24},{1,5},{5... | collective-permute-start | bytes 4718600 | tf_op jit(solution)/shard_map/ppermute | solution.py:20
  62.1 35.2 %collective-permute-start.6 = (bf16[3,1024,256]{2,1,0:T(8,128)(2,1)}, bf16[3,1024,256]{2,1,0:T(8,128)(2,1)S(1)}, u32[]{:S(2)}, u32[]{:S(2)}) collective-permute-start(bf16[3,1024,256]{2,1,0:T(8,128)(2,1)} %collective-permute-done.2), channel_id=1, source_target_pairs={{0,4},{4,0},{8,12},{12,8},{16,20},{20,16},{24,28},{28,24},{1,5},{5... | collective-permute-start | bytes 4718600 | tf_op jit(solution)/shard_map/ppermute | solution.py:20
  64.4 2.5 %copy-start.11 = (f32[384,256]{1,0:T(8,128)S(1)}, f32[384,256]{1,0:T(8,128)}, u32[]{:S(2)}) copy-start(f32[384,256]{1,0:T(8,128)} %constant_dynamic-update-slice_fusion) | copy-start | bytes 1179652
  68.9 37.0 %collective-permute-start.11 = (bf16[384,2048]{1,0:T(8,128)(2,1)S(1)}, bf16[384,2048]{1,0:T(8,128)(2,1)S(1)}, u32[]{:S(2)}, u32[]{:S(2)}) collective-permute-start(bf16[384,2048]{1,0:T(8,128)(2,1)S(1)} %collective-permute-done.9), channel_id=1, source_target_pairs={{2,3},{6,7},{10,11},{14,15},{18,19},{22,23},{26,27},{30,31}} | collective-permute-start | bytes 4718600 | tf_op jit(solution)/shard_map/ppermute | solution.py:54
  86.5 36.1 %collective-permute-start.12 = (bf16[384,2048]{1,0:T(8,128)(2,1)S(1)}, bf16[384,2048]{1,0:T(8,128)(2,1)S(1)}, u32[]{:S(2)}, u32[]{:S(2)}) collective-permute-start(bf16[384,2048]{1,0:T(8,128)(2,1)S(1)} %collective-permute-done.10), channel_id=1, source_target_pairs={{1,0},{5,4},{9,8},{13,12},{17,16},{21,20},{25,24},{29,28}} | collective-permute-start | bytes 4718600 | tf_op jit(solution)/shard_map/ppermute | solution.py:54
  97.2 2.0 %copy-start.1 = (bf16[384,2048]{1,0:T(8,128)(2,1)S(1)}, bf16[384,2048]{1,0:T(8,128)(2,1)}, u32[]{:S(2)}) copy-start(bf16[384,2048]{1,0:T(8,128)(2,1)} %param.12) | copy-start | bytes 4718596
  99.2 25.4 %copy-start = (bf16[3,8192,256]{2,1,0:T(8,128)(2,1)S(1)}, bf16[3,8192,256]{2,1,0:T(8,128)(2,1)}, u32[]{:S(2)}) copy-start(bf16[3,8192,256]{2,1,0:T(8,128)(2,1)} %constant_dynamic-update-slice_fusion.1) | copy-start | bytes 37748740
  141.7 2.8 %copy-start.18 = (f32[3,256]{1,0:T(4,128)S(1)}, f32[3,256]{1,0:T(4,128)}, u32[]{:S(2)}) copy-start(f32[3,256]{1,0:T(4,128)} %get-tuple-element.21) | copy-start | bytes 9220
  141.7 2.8 %copy-start.8 = (f32[33,16,256]{2,1,0:T(8,128)S(1)}, f32[33,16,256]{2,1,0:T(8,128)}, u32[]{:S(2)}) copy-start(f32[33,16,256]{2,1,0:T(8,128)} %get-tuple-element.31) | copy-start | bytes 1622020
  142.2 3.2 %collective-permute-start.13 = (bf16[6,768]{0,1:T(8,128)(2,1)S(1)}, bf16[6,768]{0,1:T(8,128)(2,1)S(1)}, u32[]{:S(2)}, u32[]{:S(2)}) collective-permute-start(bf16[6,768]{0,1:T(8,128)(2,1)S(1)} %slice.223), channel_id=1, source_target_pairs={{0,4},{4,8},{8,12},{12,16},{16,20},{20,24},{24,28},{1,5},{5,9},{9,... | collective-permute-start | bytes 27656 | tf_op jit(solution)/shard_map/ppermute | solution.py:15
  145.8 3.6 %copy-start.5 = (f32[768,384]{1,0:T(8,128)S(1)}, f32[768,384]{1,0:T(8,128)}, u32[]{:S(2)}) copy-start(f32[768,384]{1,0:T(8,128)} %constant.163.clone) | copy-start | bytes 3538948
  149.3 6.5 %copy-start.3 = (f32[32,16,256]{2,1,0:T(8,128)S(1)}, f32[32,16,256]{2,1,0:T(8,128)}, u32[]{:S(2)}) copy-start(f32[32,16,256]{2,1,0:T(8,128)} %slice.232) | copy-start | bytes 1572868
  150.9 22.7 %collective-permute-start.14 = (bf16[128,256]{0,1:T(8,128)(2,1)}, bf16[128,256]{0,1:T(8,128)(2,1)}, u32[]{:S(2)}, u32[]{:S(2)}) collective-permute-start(bf16[128,256]{0,1:T(8,128)(2,1)} %slice.241), channel_id=1, source_target_pairs={{0,4},{4,8},{8,12},{12,16},{16,20},{20,24},{24,28},{1,5},{5,9},{9,... | collective-permute-start | bytes 196616 | tf_op jit(solution)/shard_map/ppermute | solution.py:15
  154.2 16.3 %copy-start.22 = (pred[8]{0:T(512)(128)(4,1)S(1)}, pred[8]{0:T(512)(128)(4,1)}, u32[]{:S(2)}) copy-start(pred[8]{0:T(512)(128)(4,1)} %fusion.84) | copy-start | bytes 28
  154.2 16.5 %copy-start.7 = (f32[33,16,256]{2,1,0:T(8,128)S(1)}, f32[33,16,256]{2,1,0:T(8,128)}, u32[]{:S(2)}) copy-start(f32[33,16,256]{2,1,0:T(8,128)} %copy-done.6) | copy-start | bytes 1622020
  171.1 3.9 %copy-start.9 = (f32[768,256]{0,1:T(8,128)S(1)}, f32[768,256]{0,1:T(8,128)}, u32[]{:S(2)}) copy-start(f32[768,256]{0,1:T(8,128)} %convolution_multiply_fusion) | copy-start | bytes 2359300
  173.5 1.5 copy-start.15
  175.0 1.9 %copy-start.10 = (f32[768,256]{0,1:T(8,128)S(1)}, f32[768,256]{0,1:T(8,128)}, u32[]{:S(2)}) copy-start(f32[768,256]{0,1:T(8,128)} %fusion) | copy-start | bytes 2359300
  175.0 1.9 %copy-start.14 = (f32[384,384]{1,0:T(8,128)S(1)}, f32[384,384]{1,0:T(8,128)}, u32[]{:S(2)}) copy-start(f32[384,384]{1,0:T(8,128)} %constant.168) | copy-start | bytes 1769476

commit v3 on v2

--- a/solution.py
+++ b/solution.py
@@ -4,6 +4,8 @@
 import jax.numpy as jnp
 import numpy as np
 from jax import lax
+from jax.experimental import pallas as pl
+from jax.experimental.pallas import tpu as pltpu
 from jax.sharding import PartitionSpec as P
 
 TAPS = 128
@@ -71,7 +73,55 @@
     total = add_rows(tokens, me)
     total += add_rows(up_1, (me + 3) % 4) + add_rows(down_1, (me + 1) % 4)
     total += add_rows(up_2 + down_2, (me + 2) % 4)
+    total, up_3, down_3 = lax.optimization_barrier((total, up_3, down_3))
     return total + add_rows(up_3 + down_3, 3 - me)
+
+
+def exchange_kernel(count, own_ref, tail_ref, states_ref, behind_ref, send_sems, recv_sems):
+    me = lax.axis_index("seq")
+
+    def other(offset):
+        return {"seq": lax.rem(me + offset, count)}
+
+    barrier = pltpu.get_barrier_semaphore()
+    for offset in range(1, count):
+        pl.semaphore_signal(
+            barrier, inc=1, device_id=other(offset), device_id_type=pl.DeviceIdType.MESH
+        )
+    pl.semaphore_wait(barrier, count - 1)
+
+    def copy(source, target, slot, offset):
+        return pltpu.make_async_remote_copy(
+            src_ref=source,
+            dst_ref=target,
+            send_sem=send_sems.at[slot],
+            recv_sem=recv_sems.at[slot],
+            device_id=other(offset),
+            device_id_type=pl.DeviceIdType.MESH,
+        )
+
+    copies = [copy(tail_ref, behind_ref, 0, 1)]
+    copies += [copy(own_ref, states_ref.at[me], k, k) for k in range(1, count)]
+    for each in copies:
+        each.start()
+    states_ref[me] = own_ref[...]
+    for each in copies:
+        each.wait()
+
+
+def exchange(own, tail):
+    count = lax.axis_size("seq")
+    return pl.pallas_call(
+        lambda *refs: exchange_kernel(count, *refs),
+        out_shape=(
+            jax.ShapeDtypeStruct((count,) + own.shape, own.dtype),
+            jax.ShapeDtypeStruct(tail.shape, tail.dtype),
+        ),
+        in_specs=[pl.BlockSpec(memory_space=pltpu.VMEM)] * 2,
+        out_specs=[pl.BlockSpec(memory_space=pltpu.VMEM)] * 2,
+        scratch_shapes=[pltpu.SemaphoreType.DMA((count,)), pltpu.SemaphoreType.DMA((count,))],
+        compiler_params=pltpu.CompilerParams(collective_id=0, has_side_effects=True),
+    )(own, tail)
 
 
 def phase_angle(steps, mode_count):
@@ -142,14 +192,15 @@
     )
     product = (filtered[:, width : 2 * width] * filtered[:, 2 * width :]).astype(jnp.bfloat16)
 
-    tail = from_behind(product[rows - TAPS :], "seq").astype(jnp.float32)
     product_f = product.astype(jnp.float32)
     by_lap = product_f.reshape(laps, half, width)
     folded = jnp.sum(back_far[:, None] * by_lap[:, :, None, :], axis=0)
     own = jnp.concatenate(
         [jnp.sum(back_re * folded, axis=0), jnp.sum(back_im * folded, axis=0)], axis=0
     ).astype(jnp.bfloat16)
-    states = lax.all_gather(own, "seq").astype(jnp.float32)
+    states, tail = exchange(own, product[rows - TAPS :])
+    states = states.astype(jnp.float32)
+    tail = jnp.where(place > 0, tail.astype(jnp.float32), 0.0)
 
     seen = times(cos_sin, product_f)
     seen_re, seen_im = seen[:rows], seen[rows:]

time: 179 us -> 152 us (0.85)
  blocking collectives: 13.4 us -> 0 us
  Pallas kernels: 0 us -> 10.4 us
  waiting for transfers between devices: 56.8 us -> 47.9 us
  matrix products: 34.9 us -> 27.7 us
  local copies, waits for them, and re-layouts: 32.6 us -> 28.4 us
  starting transfers between devices: 21.8 us -> 19.6 us
  other arithmetic: 18.4 us -> 16.3 us
    all_gather x1 -> x0, blocking collectives: 13.4 us -> none  [on_device(): states = lax.all_gather(own, 'seq').astype(jnp.float32)]
    ppermute x6, waiting for transfers between devices: 34.5 us -> 22.2 us  [shift(): return lax.ppermute(value, 'ch', pairs)]
    pallas_call x0 -> x1, Pallas kernels: none -> 10.4 us  [exchange(): pl.pallas_call(lambda *refs: exchange_kernel(count, *refs), out_shape=(ja...]
    dot_general x15, matrix products: 25.7 us -> 20 us  [add_rows(): jnp.dot(value, portion[j], preferred_element_type=jnp.float32)]
    ppermute x2 -> x1, starting transfers between devices: 4.84 us -> 1.51 us  [from_behind(): lax.ppermute(value, axis, [(source, source + 1) for source in range(count...]
    ppermute x1, waiting for transfers between devices: 2 us -> 4.85 us  [gather_weights(): lax.ppermute(onward, 'seq', [(s, s ^ (4 if s % 2 == 0 else 2)) for s in r...]
    add x1, other arithmetic: 2.87 us -> 0.96 us  [on_device(): sum((short_taps[i][None] * extended[SHORT - 1 - i:SHORT - 1 - i + rows] f...]
    select_n x1, other arithmetic: 2.11 us -> 4.02 us  [gather_weights(): onward = jnp.where(me % 2 == 0, over_x, over_y)]
  transfers between devices with their start and end apart: 15 -> 14, of which waited for: 6 -> 5; matrix products, arithmetic and copies ran while one was open for 30% -> 40% of each run, Pallas kernels for 0% -> 0%
where the time goes in v3:
time: 152 us; the launch traced here: 151 us
  waiting for transfers between devices  47.9 us (32%)
  local copies, waits for them, and re-layouts  28.4 us (19%)
  matrix products  27.7 us (18%)
  starting transfers between devices  19.6 us (13%)
  other arithmetic  16.3 us (11%)
  Pallas kernels  10.4 us (7%)
    ppermute x6, waiting for transfers between devices, shift(): return lax.ppermute(value, 'ch', pairs)  22.2 us
    ppermute x6, waiting for transfers between devices, flip(): return lax.ppermute(value, 'seq', [(s, s ^ mask) for s in range(count)])  20.5 us
    dot_general x15, matrix products, add_rows(): jnp.dot(value, portion[j], preferred_element_type=jnp.float32)  20 us
    dynamic_update_slice x7, local copies, waits for them, and re-layouts, gather_weights(): whole = lax.dynamic_update_slice(whole, piece, (0, (me ^ mask) * depth, 0))  14.6 us
    ppermute x6, starting transfers between devices, shift(): return lax.ppermute(value, 'ch', pairs)  11.4 us
    pallas_call x1, Pallas kernels, exchange(): pl.pallas_call(lambda *refs: exchange_kernel(count, *refs), out_shape=(ja...  10.4 us
    dot_general x6, matrix products, times(): jnp.dot(jnp.asarray(matrix), value, precision=lax.Precision.HIGH, preferr...  7.7 us
    broadcast_in_dim x1, local copies, waits for them, and re-layouts, gather_weights(): whole = jnp.zeros((3, count * depth, weight.shape[2]), weight.dtype)  5.34 us
  transfers between devices with their start and end apart: 14, of which 5 were waited for; matrix products, arithmetic and copies ran while one was open for 40% of the time, Pallas kernels for 0%

profile of v3, /device:TPU:0, one launch (start us, length us, event | category | flops | bytes accessed | tf_op | source)
XLA Modules:
  0.0 151.1 jit_solution(5786777560233167161)
XLA Ops:
  0.0 2.9 %collective-permute-start = (bf16[3,1024,256]{2,1,0:T(8,128)(2,1)}, bf16[3,1024,256]{2,1,0:T(8,128)(2,1)}, u32[]{:S(2)}, u32[]{:S(2)}) collective-permute-start(bf16[3,1024,256]{2,1,0:T(8,128)(2,1)} %param.13), channel_id=1, source_target_pairs={{0,8},{4,12},{8,0},{12,4},{16,24},{20,28},{24,16},{28,20},{1,9},{5... | collective-permute-start | bytes 4718600 | tf_op jit(solution)/shard_map/ppermute | solution.py:22
  2.9 1.5 %collective-permute-start.1 = (bf16[3,1024,256]{2,1,0:T(8,128)(2,1)}, bf16[3,1024,256]{2,1,0:T(8,128)(2,1)}, u32[]{:S(2)}, u32[]{:S(2)}) collective-permute-start(bf16[3,1024,256]{2,1,0:T(8,128)(2,1)} %param.13), channel_id=1, source_target_pairs={{0,16},{4,20},{8,24},{12,28},{16,0},{20,4},{24,8},{28,12},{1,17},{... | collective-permute-start | bytes 4718600 | tf_op jit(solution)/shard_map/ppermute | solution.py:22
  4.5 1.3 collective-permute-start.8
  5.8 4.7 %collective-permute-start.7 = (bf16[384,2048]{1,0:T(8,128)(2,1)}, bf16[384,2048]{1,0:T(8,128)(2,1)S(1)}, u32[]{:S(2)}, u32[]{:S(2)}) collective-permute-start(bf16[384,2048]{1,0:T(8,128)(2,1)} %param.12), channel_id=1, source_target_pairs={{0,1},{1,2},{2,3},{4,5},{5,6},{6,7},{8,9},{9,10},{10,11},{12,13},{... | collective-permute-start | bytes 4718600 | tf_op jit(solution)/shard_map/ppermute | solution.py:56
  10.5 5.3 %broadcast_in_dim.25 = bf16[3,8192,256]{2,1,0:T(8,128)(2,1)} broadcast(bf16[]{:T(256)} %constant.137.clone.1), dimensions={} | broadcast | bytes 12582914 | tf_op jit(solution)/shard_map/broadcast_in_dim | solution.py:37
  15.8 1.3 constant_dynamic-update-slice_fusion.8
  17.1 20.5 %collective-permute-done = bf16[3,1024,256]{2,1,0:T(8,128)(2,1)} collective-permute-done((bf16[3,1024,256]{2,1,0:T(8,128)(2,1)}, bf16[3,1024,256]{2,1,0:T(8,128)(2,1)}, u32[]{:S(2)}, u32[]{:S(2)}) %collective-permute-start) | collective-permute-done | bytes 1572896 | tf_op jit(solution)/shard_map/ppermute | solution.py:22
  37.6 2.7 %constant_dynamic-update-slice_fusion.7 = bf16[3,8192,256]{2,1,0:T(8,128)(2,1)} fusion(bf16[3,8192,256]{2,1,0:T(8,128)(2,1)} %constant_dynamic-update-slice_fusion.8, bf16[3,1024,256]{2,1,0:T(8,128)(2,1)} %collective-permute-done, s32[]{:T(128)S(6)} %select_n.152), kind=kLoop, calls=%fused_computation.156 | loop fusion | bytes 3145732 | tf_op jit(solution)/shard_map/dynamic_update_slice | solution.py:39
  40.4 4.0 %broadcast_select_fusion = (bf16[3,1024,256]{2,1,0:T(8,128)(2,1)}, bf16[3,8192,256]{2,1,0:T(8,128)(2,1)}) fusion(bf16[3,1024,256]{2,1,0:T(8,128)(2,1)} %collective-permute-done, bf16[3,1024,256]{2,1,0:T(8,128)(2,1)} %collective-permute-done.1, pred[]{:T(512)S(6)} %eq.25, bf16[3,8192,256]{2,1,0:T(8,128)(2,1)} %constant_dynamic-update-slice_fusion.7, ...), kind=kLoop, calls=%fused_computation.3 | loop fusion | flops 786432 | bytes 6291461 | tf_op jit(solution)/shard_map/jit(_where)/select_n | solution.py:32
  44.4 1.8 %collective-permute-start.2 = (bf16[3,1024,256]{2,1,0:T(8,128)(2,1)}, bf16[3,1024,256]{2,1,0:T(8,128)(2,1)}, u32[]{:S(2)}, u32[]{:S(2)}) collective-permute-start(bf16[3,1024,256]{2,1,0:T(8,128)(2,1)} %get-tuple-element.38), channel_id=1, source_target_pairs={{0,16},{4,12},{8,24},{12,4},{16,0},{20,28},{24,8},{28,20},{1,17},{... | collective-permute-start | bytes 4718600 | tf_op jit(solution)/shard_map/ppermute | solution.py:33
  46.4 1.0 fusion.20
  47.7 1.4 collective-permute-start.10
  49.2 1.8 %collective-permute-start.9 = (bf16[384,2048]{1,0:T(8,128)(2,1)S(1)}, bf16[384,2048]{1,0:T(8,128)(2,1)}, u32[]{:S(2)}, u32[]{:S(2)}) collective-permute-start(bf16[384,2048]{1,0:T(8,128)(2,1)S(1)} %collective-permute-done.7), channel_id=1, source_target_pairs={{1,2},{2,3},{5,6},{6,7},{9,10},{10,11},{13,14},{14,15},{17,18},{18... | collective-permute-start | bytes 4718600 | tf_op jit(solution)/shard_map/ppermute | solution.py:56
  51.0 2.4 %multiply_reduce_fusion.2 = f32[32,12,256]{2,1,0:T(8,128)} fusion(f32[16,256]{1,0:T(8,128)S(1)} %get-tuple-element.42, f32[12,16,256]{2,1,0:T(8,128)S(1)} %exponential_multiply_fusion, f32[32,16,256]{2,1,0:T(8,128)S(1)} %slice.232), kind=kLoop, calls=%fused_computation.2 | loop fusion | flops 4620288 | bytes 1130496 | tf_op jit(solution)/shard_map/reduce_sum | solution.py:169
  53.4 2.0 %copy.95 = f32[12,32,256]{2,1,0:T(8,128)} copy(f32[12,32,256]{2,0,1:T(8,128)} %bitcast.100) | data formatting | bytes 786432 | tf_op jit(solution)/shard_map/transpose | solution.py:170
  55.5 1.6 %slice.233 = f32[4,32,256]{2,0,1:T(4,128)} slice(f32[12,32,256]{2,0,1:T(8,128)} %bitcast.101), slice={[0:4], [0:32], [0:256]} | slice | bytes 262144 | tf_op jit(solution)/shard_map/slice.24
  57.1 1.6 %copy.96 = f32[4,32,256]{2,1,0:T(8,128)} copy(f32[4,32,256]{2,0,1:T(4,128)} %slice.233) | data formatting | bytes 262144 | tf_op jit(solution)/shard_map/slice.24
  58.7 0.6 and_select_fusion
  59.3 0.3 collective-permute-start.5
  59.6 0.7 slice_reduce_fusion.6
  60.3 4.9 %collective-permute-done.2 = bf16[3,1024,256]{2,1,0:T(8,128)(2,1)} collective-permute-done((bf16[3,1024,256]{2,1,0:T(8,128)(2,1)}, bf16[3,1024,256]{2,1,0:T(8,128)(2,1)}, u32[]{:S(2)}, u32[]{:S(2)}) %collective-permute-start.2) | collective-permute-done | bytes 1572896 | tf_op jit(solution)/shard_map/ppermute | solution.py:33
  65.1 0.7 fusion.86
  65.8 1.6 %constant_dynamic-update-slice_fusion = f32[384,256]{1,0:T(8,128)} fusion(f32[384,256]{1,0:T(8,128)} %bitcast.103, f32[128,256]{1,0:T(8,128)S(1)} %copy-done.16, f32[4,32,256]{2,1,0:T(8,128)} %copy.96), kind=kLoop, calls=%fused_computation.144 | loop fusion | flops 32768 | bytes 393216 | tf_op jit(solution)/shard_map/scatter-add | solution.py:171
  67.4 2.4 %convolution_multiply_fusion = f32[768,256]{0,1:T(8,128)} fusion(f32[768,128]{1,0:T(8,128)} %constant.164.clone, f32[128,256]{1,0:T(8,128)S(1)} %copy-done.16), kind=kOutput, calls=%fused_computation.4 | convolution fusion | flops 151191552 | bytes 1310720 | tf_op jit(solution)/shard_map/dot_general | solution.py:147
  69.9 2.1 %fusion = f32[768,256]{0,1:T(8,128)} fusion(f32[384,256]{1,0:T(8,128)S(1)} %copy-done.12, f32[768,384]{1,0:T(8,128)S(1)} %copy-done.4), kind=kOutput, calls=%fused_computation.6 | convolution fusion | flops 453181440 | bytes 2359296 | tf_op jit(solution)/shard_map/dot_general | solution.py:147
  72.0 2.7 %constant_dynamic-update-slice_fusion.5 = bf16[3,8192,256]{2,1,0:T(8,128)(2,1)} fusion(bf16[3,8192,256]{2,1,0:T(8,128)(2,1)} %get-tuple-element.39, bf16[3,1024,256]{2,1,0:T(8,128)(2,1)} %collective-permute-done.2, s32[]{:T(128)S(6)} %select_n.157), kind=kLoop, calls=%fused_computation.154 | loop fusion | bytes 3145732 | tf_op jit(solution)/shard_map/dynamic_update_slice | solution.py:39
  74.7 0.8 collective-permute-start.11
  75.4 11.1 %collective-permute-done.10 = bf16[384,2048]{1,0:T(8,128)(2,1)} collective-permute-done((bf16[384,2048]{1,0:T(8,128)(2,1)S(1)}, bf16[384,2048]{1,0:T(8,128)(2,1)}, u32[]{:S(2)}, u32[]{:S(2)}) %collective-permute-start.10) | collective-permute-done | bytes 1572896 | tf_op jit(solution)/shard_map/ppermute | solution.py:56
  86.5 1.5 collective-permute-start.12
  88.0 2.7 %constant_dynamic-update-slice_fusion.4 = bf16[3,8192,256]{2,1,0:T(8,128)(2,1)} fusion(bf16[3,8192,256]{2,1,0:T(8,128)(2,1)} %constant_dynamic-update-slice_fusion.5, bf16[3,1024,256]{2,1,0:T(8,128)(2,1)} %collective-permute-done.3, s32[]{:T(128)S(6)} %select_n.158), kind=kLoop, calls=%fused_computation.153 | loop fusion | bytes 3145732 | tf_op jit(solution)/shard_map/dynamic_update_slice | solution.py:39
  90.7 2.7 %constant_dynamic-update-slice_fusion.3 = bf16[3,8192,256]{2,1,0:T(8,128)(2,1)} fusion(bf16[3,8192,256]{2,1,0:T(8,128)(2,1)} %constant_dynamic-update-slice_fusion.4, bf16[3,1024,256]{2,1,0:T(8,128)(2,1)} %collective-permute-done.4, s32[]{:T(128)S(6)} %select_n.159), kind=kLoop, calls=%fused_computation.152 | loop fusion | bytes 3145732 | tf_op jit(solution)/shard_map/dynamic_update_slice | solution.py:39
  93.4 1.3 constant_dynamic-update-slice_fusion.2
  94.7 1.3 constant_dynamic-update-slice_fusion.1
  95.9 0.7 copy-done.1
  96.6 2.0 %convolution_bitcast_fusion.8 = f32[384,256]{1,0:T(8,128)S(1)} fusion(bf16[384,2048]{1,0:T(8,128)(2,1)S(1)} %copy-done.1, bf16[3,8192,256]{2,1,0:T(8,128)(2,1)} %constant_dynamic-update-slice_fusion.1, s32[]{:T(128)S(6)} %select_n.162), kind=kOutput, calls=%fused_computation.15 | convolution fusion | flops 402653184 | bytes 3014660 | tf_op jit(solution)/shard_map/dot_general | solution.py:69
  98.6 2.3 %convolution_bitcast_fusion.7 = f32[384,256]{1,0:T(8,128)S(1)} fusion(bf16[384,2048]{1,0:T(8,128)(2,1)S(1)} %copy-done.1, bf16[3,8192,256]{2,1,0:T(8,128)(2,1)} %constant_dynamic-update-slice_fusion.1, s32[]{:T(128)S(6)} %add.250, s32[]{:T(128)S(6)} %select_n.162), kind=kOutput, calls=%fused_computation.14 | convolution fusion | flops 402653184 | bytes 3014664 | tf_op jit(solution)/shard_map/dot_general | solution.py:69
  100.9 1.8 %convolution_bitcast_fusion.6 = f32[384,256]{1,0:T(8,128)S(1)} fusion(bf16[384,2048]{1,0:T(8,128)(2,1)S(1)} %copy-done.1, bf16[3,8192,256]{2,1,0:T(8,128)(2,1)} %constant_dynamic-update-slice_fusion.1, s32[]{:T(128)S(6)} %add.251, s32[]{:T(128)S(6)} %select_n.162), kind=kOutput, calls=%fused_computation.13 | convolution fusion | flops 402653184 | bytes 3014664 | tf_op jit(solution)/shard_map/dot_general | solution.py:69
  102.7 1.8 %convolution_bitcast_fusion = f32[384,256]{1,0:T(8,128)S(1)} fusion(bf16[384,2048]{1,0:T(8,128)(2,1)S(1)} %collective-permute-done.8, bf16[3,8192,256]{2,1,0:T(8,128)(2,1)} %constant_dynamic-update-slice_fusion.1, s32[]{:T(128)S(6)} %add.251, s32[]{:T(128)S(6)} %select_n.166), kind=kOutput, calls=%fused_computation.7 | convolution fusion | flops 402653184 | bytes 3014664 | tf_op jit(solution)/shard_map/dot_general | solution.py:69
  104.6 0.6 convolution_bitcast_fusion.1
  105.1 0.6 convolution_bitcast_fusion.3
  105.7 0.6 convolution_bitcast_fusion.4
  106.3 0.6 convolution_bitcast_fusion.2
  106.9 0.6 convolution_bitcast_fusion.5
  107.5 2.5 %fusion.16 = f32[384,256]{1,0:T(8,128)S(1)} fusion(bf16[3,8192,256]{2,1,0:T(8,128)(2,1)S(1)} %copy-done, s32[]{:T(128)S(6)} %add.251, s32[]{:T(128)S(6)} %select_n.168, bf16[384,2048]{1,0:T(8,128)(2,1)} %collective-permute-done.9, bf16[384,2048]{1,0:T(8,128)(2,1)} %collective-permute-done.10), kind=kOutput, calls=%fused_computation.46 | convolution fusion | flops 403439616 | bytes 4587528 | tf_op jit(solution)/shard_map/dot_general | solution.py:69
  110.0 2.5 %fusion.17 = f32[384,256]{1,0:T(8,128)S(1)} fusion(bf16[3,8192,256]{2,1,0:T(8,128)(2,1)S(1)} %copy-done, s32[]{:T(128)S(6)} %add.250, s32[]{:T(128)S(6)} %select_n.168, bf16[384,2048]{1,0:T(8,128)(2,1)} %collective-permute-done.9, bf16[384,2048]{1,0:T(8,128)(2,1)} %collective-permute-done.10), kind=kOutput, calls=%fused_computation.48 | convolution fusion | flops 403439616 | bytes 4587528 | tf_op jit(solution)/shard_map/dot_general | solution.py:69
  112.5 2.5 %fusion.18 = f32[384,256]{1,0:T(8,128)S(1)} fusion(bf16[3,8192,256]{2,1,0:T(8,128)(2,1)S(1)} %copy-done, s32[]{:T(128)S(6)} %select_n.168, bf16[384,2048]{1,0:T(8,128)(2,1)} %collective-permute-done.9, bf16[384,2048]{1,0:T(8,128)(2,1)} %collective-permute-done.10), kind=kOutput, calls=%fused_computation.50 | convolution fusion | flops 403439616 | bytes 4587524 | tf_op jit(solution)/shard_map/dot_general | solution.py:69
  115.3 11.1 %collective-permute-done.12 = bf16[384,2048]{1,0:T(8,128)(2,1)S(1)} collective-permute-done((bf16[384,2048]{1,0:T(8,128)(2,1)}, bf16[384,2048]{1,0:T(8,128)(2,1)S(1)}, u32[]{:S(2)}, u32[]{:S(2)}) %collective-permute-start.12) | collective-permute-done | bytes 1572896 | tf_op jit(solution)/shard_map/ppermute | solution.py:56
  126.4 0.6 fusion.15
  127.0 0.6 fusion.14
  127.6 0.6 fusion.13
  128.4 1.5 %collective-permute-start.13 = (bf16[6,768]{1,0:T(8,128)(2,1)S(1)}, bf16[6,768]{1,0:T(8,128)(2,1)S(1)}, u32[]{:S(2)}, u32[]{:S(2)}) collective-permute-start(bf16[6,768]{1,0:T(8,128)(2,1)S(1)} %slice.223), channel_id=1, source_target_pairs={{0,4},{4,8},{8,12},{12,16},{16,20},{20,24},{24,28},{1,5},{5,9},{9,... | collective-permute-start | bytes 27656 | tf_op jit(solution)/shard_map/ppermute | solution.py:17
  130.5 1.2 maximum_convert_fusion
  131.7 1.0 fusion.4
  132.7 0.6 slice.242.refs_1_
  133.4 0.6 fusion.97
  134.1 0.6 multiply_reduce_fusion.1
  134.8 0.6 pad_maximum_fusion.refs_0_
  135.4 10.4 %shard_map.100 = (bf16[8,32,256]{2,1,0:T(8,128)(2,1)}, bf16[128,256]{1,0:T(8,128)(2,1)}) custom-call(bf16[32,256]{1,0:T(8,128)(2,1)} %pad_maximum_fusion.refs_0_, bf16[128,256]{1,0:T(8,128)(2,1)} %slice.242.refs_1_), custom_call_target="tpu_custom_call" | custom-call | tf_op jit(solution)/shard_map/pallas_call | solution.py:114
  145.8 0.9 convert_element_type.72
  147.4 0.5 multiply_reduce_fusion
  147.9 0.5 fusion.57
  148.7 0.6 fusion.33
  149.3 0.4 copy-done.14
  149.7 1.4 fusion.12
  (107 shorter events, 2.5 us)
Async XLA Ops:
  0.0 37.6 %collective-permute-start = (bf16[3,1024,256]{2,1,0:T(8,128)(2,1)}, bf16[3,1024,256]{2,1,0:T(8,128)(2,1)}, u32[]{:S(2)}, u32[]{:S(2)}) collective-permute-start(bf16[3,1024,256]{2,1,0:T(8,128)(2,1)} %param.13), channel_id=1, source_target_pairs={{0,8},{4,12},{8,0},{12,4},{16,24},{20,28},{24,16},{28,20},{1,9},{5... | collective-permute-start | bytes 4718600 | tf_op jit(solution)/shard_map/ppermute | solution.py:22
  2.9 37.4 %collective-permute-start.1 = (bf16[3,1024,256]{2,1,0:T(8,128)(2,1)}, bf16[3,1024,256]{2,1,0:T(8,128)(2,1)}, u32[]{:S(2)}, u32[]{:S(2)}) collective-permute-start(bf16[3,1024,256]{2,1,0:T(8,128)(2,1)} %param.13), channel_id=1, source_target_pairs={{0,16},{4,20},{8,24},{12,28},{16,0},{20,4},{24,8},{28,12},{1,17},{... | collective-permute-start | bytes 4718600 | tf_op jit(solution)/shard_map/ppermute | solution.py:22
  4.5 54.8 %collective-permute-start.3 = (bf16[3,1024,256]{2,1,0:T(8,128)(2,1)}, bf16[3,1024,256]{2,1,0:T(8,128)(2,1)}, u32[]{:S(2)}, u32[]{:S(2)}) collective-permute-start(bf16[3,1024,256]{2,1,0:T(8,128)(2,1)} %param.13), channel_id=1, source_target_pairs={{0,4},{4,0},{8,12},{12,8},{16,20},{20,16},{24,28},{28,24},{1,5},{5... | collective-permute-start | bytes 4718600 | tf_op jit(solution)/shard_map/ppermute | solution.py:22
  4.5 43.3 %collective-permute-start.8 = (bf16[384,2048]{1,0:T(8,128)(2,1)}, bf16[384,2048]{1,0:T(8,128)(2,1)S(1)}, u32[]{:S(2)}, u32[]{:S(2)}) collective-permute-start(bf16[384,2048]{1,0:T(8,128)(2,1)} %param.12), channel_id=1, source_target_pairs={{1,0},{2,1},{3,2},{5,4},{6,5},{7,6},{9,8},{10,9},{11,10},{13,12},{... | collective-permute-start | bytes 4718600 | tf_op jit(solution)/shard_map/ppermute | solution.py:56
  5.8 43.4 %collective-permute-start.7 = (bf16[384,2048]{1,0:T(8,128)(2,1)}, bf16[384,2048]{1,0:T(8,128)(2,1)S(1)}, u32[]{:S(2)}, u32[]{:S(2)}) collective-permute-start(bf16[384,2048]{1,0:T(8,128)(2,1)} %param.12), channel_id=1, source_target_pairs={{0,1},{1,2},{2,3},{4,5},{5,6},{6,7},{8,9},{9,10},{10,11},{12,13},{... | collective-permute-start | bytes 4718600 | tf_op jit(solution)/shard_map/ppermute | solution.py:56
  10.5 5.4 %copy-start.13 = (bf16[3,1024,256]{2,1,0:T(8,128)(2,1)S(1)}, bf16[3,1024,256]{2,1,0:T(8,128)(2,1)}, u32[]{:S(2)}) copy-start(bf16[3,1024,256]{2,1,0:T(8,128)(2,1)} %param.13) | copy-start | bytes 4718596
  40.4 6.0 %copy-start.31 = (f32[16,256]{1,0:T(8,128)S(1)}, f32[16,256]{1,0:T(8,128)}, u32[]{:S(2)}) copy-start(f32[16,256]{1,0:T(8,128)} %param.17) | copy-start | bytes 49156
  40.4 6.0 %copy-start.32 = (f32[16,256]{1,0:T(8,128)S(1)}, f32[16,256]{1,0:T(8,128)}, u32[]{:S(2)}) copy-start(f32[16,256]{1,0:T(8,128)} %param.16) | copy-start | bytes 49156
  44.4 20.7 %collective-permute-start.2 = (bf16[3,1024,256]{2,1,0:T(8,128)(2,1)}, bf16[3,1024,256]{2,1,0:T(8,128)(2,1)}, u32[]{:S(2)}, u32[]{:S(2)}) collective-permute-start(bf16[3,1024,256]{2,1,0:T(8,128)(2,1)} %get-tuple-element.38), channel_id=1, source_target_pairs={{0,16},{4,12},{8,24},{12,4},{16,0},{20,28},{24,8},{28,20},{1,17},{... | collective-permute-start | bytes 4718600 | tf_op jit(solution)/shard_map/ppermute | solution.py:33
  46.4 7.0 %copy-start.18 = (f32[16,256]{1,0:T(8,128)}, f32[16,256]{1,0:T(8,128)S(1)}, u32[]{:S(2)}) copy-start(f32[16,256]{1,0:T(8,128)S(1)} %get-tuple-element.42) | copy-start | bytes 49156
  47.5 1.7 %copy-start.6 = (f32[33,16,256]{2,1,0:T(8,128)}, f32[33,16,256]{2,1,0:T(8,128)S(1)}, u32[]{:S(2)}) copy-start(f32[33,16,256]{2,1,0:T(8,128)S(1)} %get-tuple-element.40) | copy-start | bytes 1622020
  47.5 3.5 %copy-start.2 = (f32[32,16,256]{2,1,0:T(8,128)}, f32[32,16,256]{2,1,0:T(8,128)S(1)}, u32[]{:S(2)}) copy-start(f32[32,16,256]{2,1,0:T(8,128)S(1)} %slice.232) | copy-start | bytes 1572868
  47.5 12.1 %copy-start.21 = (f32[7,3,256]{2,0,1:T(8,128)S(1)}, f32[7,3,256]{2,0,1:T(8,128)}, u32[]{:S(2)}) copy-start(f32[7,3,256]{2,0,1:T(8,128)} %param.14) | copy-start | bytes 64516
  47.5 18.3 %copy-start.16 = (f32[128,256]{1,0:T(8,128)S(1)}, f32[128,256]{1,0:T(8,128)}, u32[]{:S(2)}) copy-start(f32[128,256]{1,0:T(8,128)} %param.15) | copy-start | bytes 393220
  47.7 43.1 %collective-permute-start.4 = (bf16[3,1024,256]{2,1,0:T(8,128)(2,1)}, bf16[3,1024,256]{2,1,0:T(8,128)(2,1)}, u32[]{:S(2)}, u32[]{:S(2)}) collective-permute-start(bf16[3,1024,256]{2,1,0:T(8,128)(2,1)} %collective-permute-done), channel_id=1, source_target_pairs={{0,4},{4,0},{8,12},{12,8},{16,20},{20,16},{24,28},{28,24},{1,5},{5... | collective-permute-start | bytes 4718600 | tf_op jit(solution)/shard_map/ppermute | solution.py:22
  47.7 38.8 %collective-permute-start.10 = (bf16[384,2048]{1,0:T(8,128)(2,1)S(1)}, bf16[384,2048]{1,0:T(8,128)(2,1)}, u32[]{:S(2)}, u32[]{:S(2)}) collective-permute-start(bf16[384,2048]{1,0:T(8,128)(2,1)S(1)} %collective-permute-done.8), channel_id=1, source_target_pairs={{1,0},{2,1},{5,4},{6,5},{9,8},{10,9},{13,12},{14,13},{17,16},{18,1... | collective-permute-start | bytes 4718600 | tf_op jit(solution)/shard_map/ppermute | solution.py:56
  49.2 25.5 %collective-permute-start.9 = (bf16[384,2048]{1,0:T(8,128)(2,1)S(1)}, bf16[384,2048]{1,0:T(8,128)(2,1)}, u32[]{:S(2)}, u32[]{:S(2)}) collective-permute-start(bf16[384,2048]{1,0:T(8,128)(2,1)S(1)} %collective-permute-done.7), channel_id=1, source_target_pairs={{1,2},{2,3},{5,6},{6,7},{9,10},{10,11},{13,14},{14,15},{17,18},{18... | collective-permute-start | bytes 4718600 | tf_op jit(solution)/shard_map/ppermute | solution.py:56
  58.7 11.2 %copy-start.4 = (f32[768,384]{1,0:T(8,128)S(1)}, f32[768,384]{1,0:T(8,128)}, u32[]{:S(2)}) copy-start(f32[768,384]{1,0:T(8,128)} %constant.163.clone) | copy-start | bytes 3538948
  59.3 34.1 %collective-permute-start.5 = (bf16[3,1024,256]{2,1,0:T(8,128)(2,1)}, bf16[3,1024,256]{2,1,0:T(8,128)(2,1)S(1)}, u32[]{:S(2)}, u32[]{:S(2)}) collective-permute-start(bf16[3,1024,256]{2,1,0:T(8,128)(2,1)} %collective-permute-done.1), channel_id=1, source_target_pairs={{0,4},{4,0},{8,12},{12,8},{16,20},{20,16},{24,28},{28,24},{1,5},{5... | collective-permute-start | bytes 4718600 | tf_op jit(solution)/shard_map/ppermute | solution.py:22
  65.1 29.5 %collective-permute-start.6 = (bf16[3,1024,256]{2,1,0:T(8,128)(2,1)}, bf16[3,1024,256]{2,1,0:T(8,128)(2,1)S(1)}, u32[]{:S(2)}, u32[]{:S(2)}) collective-permute-start(bf16[3,1024,256]{2,1,0:T(8,128)(2,1)} %collective-permute-done.2), channel_id=1, source_target_pairs={{0,4},{4,0},{8,12},{12,8},{16,20},{20,16},{24,28},{28,24},{1,5},{5... | collective-permute-start | bytes 4718600 | tf_op jit(solution)/shard_map/ppermute | solution.py:22
  67.4 2.5 %copy-start.12 = (f32[384,256]{1,0:T(8,128)S(1)}, f32[384,256]{1,0:T(8,128)}, u32[]{:S(2)}) copy-start(f32[384,256]{1,0:T(8,128)} %constant_dynamic-update-slice_fusion) | copy-start | bytes 1179652
  74.7 40.6 %collective-permute-start.11 = (bf16[384,2048]{1,0:T(8,128)(2,1)}, bf16[384,2048]{1,0:T(8,128)(2,1)S(1)}, u32[]{:S(2)}, u32[]{:S(2)}) collective-permute-start(bf16[384,2048]{1,0:T(8,128)(2,1)} %collective-permute-done.9), channel_id=1, source_target_pairs={{2,3},{6,7},{10,11},{14,15},{18,19},{22,23},{26,27},{30,31}} | collective-permute-start | bytes 4718600 | tf_op jit(solution)/shard_map/ppermute | solution.py:56
  86.5 39.9 %collective-permute-start.12 = (bf16[384,2048]{1,0:T(8,128)(2,1)}, bf16[384,2048]{1,0:T(8,128)(2,1)S(1)}, u32[]{:S(2)}, u32[]{:S(2)}) collective-permute-start(bf16[384,2048]{1,0:T(8,128)(2,1)} %collective-permute-done.10), channel_id=1, source_target_pairs={{1,0},{5,4},{9,8},{13,12},{17,16},{21,20},{25,24},{29,28}} | collective-permute-start | bytes 4718600 | tf_op jit(solution)/shard_map/ppermute | solution.py:56
  94.7 2.0 %copy-start.1 = (bf16[384,2048]{1,0:T(8,128)(2,1)S(1)}, bf16[384,2048]{1,0:T(8,128)(2,1)}, u32[]{:S(2)}) copy-start(bf16[384,2048]{1,0:T(8,128)(2,1)} %param.12) | copy-start | bytes 4718596
  96.6 7.9 %copy-start = (bf16[3,8192,256]{2,1,0:T(8,128)(2,1)S(1)}, bf16[3,8192,256]{2,1,0:T(8,128)(2,1)}, u32[]{:S(2)}) copy-start(bf16[3,8192,256]{2,1,0:T(8,128)(2,1)} %constant_dynamic-update-slice_fusion.1) | copy-start | bytes 37748740
  128.2 1.8 %copy-start.30 = (f32[3,256]{1,0:T(4,128)S(1)}, f32[3,256]{1,0:T(4,128)}, u32[]{:S(2)}) copy-start(f32[3,256]{1,0:T(4,128)} %get-tuple-element.31) | copy-start | bytes 9220
  128.2 1.8 %copy-start.29 = (f32[3,256]{1,0:T(4,128)S(1)}, f32[3,256]{1,0:T(4,128)}, u32[]{:S(2)}) copy-start(f32[3,256]{1,0:T(4,128)} %get-tuple-element.35) | copy-start | bytes 9220
  128.2 1.8 %copy-start.28 = (f32[3,256]{1,0:T(4,128)S(1)}, f32[3,256]{1,0:T(4,128)}, u32[]{:S(2)}) copy-start(f32[3,256]{1,0:T(4,128)} %get-tuple-element.34) | copy-start | bytes 9220
  128.2 1.9 %copy-start.27 = (f32[3,256]{1,0:T(4,128)S(1)}, f32[3,256]{1,0:T(4,128)}, u32[]{:S(2)}) copy-start(f32[3,256]{1,0:T(4,128)} %get-tuple-element.33) | copy-start | bytes 9220
  128.2 1.9 %copy-start.26 = (f32[3,256]{1,0:T(4,128)S(1)}, f32[3,256]{1,0:T(4,128)}, u32[]{:S(2)}) copy-start(f32[3,256]{1,0:T(4,128)} %get-tuple-element.32) | copy-start | bytes 9220
  128.2 1.9 %copy-start.25 = (f32[3,256]{1,0:T(4,128)S(1)}, f32[3,256]{1,0:T(4,128)}, u32[]{:S(2)}) copy-start(f32[3,256]{1,0:T(4,128)} %get-tuple-element.37) | copy-start | bytes 9220
  128.2 1.9 %copy-start.24 = (f32[3,256]{1,0:T(4,128)S(1)}, f32[3,256]{1,0:T(4,128)}, u32[]{:S(2)}) copy-start(f32[3,256]{1,0:T(4,128)} %get-tuple-element.36) | copy-start | bytes 9220
  128.2 1.9 %copy-start.8 = (f32[33,16,256]{2,1,0:T(8,128)S(1)}, f32[33,16,256]{2,1,0:T(8,128)}, u32[]{:S(2)}) copy-start(f32[33,16,256]{2,1,0:T(8,128)} %get-tuple-element.41) | copy-start | bytes 1622020
  128.4 1.8 %copy-start.11 = (bf16[384,768]{1,0:T(8,128)(2,1)}, bf16[384,768]{1,0:T(8,128)(2,1)S(1)}, u32[]{:S(2)}) copy-start(bf16[384,768]{1,0:T(8,128)(2,1)S(1)} %fusion.11) | copy-start | bytes 1769476
  128.4 2.1 %collective-permute-start.13 = (bf16[6,768]{1,0:T(8,128)(2,1)S(1)}, bf16[6,768]{1,0:T(8,128)(2,1)S(1)}, u32[]{:S(2)}, u32[]{:S(2)}) collective-permute-start(bf16[6,768]{1,0:T(8,128)(2,1)S(1)} %slice.223), channel_id=1, source_target_pairs={{0,4},{4,8},{8,12},{12,16},{16,20},{20,24},{24,28},{1,5},{5,9},{9,... | collective-permute-start | bytes 27656 | tf_op jit(solution)/shard_map/ppermute | solution.py:17
  131.7 1.7 %copy-start.5 = (f32[768,384]{1,0:T(8,128)S(1)}, f32[768,384]{1,0:T(8,128)}, u32[]{:S(2)}) copy-start(f32[768,384]{1,0:T(8,128)} %constant.163.clone) | copy-start | bytes 3538948
  133.4 1.3 copy-start.3
  134.1 12.7 %copy-start.22 = (f32[8,16]{1,0:T(8,128)S(1)}, f32[8,16]{1,0:T(8,128)}, u32[]{:S(2)}) copy-start(f32[8,16]{1,0:T(8,128)} %get-tuple-element.44) | copy-start | bytes 1540
  134.1 12.7 %copy-start.23 = (f32[8,16]{1,0:T(8,128)S(1)}, f32[8,16]{1,0:T(8,128)}, u32[]{:S(2)}) copy-start(f32[8,16]{1,0:T(8,128)} %get-tuple-element.45) | copy-start | bytes 1540
  134.1 12.7 %copy-start.33 = (f32[8]{0:T(128)S(1)}, f32[8]{0:T(128)}, u32[]{:S(2)}) copy-start(f32[8]{0:T(128)} %get-tuple-element.49) | copy-start | bytes 100
  134.1 12.8 %copy-start.7 = (f32[33,16,256]{2,1,0:T(8,128)S(1)}, f32[33,16,256]{2,1,0:T(8,128)}, u32[]{:S(2)}) copy-start(f32[33,16,256]{2,1,0:T(8,128)} %copy-done.6) | copy-start | bytes 1622020
  134.1 12.8 %copy-start.19 = (f32[16,256]{1,0:T(8,128)S(1)}, f32[16,256]{1,0:T(8,128)}, u32[]{:S(2)}) copy-start(f32[16,256]{1,0:T(8,128)} %copy-done.18) | copy-start | bytes 49156
  146.9 1.0 copy-start.17
  146.9 1.0 copy-start.20
  147.1 1.4 copy-start.9
  147.1 1.4 copy-start.10
  147.1 1.6 %copy-start.15 = (f32[384,384]{1,0:T(8,128)S(1)}, f32[384,384]{1,0:T(8,128)}, u32[]{:S(2)}) copy-start(f32[384,384]{1,0:T(8,128)} %constant.167) | copy-start | bytes 1769476
  148.7 1.1 copy-start.14

commit v4 on v3

--- a/solution.py
+++ b/solution.py
@@ -22,15 +22,17 @@
     return lax.ppermute(value, "seq", [(s, s ^ mask) for s in range(count)])
 
 
-def gather_weights(weight):
+def gather_weights(weight, ahead=()):
     count = lax.axis_size("seq")
     if count != 8:
         return lax.all_gather(weight, "seq", axis=1, tiled=True)
     me = lax.axis_index("seq")
     over_x = flip(weight, 2)
     over_y = flip(weight, 4)
-    onward = jnp.where(me % 2 == 0, over_x, over_y)
-    diagonal = lax.ppermute(onward, "seq", [(s, s ^ (4 if s % 2 == 0 else 2)) for s in range(8)])
+    over_x, over_y, *_ = lax.optimization_barrier((over_x, over_y, *ahead))
+    by_y = lax.ppermute(over_x, "seq", [(s, s ^ 4) for s in range(0, 8, 2)])
+    by_x = lax.ppermute(over_y, "seq", [(s, s ^ 2) for s in range(1, 8, 2)])
+    diagonal = jnp.where(me % 2 == 0, by_y, by_x)
     pieces = [(0, weight), (2, over_x), (4, over_y), (6, diagonal)]
     pieces += [(mask ^ 1, flip(piece, 1)) for mask, piece in pieces]
     depth = weight.shape[1]
@@ -61,7 +63,7 @@
     down_2 = shift(down_1, [(1, 0), (2, 1)])
     up_3 = shift(up_2, [(2, 3)])
     down_3 = shift(down_2, [(1, 0)])
-    weights = gather_weights(in_weight)
+    weights = gather_weights(in_weight, (up_1, down_1))
 
     def add_rows(value, source):
         portion = lax.dynamic_slice_in_dim(weights, source * depth, depth, 1)

time: 152 us -> 163 us (1.072)
  waiting for transfers between devices: 47.9 us -> 68.5 us
  matrix products: 27.7 us -> 20.9 us
  other arithmetic: 16.3 us -> 12.5 us
  local copies, waits for them, and re-layouts: 28.4 us -> 25.8 us
  Pallas kernels: 10.4 us -> 12.4 us
    ppermute x6, waiting for transfers between devices: 22.2 us -> 67.4 us  [shift(): return lax.ppermute(value, 'ch', pairs)]
    ppermute x6, waiting for transfers between devices: 20.5 us -> 0.8 us  [flip(): return lax.ppermute(value, 'seq', [(s, s ^ mask) for s in range(count)])]
    dot_general x15, matrix products: 20 us -> 14.4 us  [add_rows(): jnp.dot(value, portion[j], preferred_element_type=jnp.float32)]
    ppermute x1 -> x2, waiting for transfers between devices: 4.85 us -> 0.01 us  [the longest x1 0.01 us: gather_weights(): by_y = lax.ppermute(over_x, 'seq', [(s, s ^ 4) for s in range(0, 8, 2)])]
    select_n x1 -> x0, other arithmetic: 4.02 us -> none  [gather_weights(): onward = jnp.where(me % 2 == 0, over_x, over_y)]
    ppermute x1 -> x2, starting transfers between devices: 1.79 us -> 5.26 us  [the longest x1 3.42 us: gather_weights(): by_y = lax.ppermute(over_x, 'seq', [(s, s ^ 4) for s in range(0, 8, 2)])]
    dynamic_update_slice x0 -> x1, other arithmetic: none -> 2.92 us  [gather_weights(): whole = lax.dynamic_update_slice(whole, piece, (0, (me ^ mask) * depth, 0))]
    pallas_call x1, Pallas kernels: 10.4 us -> 12.4 us  [exchange(): pl.pallas_call(lambda *refs: exchange_kernel(count, *refs), out_shape=(ja...]
  transfers between devices with their start and end apart: 14 -> 15, of which waited for: 5 -> 6; matrix products, arithmetic and copies ran while one was open for 40% -> 29% of each run, Pallas kernels for 0% -> 0%
where the time goes in v4:
time: 163 us; the launch traced here: 162 us
  waiting for transfers between devices  68.5 us (42%)
  local copies, waits for them, and re-layouts  25.8 us (16%)
  starting transfers between devices  21.1 us (13%)
  matrix products  20.9 us (13%)
  other arithmetic  12.5 us (8%)
  Pallas kernels  12.4 us (8%)
    ppermute x6, waiting for transfers between devices, shift(): return lax.ppermute(value, 'ch', pairs)  67.4 us
    dot_general x15, matrix products, add_rows(): jnp.dot(value, portion[j], preferred_element_type=jnp.float32)  14.4 us
    dynamic_update_slice x7, local copies, waits for them, and re-layouts, gather_weights(): whole = lax.dynamic_update_slice(whole, piece, (0, (me ^ mask) * depth, 0))  13.2 us
    pallas_call x1, Pallas kernels, exchange(): pl.pallas_call(lambda *refs: exchange_kernel(count, *refs), out_shape=(ja...  12.4 us
    ppermute x6, starting transfers between devices, shift(): return lax.ppermute(value, 'ch', pairs)  10.6 us
    dot_general x6, matrix products, times(): jnp.dot(jnp.asarray(matrix), value, precision=lax.Precision.HIGH, preferr...  6.59 us
    broadcast_in_dim x1, local copies, waits for them, and re-layouts, gather_weights(): whole = jnp.zeros((3, count * depth, weight.shape[2]), weight.dtype)  5.34 us
    ppermute x6, starting transfers between devices, flip(): return lax.ppermute(value, 'seq', [(s, s ^ mask) for s in range(count)])  3.75 us
  transfers between devices with their start and end apart: 15, of which 6 were waited for; matrix products, arithmetic and copies ran while one was open for 29% of the time, Pallas kernels for 0%

profile of v4, /device:TPU:0, one launch (start us, length us, event | category | flops | bytes accessed | tf_op | source)
XLA Modules:
  0.0 162.1 jit_solution(1835772199383643271)
XLA Ops:
  0.0 5.0 %collective-permute-start.2 = (bf16[384,2048]{1,0:T(8,128)(2,1)}, bf16[384,2048]{1,0:T(8,128)(2,1)S(1)}, u32[]{:S(2)}, u32[]{:S(2)}) collective-permute-start(bf16[384,2048]{1,0:T(8,128)(2,1)} %param.12), channel_id=1, source_target_pairs={{0,1},{1,2},{2,3},{4,5},{5,6},{6,7},{8,9},{9,10},{10,11},{12,13},{... | collective-permute-start | bytes 4718600 | tf_op jit(solution)/shard_map/ppermute | solution.py:58
  5.0 1.3 collective-permute-start.3
  6.3 1.6 collective-permute-start
  7.9 1.5 collective-permute-start.1
  9.6 0.8 sqrt_multiply_fusion
  10.4 28.5 %collective-permute-done.2 = bf16[384,2048]{1,0:T(8,128)(2,1)S(1)} collective-permute-done((bf16[384,2048]{1,0:T(8,128)(2,1)}, bf16[384,2048]{1,0:T(8,128)(2,1)S(1)}, u32[]{:S(2)}, u32[]{:S(2)}) %collective-permute-start.2) | collective-permute-done | bytes 1572896 | tf_op jit(solution)/shard_map/ppermute | solution.py:58
  38.9 4.1 %collective-permute-done.3 = bf16[384,2048]{1,0:T(8,128)(2,1)S(1)} collective-permute-done((bf16[384,2048]{1,0:T(8,128)(2,1)}, bf16[384,2048]{1,0:T(8,128)(2,1)S(1)}, u32[]{:S(2)}, u32[]{:S(2)}) %collective-permute-start.3) | collective-permute-done | bytes 1572896 | tf_op jit(solution)/shard_map/ppermute | solution.py:58
  43.0 0.8 collective-permute-done.1
  43.8 3.4 %collective-permute-start.4 = (bf16[3,1024,256]{2,1,0:T(8,128)(2,1)}, bf16[3,1024,256]{2,1,0:T(8,128)(2,1)}, u32[]{:S(2)}, u32[]{:S(2)}) collective-permute-start(bf16[3,1024,256]{2,1,0:T(8,128)(2,1)} %collective-permute-done), channel_id=1, source_target_pairs={{0,16},{8,24},{16,0},{24,8},{1,17},{9,25},{17,1},{25,9},{2,18},{10... | collective-permute-start | bytes 4718600 | tf_op jit(solution)/shard_map/ppermute | solution.py:33
  47.2 1.8 %collective-permute-start.5 = (bf16[3,1024,256]{2,1,0:T(8,128)(2,1)}, bf16[3,1024,256]{2,1,0:T(8,128)(2,1)}, u32[]{:S(2)}, u32[]{:S(2)}) collective-permute-start(bf16[3,1024,256]{2,1,0:T(8,128)(2,1)} %collective-permute-done.1), channel_id=1, source_target_pairs={{4,12},{12,4},{20,28},{28,20},{5,13},{13,5},{21,29},{29,21},{6,14}... | collective-permute-start | bytes 4718600 | tf_op jit(solution)/shard_map/ppermute | solution.py:34
  49.0 1.0 fusion.20
  50.1 0.8 copy-done.6
  51.1 0.7 copy-done.2
  51.7 1.6 multiply_reduce_fusion.2
  53.4 1.0 copy.95
  54.4 0.7 slice.233
  55.0 0.9 copy.96
  56.0 0.5 and_select_fusion
  56.6 5.3 %broadcast_in_dim.25 = bf16[3,8192,256]{2,1,0:T(8,128)(2,1)} broadcast(bf16[]{:T(256)} %constant.137.clone.1), dimensions={} | broadcast | bytes 12582914 | tf_op jit(solution)/shard_map/broadcast_in_dim | solution.py:39
  61.9 1.3 constant_dynamic-update-slice_fusion.8
  63.2 0.7 collective-permute-start.10
  64.0 1.3 collective-permute-start.11
  65.3 2.7 %constant_dynamic-update-slice_fusion.7 = bf16[3,8192,256]{2,1,0:T(8,128)(2,1)} fusion(bf16[3,8192,256]{2,1,0:T(8,128)(2,1)} %constant_dynamic-update-slice_fusion.8, bf16[3,1024,256]{2,1,0:T(8,128)(2,1)} %collective-permute-done, s32[]{:T(128)S(6)} %select_n.152), kind=kLoop, calls=%fused_computation.156 | loop fusion | bytes 3145732 | tf_op jit(solution)/shard_map/dynamic_update_slice | solution.py:41
  68.0 2.7 %constant_dynamic-update-slice_fusion.6 = bf16[3,8192,256]{2,1,0:T(8,128)(2,1)} fusion(bf16[3,8192,256]{2,1,0:T(8,128)(2,1)} %constant_dynamic-update-slice_fusion.7, bf16[3,1024,256]{2,1,0:T(8,128)(2,1)} %collective-permute-done.1, s32[]{:T(128)S(6)} %select_n.153), kind=kLoop, calls=%fused_computation.155 | loop fusion | bytes 3145732 | tf_op jit(solution)/shard_map/dynamic_update_slice | solution.py:41
  71.2 2.9 %constant_dynamic-update-slice_fusion.5 = (bf16[3,8192,256]{2,1,0:T(8,128)(2,1)}, bf16[3,1024,256]{2,1,0:T(8,128)(2,1)S(1)}) fusion(bf16[3,8192,256]{2,1,0:T(8,128)(2,1)} %constant_dynamic-update-slice_fusion.6, s32[]{:T(128)S(6)} %select_n.157, bf16[3,1024,256]{2,1,0:T(8,128)(2,1)} %collective-permute-done.4, ...), kind=kLoop, calls=%fused_computation.154 | loop fusion | flops 786432 | bytes 6291461 | tf_op jit(solution)/shard_map/dynamic_update_slice | solution.py:41
  74.3 0.7 slice_reduce_fusion.6
  74.9 0.7 fusion.86
  75.7 1.4 convolution_multiply_fusion
  77.1 2.1 %fusion = f32[768,256]{0,1:T(8,128)} fusion(f32[384,256]{1,0:T(8,128)S(1)} %constant_dynamic-update-slice_fusion, f32[768,384]{1,0:T(8,128)S(1)} %copy-done.4), kind=kOutput, calls=%fused_computation.6 | convolution fusion | flops 453181440 | bytes 2359296 | tf_op jit(solution)/shard_map/dot_general | solution.py:149
  79.2 0.8 collective-permute-start.12
  79.9 22.2 %collective-permute-done.11 = bf16[384,2048]{1,0:T(8,128)(2,1)S(1)} collective-permute-done((bf16[384,2048]{1,0:T(8,128)(2,1)S(1)}, bf16[384,2048]{1,0:T(8,128)(2,1)S(1)}, u32[]{:S(2)}, u32[]{:S(2)}) %collective-permute-start.11) | collective-permute-done | bytes 1572896 | tf_op jit(solution)/shard_map/ppermute | solution.py:58
  102.2 1.5 collective-permute-start.13
  103.7 2.7 %constant_dynamic-update-slice_fusion.4 = bf16[3,8192,256]{2,1,0:T(8,128)(2,1)} fusion(bf16[3,8192,256]{2,1,0:T(8,128)(2,1)} %get-tuple-element.42, bf16[3,1024,256]{2,1,0:T(8,128)(2,1)} %collective-permute-done.6, s32[]{:T(128)S(6)} %select_n.158), kind=kLoop, calls=%fused_computation.153 | loop fusion | bytes 3145732 | tf_op jit(solution)/shard_map/dynamic_update_slice | solution.py:41
  106.4 1.3 constant_dynamic-update-slice_fusion.3
  107.6 1.3 constant_dynamic-update-slice_fusion.2
  108.9 1.3 constant_dynamic-update-slice_fusion.1
  110.2 0.7 copy-done.1
  110.9 2.0 %convolution_bitcast_fusion.8 = f32[384,256]{1,0:T(8,128)S(1)} fusion(bf16[384,2048]{1,0:T(8,128)(2,1)S(1)} %copy-done.1, bf16[3,8192,256]{2,1,0:T(8,128)(2,1)} %constant_dynamic-update-slice_fusion.1, s32[]{:T(128)S(6)} %select_n.162), kind=kOutput, calls=%fused_computation.15 | convolution fusion | flops 402653184 | bytes 3014660 | tf_op jit(solution)/shard_map/dot_general | solution.py:71
  112.9 2.3 %convolution_bitcast_fusion.7 = f32[384,256]{1,0:T(8,128)S(1)} fusion(bf16[384,2048]{1,0:T(8,128)(2,1)S(1)} %copy-done.1, bf16[3,8192,256]{2,1,0:T(8,128)(2,1)} %constant_dynamic-update-slice_fusion.1, s32[]{:T(128)S(6)} %add.250, s32[]{:T(128)S(6)} %select_n.162), kind=kOutput, calls=%fused_computation.14 | convolution fusion | flops 402653184 | bytes 3014664 | tf_op jit(solution)/shard_map/dot_general | solution.py:71
  115.2 1.8 %convolution_bitcast_fusion.6 = f32[384,256]{1,0:T(8,128)S(1)} fusion(bf16[384,2048]{1,0:T(8,128)(2,1)S(1)} %copy-done.1, bf16[3,8192,256]{2,1,0:T(8,128)(2,1)} %constant_dynamic-update-slice_fusion.1, s32[]{:T(128)S(6)} %add.251, s32[]{:T(128)S(6)} %select_n.162), kind=kOutput, calls=%fused_computation.13 | convolution fusion | flops 402653184 | bytes 3014664 | tf_op jit(solution)/shard_map/dot_general | solution.py:71
  117.0 1.8 %convolution_bitcast_fusion = f32[384,256]{1,0:T(8,128)S(1)} fusion(bf16[384,2048]{1,0:T(8,128)(2,1)S(1)} %collective-permute-done.3, bf16[3,8192,256]{2,1,0:T(8,128)(2,1)} %constant_dynamic-update-slice_fusion.1, s32[]{:T(128)S(6)} %add.251, s32[]{:T(128)S(6)} %select_n.166), kind=kOutput, calls=%fused_computation.7 | convolution fusion | flops 402653184 | bytes 3014664 | tf_op jit(solution)/shard_map/dot_general | solution.py:71
  118.8 0.6 convolution_bitcast_fusion.1
  119.4 0.6 convolution_bitcast_fusion.2
  120.0 0.6 convolution_bitcast_fusion.5
  120.6 0.6 convolution_bitcast_fusion.4
  121.2 0.6 convolution_bitcast_fusion.3
  121.8 0.6 fusion.16
  122.4 0.6 fusion.17
  123.0 0.6 fusion.18
  123.9 12.5 %collective-permute-done.13 = bf16[384,2048]{1,0:T(8,128)(2,1)S(1)} collective-permute-done((bf16[384,2048]{1,0:T(8,128)(2,1)S(1)}, bf16[384,2048]{1,0:T(8,128)(2,1)S(1)}, u32[]{:S(2)}, u32[]{:S(2)}) %collective-permute-start.13) | collective-permute-done | bytes 1572896 | tf_op jit(solution)/shard_map/ppermute | solution.py:58
  136.4 0.6 fusion.15
  137.0 0.6 fusion.14
  137.6 0.6 fusion.13
  138.4 1.5 collective-permute-start.14
  140.7 1.0 fusion.4
  141.7 0.6 slice.242.refs_1_
  142.3 0.6 fusion.97
  143.1 0.6 multiply_reduce_fusion.1
  143.8 0.6 pad_maximum_fusion.refs_0_
  144.4 12.4 %shard_map.100 = (bf16[8,32,256]{2,1,0:T(8,128)(2,1)}, bf16[128,256]{1,0:T(8,128)(2,1)}) custom-call(bf16[32,256]{1,0:T(8,128)(2,1)} %pad_maximum_fusion.refs_0_, bf16[128,256]{1,0:T(8,128)(2,1)} %slice.242.refs_1_), custom_call_target="tpu_custom_call" | custom-call | tf_op jit(solution)/shard_map/pallas_call | solution.py:116
  156.8 0.9 convert_element_type.72
  159.0 0.5 fusion.57
  159.7 0.6 fusion.33
  160.8 1.3 fusion.12
  (105 shorter events, 4.1 us)
Async XLA Ops:
  0.0 38.9 %collective-permute-start.2 = (bf16[384,2048]{1,0:T(8,128)(2,1)}, bf16[384,2048]{1,0:T(8,128)(2,1)S(1)}, u32[]{:S(2)}, u32[]{:S(2)}) collective-permute-start(bf16[384,2048]{1,0:T(8,128)(2,1)} %param.12), channel_id=1, source_target_pairs={{0,1},{1,2},{2,3},{4,5},{5,6},{6,7},{8,9},{9,10},{10,11},{12,13},{... | collective-permute-start | bytes 4718600 | tf_op jit(solution)/shard_map/ppermute | solution.py:58
  5.0 38.0 %collective-permute-start.3 = (bf16[384,2048]{1,0:T(8,128)(2,1)}, bf16[384,2048]{1,0:T(8,128)(2,1)S(1)}, u32[]{:S(2)}, u32[]{:S(2)}) collective-permute-start(bf16[384,2048]{1,0:T(8,128)(2,1)} %param.12), channel_id=1, source_target_pairs={{1,0},{2,1},{3,2},{5,4},{6,5},{7,6},{9,8},{10,9},{11,10},{13,12},{... | collective-permute-start | bytes 4718600 | tf_op jit(solution)/shard_map/ppermute | solution.py:58
  6.3 36.7 %collective-permute-start = (bf16[3,1024,256]{2,1,0:T(8,128)(2,1)}, bf16[3,1024,256]{2,1,0:T(8,128)(2,1)}, u32[]{:S(2)}, u32[]{:S(2)}) collective-permute-start(bf16[3,1024,256]{2,1,0:T(8,128)(2,1)} %param.13), channel_id=1, source_target_pairs={{0,8},{4,12},{8,0},{12,4},{16,24},{20,28},{24,16},{28,20},{1,9},{5... | collective-permute-start | bytes 4718600 | tf_op jit(solution)/shard_map/ppermute | solution.py:22
  7.9 35.9 %collective-permute-start.1 = (bf16[3,1024,256]{2,1,0:T(8,128)(2,1)}, bf16[3,1024,256]{2,1,0:T(8,128)(2,1)}, u32[]{:S(2)}, u32[]{:S(2)}) collective-permute-start(bf16[3,1024,256]{2,1,0:T(8,128)(2,1)} %param.13), channel_id=1, source_target_pairs={{0,16},{4,20},{8,24},{12,28},{16,0},{20,4},{24,8},{28,12},{1,17},{... | collective-permute-start | bytes 4718600 | tf_op jit(solution)/shard_map/ppermute | solution.py:22
  9.4 64.7 %collective-permute-start.6 = (bf16[3,1024,256]{2,1,0:T(8,128)(2,1)}, bf16[3,1024,256]{2,1,0:T(8,128)(2,1)}, u32[]{:S(2)}, u32[]{:S(2)}) collective-permute-start(bf16[3,1024,256]{2,1,0:T(8,128)(2,1)} %param.13), channel_id=1, source_target_pairs={{0,4},{4,0},{8,12},{12,8},{16,20},{20,16},{24,28},{28,24},{1,5},{5... | collective-permute-start | bytes 4718600 | tf_op jit(solution)/shard_map/ppermute | solution.py:22
  10.4 43.0 %copy-start.18 = (f32[16,256]{1,0:T(8,128)}, f32[16,256]{1,0:T(8,128)S(1)}, u32[]{:S(2)}) copy-start(f32[16,256]{1,0:T(8,128)S(1)} %get-tuple-element.46) | copy-start | bytes 49156
  43.8 26.9 %collective-permute-start.4 = (bf16[3,1024,256]{2,1,0:T(8,128)(2,1)}, bf16[3,1024,256]{2,1,0:T(8,128)(2,1)}, u32[]{:S(2)}, u32[]{:S(2)}) collective-permute-start(bf16[3,1024,256]{2,1,0:T(8,128)(2,1)} %collective-permute-done), channel_id=1, source_target_pairs={{0,16},{8,24},{16,0},{24,8},{1,17},{9,25},{17,1},{25,9},{2,18},{10... | collective-permute-start | bytes 4718600 | tf_op jit(solution)/shard_map/ppermute | solution.py:33
  47.2 23.5 %collective-permute-start.5 = (bf16[3,1024,256]{2,1,0:T(8,128)(2,1)}, bf16[3,1024,256]{2,1,0:T(8,128)(2,1)}, u32[]{:S(2)}, u32[]{:S(2)}) collective-permute-start(bf16[3,1024,256]{2,1,0:T(8,128)(2,1)} %collective-permute-done.1), channel_id=1, source_target_pairs={{4,12},{12,4},{20,28},{28,20},{5,13},{13,5},{21,29},{29,21},{6,14}... | collective-permute-start | bytes 4718600 | tf_op jit(solution)/shard_map/ppermute | solution.py:34
  50.1 0.8 copy-start.6
  50.9 0.8 copy-start.2
  56.6 5.3 %copy-start.12 = (bf16[3,1024,256]{2,1,0:T(8,128)(2,1)S(1)}, bf16[3,1024,256]{2,1,0:T(8,128)(2,1)}, u32[]{:S(2)}) copy-start(bf16[3,1024,256]{2,1,0:T(8,128)(2,1)} %param.13) | copy-start | bytes 4718596
  63.2 16.0 %collective-permute-start.10 = (bf16[384,2048]{1,0:T(8,128)(2,1)S(1)}, bf16[384,2048]{1,0:T(8,128)(2,1)S(1)}, u32[]{:S(2)}, u32[]{:S(2)}) collective-permute-start(bf16[384,2048]{1,0:T(8,128)(2,1)S(1)} %collective-permute-done.2), channel_id=1, source_target_pairs={{1,2},{2,3},{5,6},{6,7},{9,10},{10,11},{13,14},{14,15},{17,18},{18... | collective-permute-start | bytes 4718600 | tf_op jit(solution)/shard_map/ppermute | solution.py:58
  64.0 38.2 %collective-permute-start.11 = (bf16[384,2048]{1,0:T(8,128)(2,1)S(1)}, bf16[384,2048]{1,0:T(8,128)(2,1)S(1)}, u32[]{:S(2)}, u32[]{:S(2)}) collective-permute-start(bf16[384,2048]{1,0:T(8,128)(2,1)S(1)} %collective-permute-done.3), channel_id=1, source_target_pairs={{1,0},{2,1},{5,4},{6,5},{9,8},{10,9},{13,12},{14,13},{17,16},{18,1... | collective-permute-start | bytes 4718600 | tf_op jit(solution)/shard_map/ppermute | solution.py:58
  70.6 3.6 %copy-start.21 = (f32[7,3,256]{2,0,1:T(8,128)S(1)}, f32[7,3,256]{2,0,1:T(8,128)}, u32[]{:S(2)}) copy-start(f32[7,3,256]{2,0,1:T(8,128)} %param.14) | copy-start | bytes 64516
  70.6 5.0 %copy-start.11 = (f32[12,32,256]{2,1,0:T(8,128)S(1)}, f32[12,32,256]{2,1,0:T(8,128)}, u32[]{:S(2)}) copy-start(f32[12,32,256]{2,1,0:T(8,128)} %copy.95) | copy-start | bytes 1179652
  70.6 5.0 %copy-start.15 = (f32[128,256]{1,0:T(8,128)S(1)}, f32[128,256]{1,0:T(8,128)}, u32[]{:S(2)}) copy-start(f32[128,256]{1,0:T(8,128)} %param.15) | copy-start | bytes 393220
  70.6 5.0 %copy-start.17 = (f32[768,128]{1,0:T(8,128)S(1)}, f32[768,128]{1,0:T(8,128)}, u32[]{:S(2)}) copy-start(f32[768,128]{1,0:T(8,128)} %constant.164.clone) | copy-start | bytes 1179652
  70.6 35.7 %collective-permute-start.7 = (bf16[3,1024,256]{2,1,0:T(8,128)(2,1)}, bf16[3,1024,256]{2,1,0:T(8,128)(2,1)S(1)}, u32[]{:S(2)}, u32[]{:S(2)}) collective-permute-start(bf16[3,1024,256]{2,1,0:T(8,128)(2,1)} %collective-permute-done), channel_id=1, source_target_pairs={{0,4},{4,0},{8,12},{12,8},{16,20},{20,16},{24,28},{28,24},{1,5},{5... | collective-permute-start | bytes 4718600 | tf_op jit(solution)/shard_map/ppermute | solution.py:22
  70.7 36.9 %collective-permute-start.8 = (bf16[3,1024,256]{2,1,0:T(8,128)(2,1)}, bf16[3,1024,256]{2,1,0:T(8,128)(2,1)S(1)}, u32[]{:S(2)}, u32[]{:S(2)}) collective-permute-start(bf16[3,1024,256]{2,1,0:T(8,128)(2,1)} %collective-permute-done.1), channel_id=1, source_target_pairs={{0,4},{4,0},{8,12},{12,8},{16,20},{20,16},{24,28},{28,24},{1,5},{5... | collective-permute-start | bytes 4718600 | tf_op jit(solution)/shard_map/ppermute | solution.py:22
  74.1 3.0 %copy-start.4 = (f32[768,384]{1,0:T(8,128)S(1)}, f32[768,384]{1,0:T(8,128)}, u32[]{:S(2)}) copy-start(f32[768,384]{1,0:T(8,128)} %constant.163.clone) | copy-start | bytes 3538948
  74.2 34.8 %collective-permute-start.9 = (bf16[3,1024,256]{2,1,0:T(8,128)(2,1)S(1)}, bf16[3,1024,256]{2,1,0:T(8,128)(2,1)S(1)}, u32[]{:S(2)}, u32[]{:S(2)}) collective-permute-start(bf16[3,1024,256]{2,1,0:T(8,128)(2,1)S(1)} %get-tuple-element.43), channel_id=1, source_target_pairs={{0,4},{4,0},{8,12},{12,8},{16,20},{20,16},{24,28},{28,24},{1,5},{5... | collective-permute-start | bytes 4718600 | tf_op jit(solution)/shard_map/ppermute | solution.py:22
  79.2 44.7 %collective-permute-start.12 = (bf16[384,2048]{1,0:T(8,128)(2,1)S(1)}, bf16[384,2048]{1,0:T(8,128)(2,1)S(1)}, u32[]{:S(2)}, u32[]{:S(2)}) collective-permute-start(bf16[384,2048]{1,0:T(8,128)(2,1)S(1)} %collective-permute-done.10), channel_id=1, source_target_pairs={{2,3},{6,7},{10,11},{14,15},{18,19},{22,23},{26,27},{30,31}} | collective-permute-start | bytes 4718600 | tf_op jit(solution)/shard_map/ppermute | solution.py:58
  102.2 34.2 %collective-permute-start.13 = (bf16[384,2048]{1,0:T(8,128)(2,1)S(1)}, bf16[384,2048]{1,0:T(8,128)(2,1)S(1)}, u32[]{:S(2)}, u32[]{:S(2)}) collective-permute-start(bf16[384,2048]{1,0:T(8,128)(2,1)S(1)} %collective-permute-done.11), channel_id=1, source_target_pairs={{1,0},{5,4},{9,8},{13,12},{17,16},{21,20},{25,24},{29,28}} | collective-permute-start | bytes 4718600 | tf_op jit(solution)/shard_map/ppermute | solution.py:58
  108.9 2.0 %copy-start.1 = (bf16[384,2048]{1,0:T(8,128)(2,1)S(1)}, bf16[384,2048]{1,0:T(8,128)(2,1)}, u32[]{:S(2)}) copy-start(bf16[384,2048]{1,0:T(8,128)(2,1)} %param.12) | copy-start | bytes 4718596
  110.9 7.9 %copy-start = (bf16[3,8192,256]{2,1,0:T(8,128)(2,1)S(1)}, bf16[3,8192,256]{2,1,0:T(8,128)(2,1)}, u32[]{:S(2)}) copy-start(bf16[3,8192,256]{2,1,0:T(8,128)(2,1)} %constant_dynamic-update-slice_fusion.1) | copy-start | bytes 37748740
  138.2 1.8 %copy-start.30 = (f32[3,256]{1,0:T(4,128)S(1)}, f32[3,256]{1,0:T(4,128)}, u32[]{:S(2)}) copy-start(f32[3,256]{1,0:T(4,128)} %get-tuple-element.35) | copy-start | bytes 9220
  138.2 1.8 %copy-start.29 = (f32[3,256]{1,0:T(4,128)S(1)}, f32[3,256]{1,0:T(4,128)}, u32[]{:S(2)}) copy-start(f32[3,256]{1,0:T(4,128)} %get-tuple-element.39) | copy-start | bytes 9220
  138.2 1.8 %copy-start.28 = (f32[3,256]{1,0:T(4,128)S(1)}, f32[3,256]{1,0:T(4,128)}, u32[]{:S(2)}) copy-start(f32[3,256]{1,0:T(4,128)} %get-tuple-element.38) | copy-start | bytes 9220
  138.2 1.8 %copy-start.27 = (f32[3,256]{1,0:T(4,128)S(1)}, f32[3,256]{1,0:T(4,128)}, u32[]{:S(2)}) copy-start(f32[3,256]{1,0:T(4,128)} %get-tuple-element.37) | copy-start | bytes 9220
  138.2 1.9 %copy-start.26 = (f32[3,256]{1,0:T(4,128)S(1)}, f32[3,256]{1,0:T(4,128)}, u32[]{:S(2)}) copy-start(f32[3,256]{1,0:T(4,128)} %get-tuple-element.36) | copy-start | bytes 9220
  138.2 1.9 %copy-start.25 = (f32[3,256]{1,0:T(4,128)S(1)}, f32[3,256]{1,0:T(4,128)}, u32[]{:S(2)}) copy-start(f32[3,256]{1,0:T(4,128)} %get-tuple-element.41) | copy-start | bytes 9220
  138.3 1.9 %copy-start.24 = (f32[3,256]{1,0:T(4,128)S(1)}, f32[3,256]{1,0:T(4,128)}, u32[]{:S(2)}) copy-start(f32[3,256]{1,0:T(4,128)} %get-tuple-element.40) | copy-start | bytes 9220
  138.3 1.9 %copy-start.8 = (f32[33,16,256]{2,1,0:T(8,128)S(1)}, f32[33,16,256]{2,1,0:T(8,128)}, u32[]{:S(2)}) copy-start(f32[33,16,256]{2,1,0:T(8,128)} %get-tuple-element.45) | copy-start | bytes 1622020
  138.4 2.1 %collective-permute-start.14 = (bf16[6,768]{1,0:T(8,128)(2,1)S(1)}, bf16[6,768]{1,0:T(8,128)(2,1)S(1)}, u32[]{:S(2)}, u32[]{:S(2)}) collective-permute-start(bf16[6,768]{1,0:T(8,128)(2,1)S(1)} %slice.223), channel_id=1, source_target_pairs={{0,4},{4,8},{8,12},{12,16},{16,20},{20,24},{24,28},{1,5},{5,9},{9,... | collective-permute-start | bytes 27656 | tf_op jit(solution)/shard_map/ppermute | solution.py:17
  140.7 1.7 %copy-start.5 = (f32[768,384]{1,0:T(8,128)S(1)}, f32[768,384]{1,0:T(8,128)}, u32[]{:S(2)}) copy-start(f32[768,384]{1,0:T(8,128)} %constant.163.clone) | copy-start | bytes 3538948
  142.3 1.3 copy-start.3
  143.0 14.8 %copy-start.22 = (f32[8,16]{1,0:T(8,128)S(1)}, f32[8,16]{1,0:T(8,128)}, u32[]{:S(2)}) copy-start(f32[8,16]{1,0:T(8,128)} %get-tuple-element.48) | copy-start | bytes 1540
  143.0 14.8 %copy-start.23 = (f32[8,16]{1,0:T(8,128)S(1)}, f32[8,16]{1,0:T(8,128)}, u32[]{:S(2)}) copy-start(f32[8,16]{1,0:T(8,128)} %get-tuple-element.49) | copy-start | bytes 1540
  143.0 14.8 %copy-start.31 = (f32[8]{0:T(128)S(1)}, f32[8]{0:T(128)}, u32[]{:S(2)}) copy-start(f32[8]{0:T(128)} %get-tuple-element.53) | copy-start | bytes 100
  143.0 14.9 %copy-start.7 = (f32[33,16,256]{2,1,0:T(8,128)S(1)}, f32[33,16,256]{2,1,0:T(8,128)}, u32[]{:S(2)}) copy-start(f32[33,16,256]{2,1,0:T(8,128)} %copy-done.6) | copy-start | bytes 1622020
  143.0 14.9 %copy-start.19 = (f32[16,256]{1,0:T(8,128)S(1)}, f32[16,256]{1,0:T(8,128)}, u32[]{:S(2)}) copy-start(f32[16,256]{1,0:T(8,128)} %copy-done.18) | copy-start | bytes 49156
  158.0 1.0 copy-start.16
  158.0 1.0 copy-start.20
  158.1 1.4 copy-start.9
  158.1 1.4 copy-start.10
  158.1 1.6 copy-start.14
  159.7 1.1 copy-start.13

commit v5 on v4

--- a/solution.py
+++ b/solution.py
@@ -30,9 +30,8 @@
     over_x = flip(weight, 2)
     over_y = flip(weight, 4)
     over_x, over_y, *_ = lax.optimization_barrier((over_x, over_y, *ahead))
-    by_y = lax.ppermute(over_x, "seq", [(s, s ^ 4) for s in range(0, 8, 2)])
-    by_x = lax.ppermute(over_y, "seq", [(s, s ^ 2) for s in range(1, 8, 2)])
-    diagonal = jnp.where(me % 2 == 0, by_y, by_x)
+    onward = jnp.where(me % 2 == 0, over_x, over_y)
+    diagonal = lax.ppermute(onward, "seq", [(s, s ^ (4 if s % 2 == 0 else 2)) for s in range(8)])
     pieces = [(0, weight), (2, over_x), (4, over_y), (6, diagonal)]
     pieces += [(mask ^ 1, flip(piece, 1)) for mask, piece in pieces]
     depth = weight.shape[1]

time: 163 us -> 157 us (0.963)
  waiting for transfers between devices: 68.5 us -> 55.4 us
  matrix products: 20.9 us -> 27.6 us
  starting transfers between devices: 21.1 us -> 17.8 us
  local copies, waits for them, and re-layouts: 25.8 us -> 28.9 us
  other arithmetic: 12.5 us -> 15.2 us
  Pallas kernels: 12.4 us -> 10.4 us
    ppermute x6, waiting for transfers between devices: 67.4 us -> 49.2 us  [shift(): return lax.ppermute(value, 'ch', pairs)]
    dot_general x15, matrix products: 14.4 us -> 20 us  [add_rows(): jnp.dot(value, portion[j], preferred_element_type=jnp.float32)]
    ppermute x2 -> x1, waiting for transfers between devices: 0.01 us -> 5.08 us  [gather_weights(): lax.ppermute(onward, 'seq', [(s, s ^ (4 if s % 2 == 0 else 2)) for s in r...]
    select_n x0 -> x1, other arithmetic: none -> 4 us  [gather_weights(): onward = jnp.where(me % 2 == 0, over_x, over_y)]
    ppermute x2 -> x1, starting transfers between devices: 5.26 us -> 1.54 us  [gather_weights(): lax.ppermute(onward, 'seq', [(s, s ^ (4 if s % 2 == 0 else 2)) for s in r...]
    dynamic_update_slice x1 -> x0, other arithmetic: 2.92 us -> none  [gather_weights(): whole = lax.dynamic_update_slice(whole, piece, (0, (me ^ mask) * depth, 0))]
    pallas_call x1, Pallas kernels: 12.4 us -> 10.4 us  [exchange(): pl.pallas_call(lambda *refs: exchange_kernel(count, *refs), out_shape=(ja...]
  transfers between devices with their start and end apart: 15 -> 14, of which waited for: 6 -> 7; matrix products, arithmetic and copies ran while one was open for 29% -> 38% of each run, Pallas kernels for 0% -> 0%
where the time goes in v5:
time: 157 us; the launch traced here: 156 us
  waiting for transfers between devices  55.4 us (35%)
  local copies, waits for them, and re-layouts  28.9 us (18%)
  matrix products  27.6 us (18%)
  starting transfers between devices  17.8 us (11%)
  other arithmetic  15.2 us (10%)
  Pallas kernels  10.4 us (7%)
    ppermute x6, waiting for transfers between devices, shift(): return lax.ppermute(value, 'ch', pairs)  49.2 us
    dot_general x15, matrix products, add_rows(): jnp.dot(value, portion[j], preferred_element_type=jnp.float32)  20 us
    dynamic_update_slice x7, local copies, waits for them, and re-layouts, gather_weights(): whole = lax.dynamic_update_slice(whole, piece, (0, (me ^ mask) * depth, 0))  14.6 us
    ppermute x6, starting transfers between devices, shift(): return lax.ppermute(value, 'ch', pairs)  11.6 us
    pallas_call x1, Pallas kernels, exchange(): pl.pallas_call(lambda *refs: exchange_kernel(count, *refs), out_shape=(ja...  10.4 us
    dot_general x6, matrix products, times(): jnp.dot(jnp.asarray(matrix), value, precision=lax.Precision.HIGH, preferr...  7.63 us
    broadcast_in_dim x1, local copies, waits for them, and re-layouts, gather_weights(): whole = jnp.zeros((3, count * depth, weight.shape[2]), weight.dtype)  5.34 us
    ppermute x1, waiting for transfers between devices, gather_weights(): lax.ppermute(onward, 'seq', [(s, s ^ (4 if s % 2 == 0 else 2)) for s in r...  5.08 us
  transfers between devices with their start and end apart: 14, of which 7 were waited for; matrix products, arithmetic and copies ran while one was open for 38% of the time, Pallas kernels for 0%

profile of v5, /device:TPU:0, one launch (start us, length us, event | category | flops | bytes accessed | tf_op | source)
XLA Modules:
  0.0 156.2 jit_solution(15506045123475329183)
XLA Ops:
  0.0 5.0 %collective-permute-start.2 = (bf16[384,2048]{1,0:T(8,128)(2,1)}, bf16[384,2048]{1,0:T(8,128)(2,1)S(1)}, u32[]{:S(2)}, u32[]{:S(2)}) collective-permute-start(bf16[384,2048]{1,0:T(8,128)(2,1)} %param.12), channel_id=1, source_target_pairs={{0,1},{1,2},{2,3},{4,5},{5,6},{6,7},{8,9},{9,10},{10,11},{12,13},{... | collective-permute-start | bytes 4718600 | tf_op jit(solution)/shard_map/ppermute | solution.py:57
  5.0 1.3 collective-permute-start.3
  6.3 1.6 collective-permute-start
  7.9 1.5 collective-permute-start.1
  9.4 5.3 %broadcast_in_dim.25 = bf16[3,8192,256]{2,1,0:T(8,128)(2,1)} broadcast(bf16[]{:T(256)} %constant.137.clone.1), dimensions={} | broadcast | bytes 12582914 | tf_op jit(solution)/shard_map/broadcast_in_dim | solution.py:38
  14.8 1.3 constant_dynamic-update-slice_fusion.8
  16.1 22.8 %collective-permute-done.2 = bf16[384,2048]{1,0:T(8,128)(2,1)S(1)} collective-permute-done((bf16[384,2048]{1,0:T(8,128)(2,1)}, bf16[384,2048]{1,0:T(8,128)(2,1)S(1)}, u32[]{:S(2)}, u32[]{:S(2)}) %collective-permute-start.2) | collective-permute-done | bytes 1572896 | tf_op jit(solution)/shard_map/ppermute | solution.py:57
  38.9 4.1 %collective-permute-done.3 = bf16[384,2048]{1,0:T(8,128)(2,1)S(1)} collective-permute-done((bf16[384,2048]{1,0:T(8,128)(2,1)}, bf16[384,2048]{1,0:T(8,128)(2,1)S(1)}, u32[]{:S(2)}, u32[]{:S(2)}) %collective-permute-start.3) | collective-permute-done | bytes 1572896 | tf_op jit(solution)/shard_map/ppermute | solution.py:57
  43.0 0.8 collective-permute-done.1
  43.8 2.7 %constant_dynamic-update-slice_fusion.7 = bf16[3,8192,256]{2,1,0:T(8,128)(2,1)} fusion(bf16[3,8192,256]{2,1,0:T(8,128)(2,1)} %constant_dynamic-update-slice_fusion.8, bf16[3,1024,256]{2,1,0:T(8,128)(2,1)} %collective-permute-done, s32[]{:T(128)S(6)} %select_n.152), kind=kLoop, calls=%fused_computation.156 | loop fusion | bytes 3145732 | tf_op jit(solution)/shard_map/dynamic_update_slice | solution.py:40
  46.5 4.0 %broadcast_select_fusion = (bf16[3,1024,256]{2,1,0:T(8,128)(2,1)}, bf16[3,8192,256]{2,1,0:T(8,128)(2,1)}) fusion(bf16[3,1024,256]{2,1,0:T(8,128)(2,1)} %collective-permute-done, bf16[3,1024,256]{2,1,0:T(8,128)(2,1)} %collective-permute-done.1, pred[]{:T(512)S(6)} %eq.25, bf16[3,8192,256]{2,1,0:T(8,128)(2,1)} %constant_dynamic-update-slice_fusion.7, ...), kind=kLoop, calls=%fused_computation.3 | loop fusion | flops 786432 | bytes 6291461 | tf_op jit(solution)/shard_map/jit(_where)/select_n | solution.py:33
  50.5 1.5 collective-permute-start.4
  52.3 1.0 fusion.20
  53.6 0.5 copy-done.6
  54.1 1.3 collective-permute-start.10
  55.4 1.8 %collective-permute-start.9 = (bf16[384,2048]{1,0:T(8,128)(2,1)S(1)}, bf16[384,2048]{1,0:T(8,128)(2,1)}, u32[]{:S(2)}, u32[]{:S(2)}) collective-permute-start(bf16[384,2048]{1,0:T(8,128)(2,1)S(1)} %collective-permute-done.2), channel_id=1, source_target_pairs={{1,2},{2,3},{5,6},{6,7},{9,10},{10,11},{13,14},{14,15},{17,18},{18... | collective-permute-start | bytes 4718600 | tf_op jit(solution)/shard_map/ppermute | solution.py:57
  57.3 2.4 %multiply_reduce_fusion.2 = f32[32,12,256]{2,1,0:T(8,128)} fusion(f32[16,256]{1,0:T(8,128)S(1)} %get-tuple-element.46, f32[12,16,256]{2,1,0:T(8,128)S(1)} %exponential_multiply_fusion, f32[32,16,256]{2,1,0:T(8,128)S(1)} %slice.232), kind=kLoop, calls=%fused_computation.2 | loop fusion | flops 4620288 | bytes 1130496 | tf_op jit(solution)/shard_map/reduce_sum | solution.py:170
  59.7 2.0 %copy.95 = f32[12,32,256]{2,1,0:T(8,128)} copy(f32[12,32,256]{2,0,1:T(8,128)} %bitcast.100) | data formatting | bytes 786432 | tf_op jit(solution)/shard_map/transpose | solution.py:171
  61.7 1.6 %slice.233 = f32[4,32,256]{2,0,1:T(4,128)} slice(f32[12,32,256]{2,0,1:T(8,128)} %bitcast.101), slice={[0:4], [0:32], [0:256]} | slice | bytes 262144 | tf_op jit(solution)/shard_map/slice.24
  63.3 1.6 %copy.96 = f32[4,32,256]{2,1,0:T(8,128)} copy(f32[4,32,256]{2,0,1:T(4,128)} %slice.233) | data formatting | bytes 262144 | tf_op jit(solution)/shard_map/slice.24
  64.9 0.5 and_select_fusion
  65.5 0.7 slice_reduce_fusion.6
  66.1 5.1 %collective-permute-done.4 = bf16[3,1024,256]{2,1,0:T(8,128)(2,1)} collective-permute-done((bf16[3,1024,256]{2,1,0:T(8,128)(2,1)}, bf16[3,1024,256]{2,1,0:T(8,128)(2,1)}, u32[]{:S(2)}, u32[]{:S(2)}) %collective-permute-start.4) | collective-permute-done | bytes 1572896 | tf_op jit(solution)/shard_map/ppermute | solution.py:34
  71.2 0.7 fusion.86
  71.9 1.6 %constant_dynamic-update-slice_fusion = f32[384,256]{1,0:T(8,128)} fusion(f32[384,256]{1,0:T(8,128)} %bitcast.103, f32[128,256]{1,0:T(8,128)S(1)} %copy-done.15, f32[4,32,256]{2,1,0:T(8,128)} %copy.96), kind=kLoop, calls=%fused_computation.144 | loop fusion | flops 32768 | bytes 393216 | tf_op jit(solution)/shard_map/scatter-add | solution.py:172
  73.5 2.4 %convolution_multiply_fusion = f32[768,256]{0,1:T(8,128)} fusion(f32[768,128]{1,0:T(8,128)} %constant.164.clone, f32[128,256]{1,0:T(8,128)S(1)} %copy-done.15), kind=kOutput, calls=%fused_computation.4 | convolution fusion | flops 151191552 | bytes 1310720 | tf_op jit(solution)/shard_map/dot_general | solution.py:148
  76.0 2.1 %fusion = f32[768,256]{0,1:T(8,128)} fusion(f32[384,256]{1,0:T(8,128)S(1)} %copy-done.11, f32[768,384]{1,0:T(8,128)S(1)} %copy-done.4), kind=kOutput, calls=%fused_computation.6 | convolution fusion | flops 453181440 | bytes 2359296 | tf_op jit(solution)/shard_map/dot_general | solution.py:148
  78.1 2.7 %constant_dynamic-update-slice_fusion.5 = bf16[3,8192,256]{2,1,0:T(8,128)(2,1)} fusion(bf16[3,8192,256]{2,1,0:T(8,128)(2,1)} %get-tuple-element.43, bf16[3,1024,256]{2,1,0:T(8,128)(2,1)} %collective-permute-done.4, s32[]{:T(128)S(6)} %select_n.157), kind=kLoop, calls=%fused_computation.154 | loop fusion | bytes 3145732 | tf_op jit(solution)/shard_map/dynamic_update_slice | solution.py:40
  80.7 0.8 collective-permute-start.11
  81.5 11.5 %collective-permute-done.10 = bf16[384,2048]{1,0:T(8,128)(2,1)} collective-permute-done((bf16[384,2048]{1,0:T(8,128)(2,1)S(1)}, bf16[384,2048]{1,0:T(8,128)(2,1)}, u32[]{:S(2)}, u32[]{:S(2)}) %collective-permute-start.10) | collective-permute-done | bytes 1572896 | tf_op jit(solution)/shard_map/ppermute | solution.py:57
  93.0 1.5 collective-permute-start.12
  94.5 2.7 %constant_dynamic-update-slice_fusion.4 = bf16[3,8192,256]{2,1,0:T(8,128)(2,1)} fusion(bf16[3,8192,256]{2,1,0:T(8,128)(2,1)} %constant_dynamic-update-slice_fusion.5, bf16[3,1024,256]{2,1,0:T(8,128)(2,1)} %collective-permute-done.5, s32[]{:T(128)S(6)} %select_n.158), kind=kLoop, calls=%fused_computation.153 | loop fusion | bytes 3145732 | tf_op jit(solution)/shard_map/dynamic_update_slice | solution.py:40
  97.2 2.7 %constant_dynamic-update-slice_fusion.3 = bf16[3,8192,256]{2,1,0:T(8,128)(2,1)} fusion(bf16[3,8192,256]{2,1,0:T(8,128)(2,1)} %constant_dynamic-update-slice_fusion.4, bf16[3,1024,256]{2,1,0:T(8,128)(2,1)} %collective-permute-done.6, s32[]{:T(128)S(6)} %select_n.159), kind=kLoop, calls=%fused_computation.152 | loop fusion | bytes 3145732 | tf_op jit(solution)/shard_map/dynamic_update_slice | solution.py:40
  99.9 1.3 constant_dynamic-update-slice_fusion.2
  101.2 1.3 constant_dynamic-update-slice_fusion.1
  102.4 0.7 copy-done.1
  103.1 2.0 %convolution_bitcast_fusion.8 = f32[384,256]{1,0:T(8,128)S(1)} fusion(bf16[384,2048]{1,0:T(8,128)(2,1)S(1)} %copy-done.1, bf16[3,8192,256]{2,1,0:T(8,128)(2,1)} %constant_dynamic-update-slice_fusion.1, s32[]{:T(128)S(6)} %select_n.162), kind=kOutput, calls=%fused_computation.15 | convolution fusion | flops 402653184 | bytes 3014660 | tf_op jit(solution)/shard_map/dot_general | solution.py:70
  105.1 2.3 %convolution_bitcast_fusion.7 = f32[384,256]{1,0:T(8,128)S(1)} fusion(bf16[384,2048]{1,0:T(8,128)(2,1)S(1)} %copy-done.1, bf16[3,8192,256]{2,1,0:T(8,128)(2,1)} %constant_dynamic-update-slice_fusion.1, s32[]{:T(128)S(6)} %add.250, s32[]{:T(128)S(6)} %select_n.162), kind=kOutput, calls=%fused_computation.14 | convolution fusion | flops 402653184 | bytes 3014664 | tf_op jit(solution)/shard_map/dot_general | solution.py:70
  107.4 1.8 %convolution_bitcast_fusion.6 = f32[384,256]{1,0:T(8,128)S(1)} fusion(bf16[384,2048]{1,0:T(8,128)(2,1)S(1)} %copy-done.1, bf16[3,8192,256]{2,1,0:T(8,128)(2,1)} %constant_dynamic-update-slice_fusion.1, s32[]{:T(128)S(6)} %add.251, s32[]{:T(128)S(6)} %select_n.162), kind=kOutput, calls=%fused_computation.13 | convolution fusion | flops 402653184 | bytes 3014664 | tf_op jit(solution)/shard_map/dot_general | solution.py:70
  109.2 1.8 %convolution_bitcast_fusion = f32[384,256]{1,0:T(8,128)S(1)} fusion(bf16[384,2048]{1,0:T(8,128)(2,1)S(1)} %collective-permute-done.3, bf16[3,8192,256]{2,1,0:T(8,128)(2,1)} %constant_dynamic-update-slice_fusion.1, s32[]{:T(128)S(6)} %add.251, s32[]{:T(128)S(6)} %select_n.166), kind=kOutput, calls=%fused_computation.7 | convolution fusion | flops 402653184 | bytes 3014664 | tf_op jit(solution)/shard_map/dot_general | solution.py:70
  111.0 0.6 convolution_bitcast_fusion.1
  111.6 0.6 convolution_bitcast_fusion.2
  112.2 0.6 convolution_bitcast_fusion.5
  112.8 0.6 convolution_bitcast_fusion.4
  113.4 0.6 convolution_bitcast_fusion.3
  114.0 2.5 %fusion.16 = f32[384,256]{1,0:T(8,128)S(1)} fusion(bf16[3,8192,256]{2,1,0:T(8,128)(2,1)S(1)} %copy-done, s32[]{:T(128)S(6)} %add.251, s32[]{:T(128)S(6)} %select_n.168, bf16[384,2048]{1,0:T(8,128)(2,1)} %collective-permute-done.9, bf16[384,2048]{1,0:T(8,128)(2,1)} %collective-permute-done.10), kind=kOutput, calls=%fused_computation.46 | convolution fusion | flops 403439616 | bytes 4587528 | tf_op jit(solution)/shard_map/dot_general | solution.py:70
  116.5 2.5 %fusion.17 = f32[384,256]{1,0:T(8,128)S(1)} fusion(bf16[3,8192,256]{2,1,0:T(8,128)(2,1)S(1)} %copy-done, s32[]{:T(128)S(6)} %add.250, s32[]{:T(128)S(6)} %select_n.168, bf16[384,2048]{1,0:T(8,128)(2,1)} %collective-permute-done.9, bf16[384,2048]{1,0:T(8,128)(2,1)} %collective-permute-done.10), kind=kOutput, calls=%fused_computation.48 | convolution fusion | flops 403439616 | bytes 4587528 | tf_op jit(solution)/shard_map/dot_general | solution.py:70
  119.0 2.5 %fusion.18 = f32[384,256]{1,0:T(8,128)S(1)} fusion(bf16[3,8192,256]{2,1,0:T(8,128)(2,1)S(1)} %copy-done, s32[]{:T(128)S(6)} %select_n.168, bf16[384,2048]{1,0:T(8,128)(2,1)} %collective-permute-done.9, bf16[384,2048]{1,0:T(8,128)(2,1)} %collective-permute-done.10), kind=kOutput, calls=%fused_computation.50 | convolution fusion | flops 403439616 | bytes 4587524 | tf_op jit(solution)/shard_map/dot_general | solution.py:70
  121.8 10.8 %collective-permute-done.12 = bf16[384,2048]{1,0:T(8,128)(2,1)S(1)} collective-permute-done((bf16[384,2048]{1,0:T(8,128)(2,1)}, bf16[384,2048]{1,0:T(8,128)(2,1)S(1)}, u32[]{:S(2)}, u32[]{:S(2)}) %collective-permute-start.12) | collective-permute-done | bytes 1572896 | tf_op jit(solution)/shard_map/ppermute | solution.py:57
  132.6 0.6 fusion.15
  133.2 0.6 fusion.14
  133.8 0.6 fusion.13
  134.6 1.5 collective-permute-start.13
  136.9 1.0 fusion.4
  137.9 0.6 slice.242.refs_1_
  138.5 0.6 fusion.97
  139.2 0.6 multiply_reduce_fusion.1
  140.0 0.6 pad_maximum_fusion.refs_0_
  140.6 10.4 %shard_map.100 = (bf16[8,32,256]{2,1,0:T(8,128)(2,1)}, bf16[128,256]{1,0:T(8,128)(2,1)}) custom-call(bf16[32,256]{1,0:T(8,128)(2,1)} %pad_maximum_fusion.refs_0_, bf16[128,256]{1,0:T(8,128)(2,1)} %slice.242.refs_1_), custom_call_target="tpu_custom_call" | custom-call | tf_op jit(solution)/shard_map/pallas_call | solution.py:115
  150.9 0.9 convert_element_type.72
  152.5 0.5 multiply_reduce_fusion
  153.1 0.5 fusion.57
  153.8 0.6 fusion.33
  154.8 1.3 fusion.12
  (105 shorter events, 3.0 us)
Async XLA Ops:
  0.0 38.9 %collective-permute-start.2 = (bf16[384,2048]{1,0:T(8,128)(2,1)}, bf16[384,2048]{1,0:T(8,128)(2,1)S(1)}, u32[]{:S(2)}, u32[]{:S(2)}) collective-permute-start(bf16[384,2048]{1,0:T(8,128)(2,1)} %param.12), channel_id=1, source_target_pairs={{0,1},{1,2},{2,3},{4,5},{5,6},{6,7},{8,9},{9,10},{10,11},{12,13},{... | collective-permute-start | bytes 4718600 | tf_op jit(solution)/shard_map/ppermute | solution.py:57
  5.0 38.0 %collective-permute-start.3 = (bf16[384,2048]{1,0:T(8,128)(2,1)}, bf16[384,2048]{1,0:T(8,128)(2,1)S(1)}, u32[]{:S(2)}, u32[]{:S(2)}) collective-permute-start(bf16[384,2048]{1,0:T(8,128)(2,1)} %param.12), channel_id=1, source_target_pairs={{1,0},{2,1},{3,2},{5,4},{6,5},{7,6},{9,8},{10,9},{11,10},{13,12},{... | collective-permute-start | bytes 4718600 | tf_op jit(solution)/shard_map/ppermute | solution.py:57
  6.3 36.7 %collective-permute-start = (bf16[3,1024,256]{2,1,0:T(8,128)(2,1)}, bf16[3,1024,256]{2,1,0:T(8,128)(2,1)}, u32[]{:S(2)}, u32[]{:S(2)}) collective-permute-start(bf16[3,1024,256]{2,1,0:T(8,128)(2,1)} %param.13), channel_id=1, source_target_pairs={{0,8},{4,12},{8,0},{12,4},{16,24},{20,28},{24,16},{28,20},{1,9},{5... | collective-permute-start | bytes 4718600 | tf_op jit(solution)/shard_map/ppermute | solution.py:22
  7.9 35.9 %collective-permute-start.1 = (bf16[3,1024,256]{2,1,0:T(8,128)(2,1)}, bf16[3,1024,256]{2,1,0:T(8,128)(2,1)}, u32[]{:S(2)}, u32[]{:S(2)}) collective-permute-start(bf16[3,1024,256]{2,1,0:T(8,128)(2,1)} %param.13), channel_id=1, source_target_pairs={{0,16},{4,20},{8,24},{12,28},{16,0},{20,4},{24,8},{28,12},{1,17},{... | collective-permute-start | bytes 4718600 | tf_op jit(solution)/shard_map/ppermute | solution.py:22
  9.4 56.1 %collective-permute-start.5 = (bf16[3,1024,256]{2,1,0:T(8,128)(2,1)}, bf16[3,1024,256]{2,1,0:T(8,128)(2,1)}, u32[]{:S(2)}, u32[]{:S(2)}) collective-permute-start(bf16[3,1024,256]{2,1,0:T(8,128)(2,1)} %param.13), channel_id=1, source_target_pairs={{0,4},{4,0},{8,12},{12,8},{16,20},{20,16},{24,28},{28,24},{1,5},{5... | collective-permute-start | bytes 4718600 | tf_op jit(solution)/shard_map/ppermute | solution.py:22
  9.4 5.4 %copy-start.12 = (bf16[3,1024,256]{2,1,0:T(8,128)(2,1)S(1)}, bf16[3,1024,256]{2,1,0:T(8,128)(2,1)}, u32[]{:S(2)}) copy-start(bf16[3,1024,256]{2,1,0:T(8,128)(2,1)} %param.13) | copy-start | bytes 4718596
  46.5 5.7 %copy-start.30 = (f32[16,256]{1,0:T(8,128)S(1)}, f32[16,256]{1,0:T(8,128)}, u32[]{:S(2)}) copy-start(f32[16,256]{1,0:T(8,128)} %param.17) | copy-start | bytes 49156
  46.5 5.7 %copy-start.31 = (f32[16,256]{1,0:T(8,128)S(1)}, f32[16,256]{1,0:T(8,128)}, u32[]{:S(2)}) copy-start(f32[16,256]{1,0:T(8,128)} %param.16) | copy-start | bytes 49156
  50.5 20.7 %collective-permute-start.4 = (bf16[3,1024,256]{2,1,0:T(8,128)(2,1)}, bf16[3,1024,256]{2,1,0:T(8,128)(2,1)}, u32[]{:S(2)}, u32[]{:S(2)}) collective-permute-start(bf16[3,1024,256]{2,1,0:T(8,128)(2,1)} %get-tuple-element.42), channel_id=1, source_target_pairs={{0,16},{4,12},{8,24},{12,4},{16,0},{20,28},{24,8},{28,20},{1,17},{... | collective-permute-start | bytes 4718600 | tf_op jit(solution)/shard_map/ppermute | solution.py:34
  52.3 7.4 %copy-start.17 = (f32[16,256]{1,0:T(8,128)}, f32[16,256]{1,0:T(8,128)S(1)}, u32[]{:S(2)}) copy-start(f32[16,256]{1,0:T(8,128)S(1)} %get-tuple-element.46) | copy-start | bytes 49156
  53.3 0.8 copy-start.6
  53.4 3.9 %copy-start.2 = (f32[32,16,256]{2,1,0:T(8,128)}, f32[32,16,256]{2,1,0:T(8,128)S(1)}, u32[]{:S(2)}) copy-start(f32[32,16,256]{2,1,0:T(8,128)S(1)} %slice.232) | copy-start | bytes 1572868
  53.4 12.1 %copy-start.20 = (f32[7,3,256]{2,0,1:T(8,128)S(1)}, f32[7,3,256]{2,0,1:T(8,128)}, u32[]{:S(2)}) copy-start(f32[7,3,256]{2,0,1:T(8,128)} %param.14) | copy-start | bytes 64516
  53.4 18.5 %copy-start.15 = (f32[128,256]{1,0:T(8,128)S(1)}, f32[128,256]{1,0:T(8,128)}, u32[]{:S(2)}) copy-start(f32[128,256]{1,0:T(8,128)} %param.15) | copy-start | bytes 393220
  53.5 43.7 %collective-permute-start.6 = (bf16[3,1024,256]{2,1,0:T(8,128)(2,1)}, bf16[3,1024,256]{2,1,0:T(8,128)(2,1)}, u32[]{:S(2)}, u32[]{:S(2)}) collective-permute-start(bf16[3,1024,256]{2,1,0:T(8,128)(2,1)} %collective-permute-done), channel_id=1, source_target_pairs={{0,4},{4,0},{8,12},{12,8},{16,20},{20,16},{24,28},{28,24},{1,5},{5... | collective-permute-start | bytes 4718600 | tf_op jit(solution)/shard_map/ppermute | solution.py:22
  54.1 38.9 %collective-permute-start.10 = (bf16[384,2048]{1,0:T(8,128)(2,1)S(1)}, bf16[384,2048]{1,0:T(8,128)(2,1)}, u32[]{:S(2)}, u32[]{:S(2)}) collective-permute-start(bf16[384,2048]{1,0:T(8,128)(2,1)S(1)} %collective-permute-done.3), channel_id=1, source_target_pairs={{1,0},{2,1},{5,4},{6,5},{9,8},{10,9},{13,12},{14,13},{17,16},{18,1... | collective-permute-start | bytes 4718600 | tf_op jit(solution)/shard_map/ppermute | solution.py:57
  55.4 25.3 %collective-permute-start.9 = (bf16[384,2048]{1,0:T(8,128)(2,1)S(1)}, bf16[384,2048]{1,0:T(8,128)(2,1)}, u32[]{:S(2)}, u32[]{:S(2)}) collective-permute-start(bf16[384,2048]{1,0:T(8,128)(2,1)S(1)} %collective-permute-done.2), channel_id=1, source_target_pairs={{1,2},{2,3},{5,6},{6,7},{9,10},{10,11},{13,14},{14,15},{17,18},{18... | collective-permute-start | bytes 4718600 | tf_op jit(solution)/shard_map/ppermute | solution.py:57
  64.9 11.0 %copy-start.4 = (f32[768,384]{1,0:T(8,128)S(1)}, f32[768,384]{1,0:T(8,128)}, u32[]{:S(2)}) copy-start(f32[768,384]{1,0:T(8,128)} %constant.163.clone) | copy-start | bytes 3538948
  65.5 34.4 %collective-permute-start.7 = (bf16[3,1024,256]{2,1,0:T(8,128)(2,1)}, bf16[3,1024,256]{2,1,0:T(8,128)(2,1)S(1)}, u32[]{:S(2)}, u32[]{:S(2)}) collective-permute-start(bf16[3,1024,256]{2,1,0:T(8,128)(2,1)} %collective-permute-done.1), channel_id=1, source_target_pairs={{0,4},{4,0},{8,12},{12,8},{16,20},{20,16},{24,28},{28,24},{1,5},{5... | collective-permute-start | bytes 4718600 | tf_op jit(solution)/shard_map/ppermute | solution.py:22
  71.2 29.9 %collective-permute-start.8 = (bf16[3,1024,256]{2,1,0:T(8,128)(2,1)}, bf16[3,1024,256]{2,1,0:T(8,128)(2,1)S(1)}, u32[]{:S(2)}, u32[]{:S(2)}) collective-permute-start(bf16[3,1024,256]{2,1,0:T(8,128)(2,1)} %collective-permute-done.4), channel_id=1, source_target_pairs={{0,4},{4,0},{8,12},{12,8},{16,20},{20,16},{24,28},{28,24},{1,5},{5... | collective-permute-start | bytes 4718600 | tf_op jit(solution)/shard_map/ppermute | solution.py:22
  73.5 2.4 %copy-start.11 = (f32[384,256]{1,0:T(8,128)S(1)}, f32[384,256]{1,0:T(8,128)}, u32[]{:S(2)}) copy-start(f32[384,256]{1,0:T(8,128)} %constant_dynamic-update-slice_fusion) | copy-start | bytes 1179652
  80.7 41.1 %collective-permute-start.11 = (bf16[384,2048]{1,0:T(8,128)(2,1)}, bf16[384,2048]{1,0:T(8,128)(2,1)S(1)}, u32[]{:S(2)}, u32[]{:S(2)}) collective-permute-start(bf16[384,2048]{1,0:T(8,128)(2,1)} %collective-permute-done.9), channel_id=1, source_target_pairs={{2,3},{6,7},{10,11},{14,15},{18,19},{22,23},{26,27},{30,31}} | collective-permute-start | bytes 4718600 | tf_op jit(solution)/shard_map/ppermute | solution.py:57
  93.0 39.6 %collective-permute-start.12 = (bf16[384,2048]{1,0:T(8,128)(2,1)}, bf16[384,2048]{1,0:T(8,128)(2,1)S(1)}, u32[]{:S(2)}, u32[]{:S(2)}) collective-permute-start(bf16[384,2048]{1,0:T(8,128)(2,1)} %collective-permute-done.10), channel_id=1, source_target_pairs={{1,0},{5,4},{9,8},{13,12},{17,16},{21,20},{25,24},{29,28}} | collective-permute-start | bytes 4718600 | tf_op jit(solution)/shard_map/ppermute | solution.py:57
  101.1 2.0 %copy-start.1 = (bf16[384,2048]{1,0:T(8,128)(2,1)S(1)}, bf16[384,2048]{1,0:T(8,128)(2,1)}, u32[]{:S(2)}) copy-start(bf16[384,2048]{1,0:T(8,128)(2,1)} %param.12) | copy-start | bytes 4718596
  103.1 7.9 %copy-start = (bf16[3,8192,256]{2,1,0:T(8,128)(2,1)S(1)}, bf16[3,8192,256]{2,1,0:T(8,128)(2,1)}, u32[]{:S(2)}) copy-start(bf16[3,8192,256]{2,1,0:T(8,128)(2,1)} %constant_dynamic-update-slice_fusion.1) | copy-start | bytes 37748740
  134.4 1.8 %copy-start.29 = (f32[3,256]{1,0:T(4,128)S(1)}, f32[3,256]{1,0:T(4,128)}, u32[]{:S(2)}) copy-start(f32[3,256]{1,0:T(4,128)} %get-tuple-element.35) | copy-start | bytes 9220
  134.4 1.8 %copy-start.28 = (f32[3,256]{1,0:T(4,128)S(1)}, f32[3,256]{1,0:T(4,128)}, u32[]{:S(2)}) copy-start(f32[3,256]{1,0:T(4,128)} %get-tuple-element.39) | copy-start | bytes 9220
  134.4 1.8 %copy-start.27 = (f32[3,256]{1,0:T(4,128)S(1)}, f32[3,256]{1,0:T(4,128)}, u32[]{:S(2)}) copy-start(f32[3,256]{1,0:T(4,128)} %get-tuple-element.38) | copy-start | bytes 9220
  134.4 1.8 %copy-start.26 = (f32[3,256]{1,0:T(4,128)S(1)}, f32[3,256]{1,0:T(4,128)}, u32[]{:S(2)}) copy-start(f32[3,256]{1,0:T(4,128)} %get-tuple-element.37) | copy-start | bytes 9220
  134.4 1.9 %copy-start.25 = (f32[3,256]{1,0:T(4,128)S(1)}, f32[3,256]{1,0:T(4,128)}, u32[]{:S(2)}) copy-start(f32[3,256]{1,0:T(4,128)} %get-tuple-element.36) | copy-start | bytes 9220
  134.4 1.9 %copy-start.24 = (f32[3,256]{1,0:T(4,128)S(1)}, f32[3,256]{1,0:T(4,128)}, u32[]{:S(2)}) copy-start(f32[3,256]{1,0:T(4,128)} %get-tuple-element.41) | copy-start | bytes 9220
  134.4 1.9 %copy-start.23 = (f32[3,256]{1,0:T(4,128)S(1)}, f32[3,256]{1,0:T(4,128)}, u32[]{:S(2)}) copy-start(f32[3,256]{1,0:T(4,128)} %get-tuple-element.40) | copy-start | bytes 9220
  134.4 1.9 %copy-start.8 = (f32[33,16,256]{2,1,0:T(8,128)S(1)}, f32[33,16,256]{2,1,0:T(8,128)}, u32[]{:S(2)}) copy-start(f32[33,16,256]{2,1,0:T(8,128)} %get-tuple-element.45) | copy-start | bytes 1622020
  134.6 2.1 %collective-permute-start.13 = (bf16[6,768]{1,0:T(8,128)(2,1)S(1)}, bf16[6,768]{1,0:T(8,128)(2,1)S(1)}, u32[]{:S(2)}, u32[]{:S(2)}) collective-permute-start(bf16[6,768]{1,0:T(8,128)(2,1)S(1)} %slice.223), channel_id=1, source_target_pairs={{0,4},{4,8},{8,12},{12,16},{16,20},{20,24},{24,28},{1,5},{5,9},{9,... | collective-permute-start | bytes 27656 | tf_op jit(solution)/shard_map/ppermute | solution.py:17
  136.8 1.7 %copy-start.5 = (f32[768,384]{1,0:T(8,128)S(1)}, f32[768,384]{1,0:T(8,128)}, u32[]{:S(2)}) copy-start(f32[768,384]{1,0:T(8,128)} %constant.163.clone) | copy-start | bytes 3538948
  138.5 1.3 copy-start.3
  139.2 12.7 %copy-start.21 = (f32[8,16]{1,0:T(8,128)S(1)}, f32[8,16]{1,0:T(8,128)}, u32[]{:S(2)}) copy-start(f32[8,16]{1,0:T(8,128)} %get-tuple-element.48) | copy-start | bytes 1540
  139.2 12.7 %copy-start.22 = (f32[8,16]{1,0:T(8,128)S(1)}, f32[8,16]{1,0:T(8,128)}, u32[]{:S(2)}) copy-start(f32[8,16]{1,0:T(8,128)} %get-tuple-element.49) | copy-start | bytes 1540
  139.2 12.7 %copy-start.32 = (f32[8]{0:T(128)S(1)}, f32[8]{0:T(128)}, u32[]{:S(2)}) copy-start(f32[8]{0:T(128)} %get-tuple-element.53) | copy-start | bytes 100
  139.2 12.8 %copy-start.7 = (f32[33,16,256]{2,1,0:T(8,128)S(1)}, f32[33,16,256]{2,1,0:T(8,128)}, u32[]{:S(2)}) copy-start(f32[33,16,256]{2,1,0:T(8,128)} %copy-done.6) | copy-start | bytes 1622020
  139.2 12.8 %copy-start.18 = (f32[16,256]{1,0:T(8,128)S(1)}, f32[16,256]{1,0:T(8,128)}, u32[]{:S(2)}) copy-start(f32[16,256]{1,0:T(8,128)} %copy-done.17) | copy-start | bytes 49156
  152.0 1.0 copy-start.16
  152.1 1.0 copy-start.19
  152.2 1.4 copy-start.9
  152.2 1.4 copy-start.10
  152.2 1.6 copy-start.14
  153.8 1.1 copy-start.13
